TPU v7x, 32 devices: a whole 2x2x4 slice. The times are simulated.
32 devices in a mesh: segment: 2 (over core), angle: 8 (over z, x), tile: 2 (over y).
Axes of the slice: x: 2, y: 2, z: 4, core: 2. Of those that a mesh axis runs over, the one named last changes fastest.
Arguments:
- sinogram: float32 [32, 32, 4096], P(('segment', 'angle'), 'tile'), may hold values from -6 to 6
- paganin_width: float32 [1], replicated, may hold values from 2 to 8
- window_block: int32 [32, 2], replicated, may hold values from 0 to 28
Outputs:
- volume: float32 [2, 32, 32768], P('tile', None, ('segment', 'angle'))
All inputs are finite; a program needn't handle non-finite values.
Results may differ from a plain program's by a relative error of at most 0.0035.
Values may be sent and summed in bfloat16 or wider, within the bound.
No kernel may reach another device: no remote copies, remote signals or barrier semaphores. Data moves between devices by JAX's collectives and lax.ppermute only.
A program may use at most 64 MiB of HBM per device.

v0:
```python
import functools
import math

import jax
import jax.numpy as jnp
import numpy as np
from jax import lax
from jax.experimental import pallas as pl
from jax.experimental.pallas import tpu as pltpu
from jax.sharding import PartitionSpec as P

WIN = 512
BAND = 128
ROWS_DEV = 8
TCOLS = 256
LANES = 128
CHUNK = 32
DEPTH = 48
SLOT = 64
PER = LANES // SLOT


def split(value):
    high = value.astype(jnp.bfloat16)
    return high, (value - high.astype(jnp.float32)).astype(jnp.bfloat16)


def three_dots(rows, taps):
    (row_high, row_low), (tap_high, tap_low) = rows, taps
    dot = functools.partial(jnp.dot, preferred_element_type=jnp.float32)
    return dot(row_high, tap_high) + (dot(row_low, tap_high) + dot(row_high, tap_low))


def offsets(depth, width, shift):
    return (
        lax.broadcasted_iota(jnp.int32, (depth, width), 0)
        - lax.broadcasted_iota(jnp.int32, (depth, width), 1)
        - shift
    )


def filter_kernel(plan, width, blocks_ref, table, rows_ref, *refs):
    tiles, outs, first_bin = plan
    outputs, (info, blocks, padded, raw, smooth, arrived) = refs[:tiles], refs[tiles:]
    local, slices, bins = rows_ref.shape
    block_total = bins // LANES
    raw_wide = raw.shape[1]
    smooth_blocks = smooth.shape[1] // LANES
    height = local * slices
    ahead = 2 * LANES

    place = lax.axis_index("segment") * lax.axis_size("angle") + lax.axis_index("angle")
    copies = [
        pltpu.make_async_copy(blocks_ref, blocks, arrived.at[local]),
        pltpu.make_async_copy(table.at[place], info, arrived.at[local + 1]),
    ]
    copies += [
        pltpu.make_async_copy(
            rows_ref.at[angle], padded.at[angle, :, pl.ds(ahead, bins)], arrived.at[angle]
        )
        for angle in range(local)
    ]
    for copy in copies:
        copy.start()
    behind = padded.shape[2] - ahead - bins
    padded[:, :, :ahead] = jnp.zeros((local, slices, ahead), jnp.float32)
    padded[:, :, ahead + bins :] = jnp.zeros((local, slices, behind), jnp.float32)

    decay = width[0]
    steps = (lax.broadcasted_iota(jnp.int32, (1, BAND), 1) + 1).astype(jnp.float32)
    total = 1.0 + 2.0 * jnp.sum(jnp.exp(-steps / decay), axis=1, keepdims=True)
    away = offsets(2 * 256, 256, BAND)
    spread = jnp.abs(away)
    paganin = jnp.where(
        spread <= BAND, jnp.exp(-spread.astype(jnp.float32) / decay) / total, 0.0
    )
    paganin = split(paganin)
    away = offsets(512, LANES, BAND + first_bin)
    spread = jnp.abs(away)
    squared = jnp.maximum(spread * spread, 1).astype(jnp.float32)
    odd = jnp.logical_and(spread <= BAND, (spread & 1) == 1)
    ramp = jnp.where(odd, -1.0 / (math.pi * math.pi * squared), 0.0)
    ramp = split(jnp.where(away == 0, 0.25, ramp))

    for copy in copies:
        copy.wait()
    first = place * local
    mine = lax.axis_index("tile")
    starts = []
    for turn in range(tiles):
        tile = lax.rem(mine - turn + tiles, tiles)
        for angle in range(local):
            start = blocks[tile, first + angle]
            starts.append(start)
            at = (turn * local + angle) * slices
            lanes = pl.ds(pl.multiple_of(start * LANES, LANES), raw_wide)
            raw[at : at + slices, :] = padded[angle, :, lanes]
    high, low = split(raw[...])
    for pair in range(smooth_blocks // 2):
        at = slice(pair * 256, pair * 256 + 512)
        smooth[:, pair * 256 : (pair + 1) * 256] = three_dots(
            (high[:, at], low[:, at]), paganin
        )
    for index, start in enumerate(starts):
        at = slice(index * slices, (index + 1) * slices)
        for j in range(smooth_blocks):
            if 1 <= j <= WIN // LANES:
                continue
            block = start - 1 + j
            inside = jnp.logical_and(block >= 0, block < block_total)
            lanes = slice(j * LANES, (j + 1) * LANES)
            smooth[at, lanes] = jnp.where(inside, smooth[at, lanes], 0.0)
    high, low = split(smooth[...])
    for j in range(outs):
        at = slice(j * LANES, j * LANES + 512)
        value = three_dots((high[:, at], low[:, at]), ramp)
        for turn in range(tiles):
            part = value[turn * height : (turn + 1) * height]
            outputs[turn][:, j * LANES : (j + 1) * LANES] = part.astype(jnp.bfloat16)


def read(info, index):
    return info[index // LANES, index % LANES]


def hat_kernel(plan, info, hats):
    from_part, half, tile_rows, angle_total = plan
    parts, chunks, depth, pixels = hats.shape
    count = depth // SLOT
    place = lax.axis_index("segment") * lax.axis_size("angle") + lax.axis_index("angle")
    first_row = (place * ROWS_DEV).astype(jnp.float32) - (tile_rows - 1) / 2.0
    lane = lax.broadcasted_iota(jnp.int32, (8, pixels), 1)
    depth_step = lax.broadcasted_iota(jnp.int32, (8, pixels), 0).astype(jnp.float32)
    y = (lane // CHUNK).astype(jnp.float32) + first_row
    x = (lane % CHUNK).astype(jnp.float32)
    gap = jnp.zeros((SLOT - DEPTH, pixels), jnp.bfloat16)
    for part in range(parts):

        def step(index, carry, part=part):
            angle = (from_part + part) * count + index
            cosine, sine = read(info, angle), read(info, angle_total + angle)
            at = pl.multiple_of(index * SLOT, SLOT)
            for chunk in range(chunks):
                left = chunk * CHUNK - (TCOLS - 1) / 2.0
                low = read(info, 2 * angle_total + angle * chunks + chunk)
                across = (x + left) * cosine + y * sine + (half - low) - depth_step
                rows = [
                    jnp.maximum(0.0, 1.0 - jnp.abs(across - 8.0 * j)) for j in range(DEPTH // 8)
                ]
                rows = jnp.concatenate(rows, axis=0).astype(jnp.bfloat16)
                hats[part, chunk, pl.ds(at, DEPTH), :] = rows
                hats[part, chunk, pl.ds(at + DEPTH, SLOT - DEPTH), :] = gap
            return carry

        lax.fori_loop(0, count, step, 0)


def project_kernel(plan, info, windows, hats, *refs):
    part, hat_part, local, angle_total, last = plan
    before, (out, held, cut) = refs[:-3], refs[-3:]
    chunks, depth, pixels = hats.shape[1:]
    sources, tiles, height, wide = windows.shape
    slices = height // local
    count = depth // SLOT
    lane_blocks = wide // LANES
    for source in range(sources):
        for turn in range(tiles):
            piece = windows[source, turn].astype(held.dtype)
            for angle in range(local):
                held[source * local + angle, turn * slices : (turn + 1) * slices, :] = piece[
                    angle * slices : (angle + 1) * slices
                ]
    lane = lax.broadcasted_iota(jnp.int32, (slices * tiles, LANES), 1)

    def step(pair, carry):
        for chunk in range(chunks):
            merged = None
            for spot in range(PER):
                index = pair * PER + spot
                low = read(info, 2 * angle_total + (part * count + index) * chunks + chunk)
                low = low.astype(jnp.int32)
                block = low // LANES
                past = low - block * LANES
                after = jnp.minimum(block + 1, lane_blocks - 1)
                near = pl.ds(pl.multiple_of(block * LANES, LANES), LANES)
                far = pl.ds(pl.multiple_of(after * LANES, LANES), LANES)
                value = jnp.where(lane >= past, held[index, :, near], held[index, :, far])
                turn_by = (spot * SLOT + LANES - past) & (LANES - 1)
                value = pltpu.roll(value, turn_by, 1)
                merged = value if spot == 0 else jnp.where(lane < spot * SLOT, merged, value)
            at = pl.ds(pl.multiple_of(pair * LANES, LANES), LANES)
            cut[chunk, :, at] = merged.astype(jnp.bfloat16)
        return carry

    lax.fori_loop(0, count // PER, step, 0, unroll=4)
    sums = []
    for chunk in range(chunks):
        value = jnp.dot(cut[chunk], hats[hat_part, chunk], preferred_element_type=jnp.float32)
        if before:
            value = value + before[0][chunk]
        sums.append(value)
        if not last:
            out[chunk] = value
    if not last:
        return
    mine = lax.axis_index("tile")
    for pair in range(TCOLS // LANES):
        near = sums[pair * (LANES // CHUNK) : (pair + 1) * (LANES // CHUNK)]
        for row in range(ROWS_DEV):
            value = jnp.concatenate(
                [part[:, row * CHUNK : (row + 1) * CHUNK] for part in near], axis=1
            )
            at = row * TCOLS + pair * LANES
            if slices % 8 == 0:
                for turn in range(tiles):
                    tile = lax.rem(mine + turn, tiles)
                    into = pl.ds(pl.multiple_of(tile * slices, slices), slices)
                    out[0, into, at : at + LANES] = value[turn * slices : (turn + 1) * slices]
            else:
                out[0, :, at : at + LANES] = pltpu.roll(value, mine * slices, 0)


def shifted(value, axis, by):
    size = lax.axis_size(axis)
    return lax.ppermute(value, axis, [(i, (i - by) % size) for i in range(size)])


def swapped(value, axis, by):
    return lax.ppermute(value, axis, [(i, i ^ by) for i in range(lax.axis_size(axis))])


def body(sinogram, paganin_width, window_block):
    local, slices, bins = sinogram.shape
    segments, spots, tiles = (lax.axis_size(name) for name in ("segment", "angle", "tile"))
    segment, spot = lax.axis_index("segment"), lax.axis_index("angle")
    groups = segments * spots
    angle_total = local * groups
    tile_rows = ROWS_DEV * groups
    reach = math.hypot((TCOLS - 1) / 2, (tile_rows - 1) / 2)
    first_bin = max(0, int(WIN / 2 - reach - 0.01)) // 16 * 16
    last_bin = min(WIN - 1, int(WIN / 2 + reach + 0.01) + 1)
    outs = -(-(last_bin + 1 - first_bin) // LANES)
    assert first_bin + (outs - 1) * LANES < WIN and first_bin < LANES
    assert spots & (spots - 1) == 0 and spots > 1
    smooth_blocks = -(-(outs + 3) // 2) * 2
    chunks, pixels = TCOLS // CHUNK, ROWS_DEV * CHUNK
    half = WIN / 2.0 - first_bin

    smem = pl.BlockSpec(memory_space=pltpu.SMEM)
    vmem = pl.BlockSpec(memory_space=pltpu.VMEM)
    hat_bytes = angle_total * SLOT * ROWS_DEV * TCOLS * 2
    params = pltpu.CompilerParams(vmem_limit_bytes=hat_bytes + 12 * 1024 * 1024)
    height = local * slices
    block_total = bins // LANES
    reached = [0]
    for bit in reversed(range(1, spots.bit_length() - 1)):
        reached += [other ^ (1 << bit) for other in reached]
    order = np.array([[other ^ swap for other in reached] for swap in (0, 1)], np.int32)
    order = np.repeat(order.reshape(-1), local), np.tile(np.arange(local), spots)
    where = np.arange(groups)[:, None]
    by = np.arange(segments)[:, None] + where[:, :, None] // spots
    angles = (where % spots ^ order[0]) * local + order[1]
    angles = by % segments * (spots * local) + angles[:, None]
    theta = math.pi * angles.reshape(groups, angle_total) / angle_total
    cosine, sine = np.cos(theta), np.sin(theta)
    left = np.arange(chunks) * CHUNK - (TCOLS - 1) / 2.0
    edges = np.minimum(cosine[..., None] * left, cosine[..., None] * (left + (CHUNK - 1)))
    top = where * ROWS_DEV - (tile_rows - 1) / 2.0
    rise = np.minimum(sine * top, sine * (top + (ROWS_DEV - 1)))
    lows = np.floor(edges + rise[..., None] + (half - 0.01)).astype(np.int32)
    lows = lows.astype(np.float32).reshape(groups, -1)
    table = np.concatenate([cosine.astype(np.float32), sine.astype(np.float32), lows], axis=1)
    info_rows = -(-table.shape[1] // (8 * LANES)) * 8
    table = np.pad(table, ((0, 0), (0, info_rows * LANES - table.shape[1])))
    table = jnp.asarray(table.reshape(groups, info_rows, LANES))

    *cut, info = pl.pallas_call(
        functools.partial(filter_kernel, (tiles, outs, first_bin)),
        out_shape=[jax.ShapeDtypeStruct((height, outs * LANES), jnp.bfloat16)] * tiles
        + [jax.ShapeDtypeStruct((info_rows, LANES), jnp.float32)],
        in_specs=[smem] + [pl.BlockSpec(memory_space=pltpu.HBM)] * 3,
        out_specs=[vmem] * (tiles + 1),
        scratch_shapes=[
            pltpu.SMEM(window_block.T.shape, jnp.int32),
            pltpu.VMEM(
                (local, slices, (block_total - WIN // LANES + smooth_blocks + 2) * LANES),
                jnp.float32,
            ),
            pltpu.VMEM((height * tiles, (smooth_blocks + 2) * LANES), jnp.float32),
            pltpu.VMEM((height * tiles, smooth_blocks * LANES), jnp.float32),
            pltpu.SemaphoreType.DMA((local + 2,)),
        ],
        compiler_params=params,
        name="filter",
    )(
        paganin_width,
        *(pltpu.with_memory_space_constraint(v, pltpu.HBM) for v in (window_block.T, table, sinogram)),
    )

    depth = spots * local // 2 * SLOT
    def hats_of(by, after):
        ready = lax.optimization_barrier((info, *after))[0]
        return pl.pallas_call(
            functools.partial(hat_kernel, (2 * by, half, tile_rows, angle_total)),
            out_shape=jax.ShapeDtypeStruct((2, chunks, depth, pixels), jnp.bfloat16),
            in_specs=[smem],
            out_specs=vmem,
            compiler_params=params,
            cost_estimate=pl.CostEstimate(
                flops=2 * chunks * depth * pixels * 16, bytes_accessed=0, transcendentals=0
            ),
            name="hats",
        )(ready)

    arrived = [cut[0]] + [shifted(cut[turn], "tile", turn) for turn in range(1, tiles)]
    hats = [hats_of(0, cut)]
    arrived, hats[0] = lax.optimization_barrier((arrived, hats[0]))
    pieces = jnp.stack(arrived)[None]
    for bit in reversed(range(1, spots.bit_length() - 1)):
        sent = swapped(pieces, "angle", 1 << bit)
        if len(hats) < segments:
            hats.append(hats_of(len(hats), (pieces,)))
            sent, hats[-1] = lax.optimization_barrier((sent, hats[-1]))
        pieces = jnp.concatenate([pieces, sent])
    while len(hats) < segments:
        hats.append(hats_of(len(hats), (pieces,)))
    held_type = jnp.bfloat16 if slices % 16 == 0 else jnp.float32

    def project(by, which, windows, sums, last=False):
        value = pl.pallas_call(
            functools.partial(project_kernel, (2 * by + which, which, local, angle_total, last)),
            out_shape=jax.ShapeDtypeStruct(
                (1, slices * tiles, ROWS_DEV * TCOLS)
                if last
                else (chunks, slices * tiles, pixels),
                jnp.float32,
            ),
            in_specs=[smem] + [vmem] * (2 + len(sums)),
            out_specs=vmem,
            scratch_shapes=[
                pltpu.VMEM((spots * local // 2, slices * tiles, outs * LANES), held_type),
                pltpu.VMEM((chunks, slices * tiles, depth), jnp.bfloat16),
            ],
            compiler_params=params,
            cost_estimate=pl.CostEstimate(
                flops=32 * slices * tiles * chunks * depth * pixels,
                bytes_accessed=0,
                transcendentals=0,
            ),
            name="project",
        )(info, windows, hats[by], *sums)
        return (value,)

    crossed = swapped(pieces, "angle", 1)
    sums = project(0, 0, pieces, ())
    for by in range(1, segments):
        sums = project(by, 0, shifted(pieces, "segment", by), sums)
    crossed, sums = lax.optimization_barrier((crossed, sums))
    others = [shifted(crossed, "segment", by) for by in range(1, segments)]
    sums = project(0, 1, crossed, sums, segments == 1)
    for by in range(1, segments):
        sums = project(by, 1, others[by - 1], sums, by == segments - 1)
    return sums[0]


def solution(mesh):
    in_specs = (P(("segment", "angle"), "tile", None), P(), P())
    out_specs = P("tile", None, ("segment", "angle"))
    return jax.shard_map(body, mesh=mesh, in_specs=in_specs, out_specs=out_specs, check_vma=False)
```

profile of v0, /device:TPU:0, one launch (start us, length us, event | category | flops | bytes accessed | tf_op | source)
XLA Modules:
  0.0 29.1 jit_solution(3262976585484006641)
XLA Ops:
  0.7 2.0 %filter.1 = (bf16[32,384]{1,0:T(8,128)(2,1)S(1)}, bf16[32,384]{1,0:T(8,128)(2,1)S(1)}, f32[8,128]{1,0:T(8,128)S(1)}) custom-call(f32[1]{0:T(128)S(6)} %copy.5.width, s32[2,32]{1,0:T(2,128)} %bitcast.7, f32[16,8,128]{2,1,0:T(8,128)} %constant.2.clone.table, f32[2,16,4096]{2,1,0:T(8,128)} %rows_ref.1), custom_call_target="tpu_custom_call" | custom-call | tf_op jit(solution)/shard_map/filter/pallas_call | solution.py:277
  2.7 3.0 %collective-permute-start = (bf16[32,384]{1,0:T(8,128)(2,1)S(1)}, bf16[32,384]{1,0:T(8,128)(2,1)S(1)}, u32[]{:S(2)}, u32[]{:S(2)}) collective-permute-start(bf16[32,384]{1,0:T(8,128)(2,1)S(1)} %get-tuple-element.19), channel_id=1, source_target_pairs={{0,1},{1,0},{2,3},{3,2},{4,5},{5,4},{6,7},{7,6},{8,9},{9,8},{10,11... | collective-permute-start | bytes 73736 | tf_op jit(solution)/shard_map/ppermute | solution.py:225
  5.7 2.3 %hats.2 = bf16[2,8,512,256]{3,2,1,0:T(8,128)(2,1)S(1)} custom-call(f32[8,128]{1,0:T(8,128)S(1)} %get-tuple-element.23.info), custom_call_target="tpu_custom_call" | custom-call | flops 33554432 | tf_op jit(solution)/shard_map/hats/pallas_call | solution.py:303
  8.0 0.0 collective-permute-done
  8.1 2.7 %collective-permute-start.1 = (bf16[1,2,32,384]{3,2,1,0:T(8,128)(2,1)S(1)}, bf16[1,2,32,384]{3,2,1,0:T(8,128)(2,1)S(1)}, u32[]{:S(2)}, u32[]{:S(2)}) collective-permute-start(bf16[1,2,32,384]{3,2,1,0:T(8,128)(2,1)S(1)} %maximum_bitcast_fusion), channel_id=1, source_target_pairs={{0,8},{2,10},{4,12},{6,14},{8,0},{10,2},{12,4},{14,6},{1,9},{3,11}... | collective-permute-start | bytes 147464 | tf_op jit(solution)/shard_map/ppermute | solution.py:229
  10.7 2.4 %hats.3 = bf16[2,8,512,256]{3,2,1,0:T(8,128)(2,1)S(1)} custom-call(f32[8,128]{1,0:T(8,128)S(1)} %get-tuple-element.23.info), custom_call_target="tpu_custom_call" | custom-call | flops 33554432 | tf_op jit(solution)/shard_map/hats/pallas_call | solution.py:303
  13.1 0.2 collective-permute-done.1
  13.3 1.5 %collective-permute-start.2 = (bf16[2,2,32,384]{3,2,1,0:T(8,128)(2,1)S(1)}, bf16[2,2,32,384]{3,2,1,0:T(8,128)(2,1)S(1)}, u32[]{:S(2)}, u32[]{:S(2)}) collective-permute-start(bf16[2,2,32,384]{3,2,1,0:T(8,128)(2,1)S(1)} %pad_maximum_fusion.1), channel_id=1, source_target_pairs={{0,4},{2,6},{4,0},{6,2},{8,12},{10,14},{12,8},{14,10},{1,5},{3,7},... | collective-permute-start | bytes 294920 | tf_op jit(solution)/shard_map/ppermute | solution.py:229
  14.8 3.2 %collective-permute-done.2 = bf16[2,2,32,384]{3,2,1,0:T(8,128)(2,1)S(1)} collective-permute-done((bf16[2,2,32,384]{3,2,1,0:T(8,128)(2,1)S(1)}, bf16[2,2,32,384]{3,2,1,0:T(8,128)(2,1)S(1)}, u32[]{:S(2)}, u32[]{:S(2)}) %collective-permute-start.2) | collective-permute-done | bytes 98336 | tf_op jit(solution)/shard_map/ppermute | solution.py:229
  18.0 0.1 collective-permute-start.4
  18.1 1.6 %collective-permute-start.3 = (bf16[4,2,32,384]{3,2,1,0:T(8,128)(2,1)S(1)}, bf16[4,2,32,384]{3,2,1,0:T(8,128)(2,1)S(1)}, u32[]{:S(2)}, u32[]{:S(2)}) collective-permute-start(bf16[4,2,32,384]{3,2,1,0:T(8,128)(2,1)S(1)} %pad_maximum_fusion.windows), channel_id=1, source_target_pairs={{0,2},{2,0},{4,6},{6,4},{8,10},{10,8},{12,14},{14,12},{1,3},{3,1},... | collective-permute-start | bytes 589832 | tf_op jit(solution)/shard_map/ppermute | solution.py:229
  19.6 1.4 %project.4.refs_0_ = f32[8,32,256]{2,1,0:T(8,128)S(1)} custom-call(f32[8,128]{1,0:T(8,128)S(1)} %get-tuple-element.23.info, bf16[4,2,32,384]{3,2,1,0:T(8,128)(2,1)S(1)} %pad_maximum_fusion.windows, bf16[2,8,512,256]{3,2,1,0:T(8,128)(2,1)S(1)} %hats.2), custom_call_target="tpu_custom_call" | custom-call | flops 1073741824 | tf_op jit(solution)/shard_map/project/pallas_call | solution.py:330
  21.1 0.0 collective-permute-done.4.windows
  21.1 1.4 %project.5.refs_0_ = f32[8,32,256]{2,1,0:T(8,128)S(1)} custom-call(f32[8,128]{1,0:T(8,128)S(1)} %get-tuple-element.23.info, bf16[4,2,32,384]{3,2,1,0:T(8,128)(2,1)S(1)} %collective-permute-done.4.windows, bf16[2,8,512,256]{3,2,1,0:T(8,128)(2,1)S(1)} %hats.3, f32[8,32,256]{2,1,0:T(8,128)S(1)} %project.4.refs_0_), custom_call_target="tpu_custom_call" | custom-call | flops 1073741824 | tf_op jit(solution)/shard_map/project/pallas_call | solution.py:330
  22.5 2.9 %collective-permute-done.3.windows = bf16[4,2,32,384]{3,2,1,0:T(8,128)(2,1)S(1)} collective-permute-done((bf16[4,2,32,384]{3,2,1,0:T(8,128)(2,1)S(1)}, bf16[4,2,32,384]{3,2,1,0:T(8,128)(2,1)S(1)}, u32[]{:S(2)}, u32[]{:S(2)}) %collective-permute-start.3) | collective-permute-done | bytes 196640 | tf_op jit(solution)/shard_map/ppermute | solution.py:229
  25.4 0.0 collective-permute-start.5
  25.4 1.4 %project.6.refs_0_ = f32[8,32,256]{2,1,0:T(8,128)S(1)} custom-call(f32[8,128]{1,0:T(8,128)S(1)} %get-tuple-element.23.info, bf16[4,2,32,384]{3,2,1,0:T(8,128)(2,1)S(1)} %collective-permute-done.3.windows, bf16[2,8,512,256]{3,2,1,0:T(8,128)(2,1)S(1)} %hats.2, f32[8,32,256]{2,1,0:T(8,128)S(1)} %project.5.refs_0_), custom_call_target="tpu_custom_call" | custom-call | flops 1073741824 | tf_op jit(solution)/shard_map/project/pallas_call | solution.py:330
  26.8 0.0 collective-permute-done.5.windows
  26.8 2.3 %project.7 = f32[1,32,2048]{2,1,0:T(8,128)} custom-call(f32[8,128]{1,0:T(8,128)S(1)} %get-tuple-element.23.info, bf16[4,2,32,384]{3,2,1,0:T(8,128)(2,1)S(1)} %collective-permute-done.5.windows, bf16[2,8,512,256]{3,2,1,0:T(8,128)(2,1)S(1)} %hats.3, f32[8,32,256]{2,1,0:T(8,128)S(1)} %project.6.refs_0_), custom_call_target="tpu_custom_call" | custom-call | flops 1073741824 | tf_op jit(solution)/shard_map/project/pallas_call | solution.py:330
  (3 shorter events, 0.1 us)
Async XLA Ops:
  2.7 5.4 %collective-permute-start = (bf16[32,384]{1,0:T(8,128)(2,1)S(1)}, bf16[32,384]{1,0:T(8,128)(2,1)S(1)}, u32[]{:S(2)}, u32[]{:S(2)}) collective-permute-start(bf16[32,384]{1,0:T(8,128)(2,1)S(1)} %get-tuple-element.19), channel_id=1, source_target_pairs={{0,1},{1,0},{2,3},{3,2},{4,5},{5,4},{6,7},{7,6},{8,9},{9,8},{10,11... | collective-permute-start | bytes 73736 | tf_op jit(solution)/shard_map/ppermute | solution.py:225
  8.1 5.2 %collective-permute-start.1 = (bf16[1,2,32,384]{3,2,1,0:T(8,128)(2,1)S(1)}, bf16[1,2,32,384]{3,2,1,0:T(8,128)(2,1)S(1)}, u32[]{:S(2)}, u32[]{:S(2)}) collective-permute-start(bf16[1,2,32,384]{3,2,1,0:T(8,128)(2,1)S(1)} %maximum_bitcast_fusion), channel_id=1, source_target_pairs={{0,8},{2,10},{4,12},{6,14},{8,0},{10,2},{12,4},{14,6},{1,9},{3,11}... | collective-permute-start | bytes 147464 | tf_op jit(solution)/shard_map/ppermute | solution.py:229
  13.3 4.7 %collective-permute-start.2 = (bf16[2,2,32,384]{3,2,1,0:T(8,128)(2,1)S(1)}, bf16[2,2,32,384]{3,2,1,0:T(8,128)(2,1)S(1)}, u32[]{:S(2)}, u32[]{:S(2)}) collective-permute-start(bf16[2,2,32,384]{3,2,1,0:T(8,128)(2,1)S(1)} %pad_maximum_fusion.1), channel_id=1, source_target_pairs={{0,4},{2,6},{4,0},{6,2},{8,12},{10,14},{12,8},{14,10},{1,5},{3,7},... | collective-permute-start | bytes 294920 | tf_op jit(solution)/shard_map/ppermute | solution.py:229
  18.0 3.1 %collective-permute-start.4 = (bf16[4,2,32,384]{3,2,1,0:T(8,128)(2,1)S(1)}, bf16[4,2,32,384]{3,2,1,0:T(8,128)(2,1)S(1)}, u32[]{:S(2)}, u32[]{:S(2)}) collective-permute-start(bf16[4,2,32,384]{3,2,1,0:T(8,128)(2,1)S(1)} %pad_maximum_fusion.windows), channel_id=1, source_target_pairs={{0,16},{16,0},{1,17},{17,1},{2,18},{18,2},{3,19},{19,3},{4,20},{20... | collective-permute-start | bytes 589832 | tf_op jit(solution)/shard_map/ppermute | solution.py:225
  18.1 7.3 %collective-permute-start.3 = (bf16[4,2,32,384]{3,2,1,0:T(8,128)(2,1)S(1)}, bf16[4,2,32,384]{3,2,1,0:T(8,128)(2,1)S(1)}, u32[]{:S(2)}, u32[]{:S(2)}) collective-permute-start(bf16[4,2,32,384]{3,2,1,0:T(8,128)(2,1)S(1)} %pad_maximum_fusion.windows), channel_id=1, source_target_pairs={{0,2},{2,0},{4,6},{6,4},{8,10},{10,8},{12,14},{14,12},{1,3},{3,1},... | collective-permute-start | bytes 589832 | tf_op jit(solution)/shard_map/ppermute | solution.py:229
  25.4 1.5 %collective-permute-start.5 = (bf16[4,2,32,384]{3,2,1,0:T(8,128)(2,1)S(1)}, bf16[4,2,32,384]{3,2,1,0:T(8,128)(2,1)S(1)}, u32[]{:S(2)}, u32[]{:S(2)}) collective-permute-start(bf16[4,2,32,384]{3,2,1,0:T(8,128)(2,1)S(1)} %collective-permute-done.3.windows), channel_id=1, source_target_pairs={{0,16},{16,0},{1,17},{17,1},{2,18},{18,2},{3,19},{19,3},{4,20},{20... | collective-permute-start | bytes 589832 | tf_op jit(solution)/shard_map/ppermute | solution.py:225
where the time goes:
time: 29.3 us; the launch traced here: 29.1 us
  Pallas kernels  13.3 us (45%)
  starting transfers between devices  8.84 us (30%)
  waiting for transfers between devices  6.18 us (21%)
  between operations  0.73 us (2%)
    pallas_call x4, Pallas kernels, project(): pl.pallas_call(functools.partial(project_kernel, (2 * by + which, which,...  6.6 us
    ppermute x3, waiting for transfers between devices, swapped(): lax.ppermute(value, axis, [(i, i ^ by) for i in range(lax.axis_size(axis))])  6.17 us
    ppermute x3, starting transfers between devices, swapped(): lax.ppermute(value, axis, [(i, i ^ by) for i in range(lax.axis_size(axis))])  5.74 us
    pallas_call x2, Pallas kernels, hats_of(): pl.pallas_call(functools.partial(hat_kernel, (2 * by, half, tile_rows, an...  4.7 us
    ppermute x3, starting transfers between devices, shifted(): lax.ppermute(value, axis, [(i, (i - by) % size) for i in range(size)])  3.1 us
    pallas_call x1, Pallas kernels, body(): pl.pallas_call(functools.partial(filter_kernel, (tiles, outs, first_bin))...  2 us
  transfers between devices with their start and end apart: 6, of which 3 were waited for; matrix products, arithmetic and copies ran while one was open for 0% of the time, Pallas kernels for 31%

commit v1 on v0

--- a/solution.py
+++ b/solution.py
@@ -14,6 +14,7 @@
 ROWS_DEV = 8
 TCOLS = 256
 LANES = 128
+LANE_BITS = 7
 CHUNK = 32
 DEPTH = 48
 SLOT = 64
@@ -25,10 +26,15 @@
     return high, (value - high.astype(jnp.float32)).astype(jnp.bfloat16)
 
 
-def three_dots(rows, taps):
-    (row_high, row_low), (tap_high, tap_low) = rows, taps
+def banded(value, taps, starts):
+    tap_high, tap_low = taps
     dot = functools.partial(jnp.dot, preferred_element_type=jnp.float32)
-    return dot(row_high, tap_high) + (dot(row_low, tap_high) + dot(row_high, tap_low))
+    cut = [value[:, start : start + tap_high.shape[0]] for start in starts]
+    high, low = split(jnp.concatenate(cut, axis=0))
+    both = dot(jnp.concatenate([high, low], axis=0), tap_high)
+    result = both[: high.shape[0]] + (both[high.shape[0] :] + dot(high, tap_low))
+    rows = value.shape[0]
+    return [result[index * rows : (index + 1) * rows] for index in range(len(starts))]
 
 
 def offsets(depth, width, shift):
@@ -95,12 +101,9 @@
             at = (turn * local + angle) * slices
             lanes = pl.ds(pl.multiple_of(start * LANES, LANES), raw_wide)
             raw[at : at + slices, :] = padded[angle, :, lanes]
-    high, low = split(raw[...])
-    for pair in range(smooth_blocks // 2):
-        at = slice(pair * 256, pair * 256 + 512)
-        smooth[:, pair * 256 : (pair + 1) * 256] = three_dots(
-            (high[:, at], low[:, at]), paganin
-        )
+    pairs = range(0, smooth_blocks * LANES, 256)
+    for at, value in zip(pairs, banded(raw[...], paganin, pairs)):
+        smooth[:, at : at + 256] = value
     for index, start in enumerate(starts):
         at = slice(index * slices, (index + 1) * slices)
         for j in range(smooth_blocks):
@@ -110,22 +113,20 @@
             inside = jnp.logical_and(block >= 0, block < block_total)
             lanes = slice(j * LANES, (j + 1) * LANES)
             smooth[at, lanes] = jnp.where(inside, smooth[at, lanes], 0.0)
-    high, low = split(smooth[...])
-    for j in range(outs):
-        at = slice(j * LANES, j * LANES + 512)
-        value = three_dots((high[:, at], low[:, at]), ramp)
+    lanes = range(0, outs * LANES, LANES)
+    for j, value in enumerate(banded(smooth[...], ramp, lanes)):
         for turn in range(tiles):
             part = value[turn * height : (turn + 1) * height]
             outputs[turn][:, j * LANES : (j + 1) * LANES] = part.astype(jnp.bfloat16)
 
 
 def read(info, index):
-    return info[index // LANES, index % LANES]
+    return info[index >> LANE_BITS, index & (LANES - 1)]
 
 
 def hat_kernel(plan, info, hats):
-    from_part, half, tile_rows, angle_total = plan
-    parts, chunks, depth, pixels = hats.shape
+    part, half, tile_rows, angle_total = plan
+    chunks, depth, pixels = hats.shape
     count = depth // SLOT
     place = lax.axis_index("segment") * lax.axis_size("angle") + lax.axis_index("angle")
     first_row = (place * ROWS_DEV).astype(jnp.float32) - (tile_rows - 1) / 2.0
@@ -134,31 +135,28 @@
     y = (lane // CHUNK).astype(jnp.float32) + first_row
     x = (lane % CHUNK).astype(jnp.float32)
     gap = jnp.zeros((SLOT - DEPTH, pixels), jnp.bfloat16)
-    for part in range(parts):
-
-        def step(index, carry, part=part):
-            angle = (from_part + part) * count + index
-            cosine, sine = read(info, angle), read(info, angle_total + angle)
-            at = pl.multiple_of(index * SLOT, SLOT)
-            for chunk in range(chunks):
-                left = chunk * CHUNK - (TCOLS - 1) / 2.0
-                low = read(info, 2 * angle_total + angle * chunks + chunk)
-                across = (x + left) * cosine + y * sine + (half - low) - depth_step
-                rows = [
-                    jnp.maximum(0.0, 1.0 - jnp.abs(across - 8.0 * j)) for j in range(DEPTH // 8)
-                ]
-                rows = jnp.concatenate(rows, axis=0).astype(jnp.bfloat16)
-                hats[part, chunk, pl.ds(at, DEPTH), :] = rows
-                hats[part, chunk, pl.ds(at + DEPTH, SLOT - DEPTH), :] = gap
-            return carry
-
-        lax.fori_loop(0, count, step, 0)
+
+    def step(index, carry):
+        angle = part * count + index
+        cosine, sine = read(info, angle), read(info, angle_total + angle)
+        at = pl.multiple_of(index * SLOT, SLOT)
+        for chunk in range(chunks):
+            left = chunk * CHUNK - (TCOLS - 1) / 2.0
+            low = read(info, 2 * angle_total + angle * chunks + chunk)
+            across = (x + left) * cosine + y * sine + (half - low) - depth_step
+            rows = [jnp.maximum(0.0, 1.0 - jnp.abs(across - 8.0 * j)) for j in range(DEPTH // 8)]
+            rows = jnp.concatenate(rows, axis=0).astype(jnp.bfloat16)
+            hats[chunk, pl.ds(at, DEPTH), :] = rows
+            hats[chunk, pl.ds(at + DEPTH, SLOT - DEPTH), :] = gap
+        return carry
+
+    lax.fori_loop(0, count, step, 0)
 
 
 def project_kernel(plan, info, windows, hats, *refs):
-    part, hat_part, local, angle_total, last = plan
+    part, local, angle_total, last = plan
     before, (out, held, cut) = refs[:-3], refs[-3:]
-    chunks, depth, pixels = hats.shape[1:]
+    chunks, depth, pixels = hats.shape
     sources, tiles, height, wide = windows.shape
     slices = height // local
     count = depth // SLOT
@@ -179,8 +177,8 @@
                 index = pair * PER + spot
                 low = read(info, 2 * angle_total + (part * count + index) * chunks + chunk)
                 low = low.astype(jnp.int32)
-                block = low // LANES
-                past = low - block * LANES
+                block = low >> LANE_BITS
+                past = low & (LANES - 1)
                 after = jnp.minimum(block + 1, lane_blocks - 1)
                 near = pl.ds(pl.multiple_of(block * LANES, LANES), LANES)
                 far = pl.ds(pl.multiple_of(after * LANES, LANES), LANES)
@@ -195,7 +193,7 @@
     lax.fori_loop(0, count // PER, step, 0, unroll=4)
     sums = []
     for chunk in range(chunks):
-        value = jnp.dot(cut[chunk], hats[hat_part, chunk], preferred_element_type=jnp.float32)
+        value = jnp.dot(cut[chunk], hats[chunk], preferred_element_type=jnp.float32)
         if before:
             value = value + before[0][chunk]
         sums.append(value)
@@ -298,37 +296,40 @@
     )
 
     depth = spots * local // 2 * SLOT
-    def hats_of(by, after):
+    def hats_of(by, which, after):
         ready = lax.optimization_barrier((info, *after))[0]
         return pl.pallas_call(
-            functools.partial(hat_kernel, (2 * by, half, tile_rows, angle_total)),
-            out_shape=jax.ShapeDtypeStruct((2, chunks, depth, pixels), jnp.bfloat16),
+            functools.partial(hat_kernel, (2 * by + which, half, tile_rows, angle_total)),
+            out_shape=jax.ShapeDtypeStruct((chunks, depth, pixels), jnp.bfloat16),
             in_specs=[smem],
             out_specs=vmem,
             compiler_params=params,
             cost_estimate=pl.CostEstimate(
-                flops=2 * chunks * depth * pixels * 16, bytes_accessed=0, transcendentals=0
+                flops=chunks * depth * pixels * 16, bytes_accessed=0, transcendentals=0
             ),
             name="hats",
         )(ready)
 
-    arrived = [cut[0]] + [shifted(cut[turn], "tile", turn) for turn in range(1, tiles)]
-    hats = [hats_of(0, cut)]
-    arrived, hats[0] = lax.optimization_barrier((arrived, hats[0]))
-    pieces = jnp.stack(arrived)[None]
+    hats = {}
+    left_over = [(by, which) for which in (0, 1) for by in range(segments)]
+
+    def beside(moved, after, count=1):
+        names = [left_over.pop(0) for _ in range(min(count, len(left_over)))]
+        made = [hats_of(*name, after) for name in names]
+        moved, made = lax.optimization_barrier((moved, made))
+        hats.update(zip(names, made))
+        return moved
+
+    moved = [shifted(cut[turn], "tile", turn) for turn in range(1, tiles)]
+    pieces = jnp.stack([cut[0]] + beside(moved, cut))[None]
     for bit in reversed(range(1, spots.bit_length() - 1)):
-        sent = swapped(pieces, "angle", 1 << bit)
-        if len(hats) < segments:
-            hats.append(hats_of(len(hats), (pieces,)))
-            sent, hats[-1] = lax.optimization_barrier((sent, hats[-1]))
-        pieces = jnp.concatenate([pieces, sent])
-    while len(hats) < segments:
-        hats.append(hats_of(len(hats), (pieces,)))
+        moved = beside(swapped(pieces, "angle", 1 << bit), (pieces,))
+        pieces = jnp.concatenate([pieces, moved])
     held_type = jnp.bfloat16 if slices % 16 == 0 else jnp.float32
 
     def project(by, which, windows, sums, last=False):
         value = pl.pallas_call(
-            functools.partial(project_kernel, (2 * by + which, which, local, angle_total, last)),
+            functools.partial(project_kernel, (2 * by + which, local, angle_total, last)),
             out_shape=jax.ShapeDtypeStruct(
                 (1, slices * tiles, ROWS_DEV * TCOLS)
                 if last
@@ -348,14 +349,14 @@
                 transcendentals=0,
             ),
             name="project",
-        )(info, windows, hats[by], *sums)
+        )(info, windows, hats[by, which], *sums)
         return (value,)
 
     crossed = swapped(pieces, "angle", 1)
     sums = project(0, 0, pieces, ())
     for by in range(1, segments):
         sums = project(by, 0, shifted(pieces, "segment", by), sums)
-    crossed, sums = lax.optimization_barrier((crossed, sums))
+    crossed, sums = beside((crossed, sums), (pieces,), len(left_over))
     others = [shifted(crossed, "segment", by) for by in range(1, segments)]
     sums = project(0, 1, crossed, sums, segments == 1)
     for by in range(1, segments):

time: 29.3 us -> 28.5 us (0.973)
  waiting for transfers between devices: 6.18 us -> 4.69 us
  starting transfers between devices: 8.84 us -> 10.1 us
  Pallas kernels: 13.3 us -> 12.8 us
    ppermute x3, waiting for transfers between devices: 6.17 us -> 3.94 us  [swapped(): lax.ppermute(value, axis, [(i, i ^ by) for i in range(lax.axis_size(axis))])]
    ppermute x3, starting transfers between devices: 5.74 us -> 7.01 us  [swapped(): lax.ppermute(value, axis, [(i, i ^ by) for i in range(lax.axis_size(axis))])]
    ppermute x3, waiting for transfers between devices: 0.01 us -> 0.74 us  [shifted(): lax.ppermute(value, axis, [(i, (i - by) % size) for i in range(size)])]
    pallas_call x6 -> x8, Pallas kernels: 11.3 us -> 10.8 us  [the longest x4 5.8 us: project(): pl.pallas_call(functools.partial(project_kernel, (2 * by + which, local,...]
  transfers between devices with their start and end apart: 6 -> 6, of which waited for: 3 -> 5; matrix products, arithmetic and copies ran while one was open for 0% -> 0% of each run, Pallas kernels for 31% -> 31%
where the time goes in v1:
time: 28.5 us; the launch traced here: 28.3 us
  Pallas kernels  12.8 us (45%)
  starting transfers between devices  10.1 us (35%)
  waiting for transfers between devices  4.69 us (16%)
  between operations  0.71 us (2%)
    ppermute x3, starting transfers between devices, swapped(): lax.ppermute(value, axis, [(i, i ^ by) for i in range(lax.axis_size(axis))])  7.01 us
    pallas_call x4, Pallas kernels, project(): pl.pallas_call(functools.partial(project_kernel, (2 * by + which, local,...  5.8 us
    pallas_call x4, Pallas kernels, hats_of(): pl.pallas_call(functools.partial(hat_kernel, (2 * by + which, half, tile_...  5.05 us
    ppermute x3, waiting for transfers between devices, swapped(): lax.ppermute(value, axis, [(i, i ^ by) for i in range(lax.axis_size(axis))])  3.94 us
    ppermute x3, starting transfers between devices, shifted(): lax.ppermute(value, axis, [(i, (i - by) % size) for i in range(size)])  3.11 us
    pallas_call x1, Pallas kernels, body(): pl.pallas_call(functools.partial(filter_kernel, (tiles, outs, first_bin))...  1.92 us
    ppermute x3, waiting for transfers between devices, shifted(): lax.ppermute(value, axis, [(i, (i - by) % size) for i in range(size)])  0.74 us
  transfers between devices with their start and end apart: 6, of which 5 were waited for; matrix products, arithmetic and copies ran while one was open for 0% of the time, Pallas kernels for 31%

profile of v1, /device:TPU:0, one launch (start us, length us, event | category | flops | bytes accessed | tf_op | source)
XLA Modules:
  0.0 28.3 jit_solution(12040088608212553401)
XLA Ops:
  0.7 1.9 %filter.1 = (bf16[32,384]{1,0:T(8,128)(2,1)S(1)}, bf16[32,384]{1,0:T(8,128)(2,1)S(1)}, f32[8,128]{1,0:T(8,128)S(1)}) custom-call(f32[1]{0:T(128)S(6)} %copy.5.width, s32[2,32]{1,0:T(2,128)} %bitcast.7, f32[16,8,128]{2,1,0:T(8,128)} %constant.2.clone.table, f32[2,16,4096]{2,1,0:T(8,128)} %rows_ref.1), custom_call_target="tpu_custom_call" | custom-call | tf_op jit(solution)/shard_map/filter/pallas_call | solution.py:275
  2.6 3.0 %collective-permute-start = (bf16[32,384]{1,0:T(8,128)(2,1)S(1)}, bf16[32,384]{1,0:T(8,128)(2,1)S(1)}, u32[]{:S(2)}, u32[]{:S(2)}) collective-permute-start(bf16[32,384]{1,0:T(8,128)(2,1)S(1)} %get-tuple-element.23), channel_id=1, source_target_pairs={{0,1},{1,0},{2,3},{3,2},{4,5},{5,4},{6,7},{7,6},{8,9},{9,8},{10,11... | collective-permute-start | bytes 73736 | tf_op jit(solution)/shard_map/ppermute | solution.py:223
  5.6 1.2 %hats.4 = bf16[8,512,256]{2,1,0:T(8,128)(2,1)S(1)} custom-call(f32[8,128]{1,0:T(8,128)S(1)} %get-tuple-element.32.info), custom_call_target="tpu_custom_call" | custom-call | flops 16777216 | tf_op jit(solution)/shard_map/hats/pallas_call | solution.py:301
  6.9 0.6 %collective-permute-done = bf16[32,384]{1,0:T(8,128)(2,1)S(1)} collective-permute-done((bf16[32,384]{1,0:T(8,128)(2,1)S(1)}, bf16[32,384]{1,0:T(8,128)(2,1)S(1)}, u32[]{:S(2)}, u32[]{:S(2)}) %collective-permute-start) | collective-permute-done | bytes 24608 | tf_op jit(solution)/shard_map/ppermute | solution.py:223
  7.4 3.2 %collective-permute-start.1 = (bf16[1,2,32,384]{3,2,1,0:T(8,128)(2,1)S(1)}, bf16[1,2,32,384]{3,2,1,0:T(8,128)(2,1)S(1)}, u32[]{:S(2)}, u32[]{:S(2)}) collective-permute-start(bf16[1,2,32,384]{3,2,1,0:T(8,128)(2,1)S(1)} %maximum_bitcast_fusion), channel_id=1, source_target_pairs={{0,8},{2,10},{4,12},{6,14},{8,0},{10,2},{12,4},{14,6},{1,9},{3,11}... | collective-permute-start | bytes 147464 | tf_op jit(solution)/shard_map/ppermute | solution.py:227
  10.6 1.3 %hats.5 = bf16[8,512,256]{2,1,0:T(8,128)(2,1)S(1)} custom-call(f32[8,128]{1,0:T(8,128)S(1)} %get-tuple-element.32.info), custom_call_target="tpu_custom_call" | custom-call | flops 16777216 | tf_op jit(solution)/shard_map/hats/pallas_call | solution.py:301
  11.9 0.8 %collective-permute-done.1 = bf16[1,2,32,384]{3,2,1,0:T(8,128)(2,1)S(1)} collective-permute-done((bf16[1,2,32,384]{3,2,1,0:T(8,128)(2,1)S(1)}, bf16[1,2,32,384]{3,2,1,0:T(8,128)(2,1)S(1)}, u32[]{:S(2)}, u32[]{:S(2)}) %collective-permute-start.1) | collective-permute-done | bytes 49184 | tf_op jit(solution)/shard_map/ppermute | solution.py:227
  12.7 2.0 %collective-permute-start.2 = (bf16[2,2,32,384]{3,2,1,0:T(8,128)(2,1)S(1)}, bf16[2,2,32,384]{3,2,1,0:T(8,128)(2,1)S(1)}, u32[]{:S(2)}, u32[]{:S(2)}) collective-permute-start(bf16[2,2,32,384]{3,2,1,0:T(8,128)(2,1)S(1)} %pad_maximum_fusion.1), channel_id=1, source_target_pairs={{0,4},{2,6},{4,0},{6,2},{8,12},{10,14},{12,8},{14,10},{1,5},{3,7},... | collective-permute-start | bytes 294920 | tf_op jit(solution)/shard_map/ppermute | solution.py:227
  14.6 1.3 %hats.6 = bf16[8,512,256]{2,1,0:T(8,128)(2,1)S(1)} custom-call(f32[8,128]{1,0:T(8,128)S(1)} %get-tuple-element.32.info), custom_call_target="tpu_custom_call" | custom-call | flops 16777216 | tf_op jit(solution)/shard_map/hats/pallas_call | solution.py:301
  15.9 1.4 %collective-permute-done.2 = bf16[2,2,32,384]{3,2,1,0:T(8,128)(2,1)S(1)} collective-permute-done((bf16[2,2,32,384]{3,2,1,0:T(8,128)(2,1)S(1)}, bf16[2,2,32,384]{3,2,1,0:T(8,128)(2,1)S(1)}, u32[]{:S(2)}, u32[]{:S(2)}) %collective-permute-start.2) | collective-permute-done | bytes 98336 | tf_op jit(solution)/shard_map/ppermute | solution.py:227
  17.4 0.1 collective-permute-start.4
  17.5 1.9 %collective-permute-start.3 = (bf16[4,2,32,384]{3,2,1,0:T(8,128)(2,1)S(1)}, bf16[4,2,32,384]{3,2,1,0:T(8,128)(2,1)S(1)}, u32[]{:S(2)}, u32[]{:S(2)}) collective-permute-start(bf16[4,2,32,384]{3,2,1,0:T(8,128)(2,1)S(1)} %pad_maximum_fusion.windows), channel_id=1, source_target_pairs={{0,2},{2,0},{4,6},{6,4},{8,10},{10,8},{12,14},{14,12},{1,3},{3,1},... | collective-permute-start | bytes 589832 | tf_op jit(solution)/shard_map/ppermute | solution.py:227
  19.4 1.3 %hats.7 = bf16[8,512,256]{2,1,0:T(8,128)(2,1)S(1)} custom-call(f32[8,128]{1,0:T(8,128)S(1)} %get-tuple-element.32.info), custom_call_target="tpu_custom_call" | custom-call | flops 16777216 | tf_op jit(solution)/shard_map/hats/pallas_call | solution.py:301
  20.6 1.2 %project.4.refs_0_ = f32[8,32,256]{2,1,0:T(8,128)S(1)} custom-call(f32[8,128]{1,0:T(8,128)S(1)} %get-tuple-element.32.info, bf16[4,2,32,384]{3,2,1,0:T(8,128)(2,1)S(1)} %pad_maximum_fusion.windows, bf16[8,512,256]{2,1,0:T(8,128)(2,1)S(1)} %hats.4), custom_call_target="tpu_custom_call" | custom-call | flops 1073741824 | tf_op jit(solution)/shard_map/project/pallas_call | solution.py:331
  21.9 0.0 collective-permute-done.4.windows
  21.9 1.3 %project.5.refs_0_ = f32[8,32,256]{2,1,0:T(8,128)S(1)} custom-call(f32[8,128]{1,0:T(8,128)S(1)} %get-tuple-element.32.info, bf16[4,2,32,384]{3,2,1,0:T(8,128)(2,1)S(1)} %collective-permute-done.4.windows, bf16[8,512,256]{2,1,0:T(8,128)(2,1)S(1)} %hats.5, f32[8,32,256]{2,1,0:T(8,128)S(1)} %project.4.refs_0_), custom_call_target="tpu_custom_call" | custom-call | flops 1073741824 | tf_op jit(solution)/shard_map/project/pallas_call | solution.py:331
  23.1 1.7 %collective-permute-done.3.windows = bf16[4,2,32,384]{3,2,1,0:T(8,128)(2,1)S(1)} collective-permute-done((bf16[4,2,32,384]{3,2,1,0:T(8,128)(2,1)S(1)}, bf16[4,2,32,384]{3,2,1,0:T(8,128)(2,1)S(1)}, u32[]{:S(2)}, u32[]{:S(2)}) %collective-permute-start.3) | collective-permute-done | bytes 196640 | tf_op jit(solution)/shard_map/ppermute | solution.py:227
  24.8 0.0 collective-permute-start.5
  24.9 1.2 %project.6.refs_0_ = f32[8,32,256]{2,1,0:T(8,128)S(1)} custom-call(f32[8,128]{1,0:T(8,128)S(1)} %get-tuple-element.32.info, bf16[4,2,32,384]{3,2,1,0:T(8,128)(2,1)S(1)} %collective-permute-done.3.windows, bf16[8,512,256]{2,1,0:T(8,128)(2,1)S(1)} %hats.6, f32[8,32,256]{2,1,0:T(8,128)S(1)} %project.5.refs_0_), custom_call_target="tpu_custom_call" | custom-call | flops 1073741824 | tf_op jit(solution)/shard_map/project/pallas_call | solution.py:331
  26.1 0.2 collective-permute-done.5.windows
  26.3 2.1 %project.7 = f32[1,32,2048]{2,1,0:T(8,128)} custom-call(f32[8,128]{1,0:T(8,128)S(1)} %get-tuple-element.32.info, bf16[4,2,32,384]{3,2,1,0:T(8,128)(2,1)S(1)} %collective-permute-done.5.windows, bf16[8,512,256]{2,1,0:T(8,128)(2,1)S(1)} %hats.7, f32[8,32,256]{2,1,0:T(8,128)S(1)} %project.6.refs_0_), custom_call_target="tpu_custom_call" | custom-call | flops 1073741824 | tf_op jit(solution)/shard_map/project/pallas_call | solution.py:331
  (3 shorter events, 0.1 us)
Async XLA Ops:
  2.6 4.8 %collective-permute-start = (bf16[32,384]{1,0:T(8,128)(2,1)S(1)}, bf16[32,384]{1,0:T(8,128)(2,1)S(1)}, u32[]{:S(2)}, u32[]{:S(2)}) collective-permute-start(bf16[32,384]{1,0:T(8,128)(2,1)S(1)} %get-tuple-element.23), channel_id=1, source_target_pairs={{0,1},{1,0},{2,3},{3,2},{4,5},{5,4},{6,7},{7,6},{8,9},{9,8},{10,11... | collective-permute-start | bytes 73736 | tf_op jit(solution)/shard_map/ppermute | solution.py:223
  7.4 5.2 %collective-permute-start.1 = (bf16[1,2,32,384]{3,2,1,0:T(8,128)(2,1)S(1)}, bf16[1,2,32,384]{3,2,1,0:T(8,128)(2,1)S(1)}, u32[]{:S(2)}, u32[]{:S(2)}) collective-permute-start(bf16[1,2,32,384]{3,2,1,0:T(8,128)(2,1)S(1)} %maximum_bitcast_fusion), channel_id=1, source_target_pairs={{0,8},{2,10},{4,12},{6,14},{8,0},{10,2},{12,4},{14,6},{1,9},{3,11}... | collective-permute-start | bytes 147464 | tf_op jit(solution)/shard_map/ppermute | solution.py:227
  12.7 4.7 %collective-permute-start.2 = (bf16[2,2,32,384]{3,2,1,0:T(8,128)(2,1)S(1)}, bf16[2,2,32,384]{3,2,1,0:T(8,128)(2,1)S(1)}, u32[]{:S(2)}, u32[]{:S(2)}) collective-permute-start(bf16[2,2,32,384]{3,2,1,0:T(8,128)(2,1)S(1)} %pad_maximum_fusion.1), channel_id=1, source_target_pairs={{0,4},{2,6},{4,0},{6,2},{8,12},{10,14},{12,8},{14,10},{1,5},{3,7},... | collective-permute-start | bytes 294920 | tf_op jit(solution)/shard_map/ppermute | solution.py:227
  17.4 4.5 %collective-permute-start.4 = (bf16[4,2,32,384]{3,2,1,0:T(8,128)(2,1)S(1)}, bf16[4,2,32,384]{3,2,1,0:T(8,128)(2,1)S(1)}, u32[]{:S(2)}, u32[]{:S(2)}) collective-permute-start(bf16[4,2,32,384]{3,2,1,0:T(8,128)(2,1)S(1)} %pad_maximum_fusion.windows), channel_id=1, source_target_pairs={{0,16},{16,0},{1,17},{17,1},{2,18},{18,2},{3,19},{19,3},{4,20},{20... | collective-permute-start | bytes 589832 | tf_op jit(solution)/shard_map/ppermute | solution.py:223
  17.5 7.4 %collective-permute-start.3 = (bf16[4,2,32,384]{3,2,1,0:T(8,128)(2,1)S(1)}, bf16[4,2,32,384]{3,2,1,0:T(8,128)(2,1)S(1)}, u32[]{:S(2)}, u32[]{:S(2)}) collective-permute-start(bf16[4,2,32,384]{3,2,1,0:T(8,128)(2,1)S(1)} %pad_maximum_fusion.windows), channel_id=1, source_target_pairs={{0,2},{2,0},{4,6},{6,4},{8,10},{10,8},{12,14},{14,12},{1,3},{3,1},... | collective-permute-start | bytes 589832 | tf_op jit(solution)/shard_map/ppermute | solution.py:227
  24.8 1.4 %collective-permute-start.5 = (bf16[4,2,32,384]{3,2,1,0:T(8,128)(2,1)S(1)}, bf16[4,2,32,384]{3,2,1,0:T(8,128)(2,1)S(1)}, u32[]{:S(2)}, u32[]{:S(2)}) collective-permute-start(bf16[4,2,32,384]{3,2,1,0:T(8,128)(2,1)S(1)} %collective-permute-done.3.windows), channel_id=1, source_target_pairs={{0,16},{16,0},{1,17},{17,1},{2,18},{18,2},{3,19},{19,3},{4,20},{20... | collective-permute-start | bytes 589832 | tf_op jit(solution)/shard_map/ppermute | solution.py:223

commit v2 on v1

--- a/solution.py
+++ b/solution.py
@@ -153,10 +153,11 @@
     lax.fori_loop(0, count, step, 0)
 
 
-def project_kernel(plan, info, windows, hats, *refs):
-    part, local, angle_total, last = plan
-    before, (out, held, cut) = refs[:-3], refs[-3:]
-    chunks, depth, pixels = hats.shape
+def project_kernel(plan, info, windows, *refs):
+    part, hat_count, local, angle_total, last = plan
+    hats, before, (out, held, cut) = refs[:hat_count], refs[hat_count:-3], refs[-3:]
+    chunks, hat_depth, pixels = hats[0].shape
+    depth = hat_count * hat_depth
     sources, tiles, height, wide = windows.shape
     slices = height // local
     count = depth // SLOT
@@ -193,9 +194,11 @@
     lax.fori_loop(0, count // PER, step, 0, unroll=4)
     sums = []
     for chunk in range(chunks):
-        value = jnp.dot(cut[chunk], hats[chunk], preferred_element_type=jnp.float32)
-        if before:
-            value = value + before[0][chunk]
+        value = before[0][chunk] if before else None
+        for index, hat in enumerate(hats):
+            lanes = slice(index * hat_depth, (index + 1) * hat_depth)
+            more = jnp.dot(cut[chunk, :, lanes], hat[chunk], preferred_element_type=jnp.float32)
+            value = more if value is None else value + more
         sums.append(value)
         if not last:
             out[chunk] = value
@@ -250,11 +253,15 @@
     params = pltpu.CompilerParams(vmem_limit_bytes=hat_bytes + 12 * 1024 * 1024)
     height = local * slices
     block_total = bins // LANES
+    bits = [1 << bit for bit in reversed(range(spots.bit_length() - 1))]
+    exchanges = [(bits[0],)]
+    for first in range(1, len(bits), 2):
+        pair = bits[first : first + 2]
+        exchanges.append((*pair, sum(pair)) if len(pair) == 2 else tuple(pair))
     reached = [0]
-    for bit in reversed(range(1, spots.bit_length() - 1)):
-        reached += [other ^ (1 << bit) for other in reached]
-    order = np.array([[other ^ swap for other in reached] for swap in (0, 1)], np.int32)
-    order = np.repeat(order.reshape(-1), local), np.tile(np.arange(local), spots)
+    for masks in exchanges:
+        reached = [other ^ mask for mask in (0, *masks) for other in reached]
+    order = np.repeat(np.array(reached), local), np.tile(np.arange(local), spots)
     where = np.arange(groups)[:, None]
     by = np.arange(segments)[:, None] + where[:, :, None] // spots
     angles = (where % spots ^ order[0]) * local + order[1]
@@ -296,10 +303,10 @@
     )
 
     depth = spots * local // 2 * SLOT
-    def hats_of(by, which, after):
+    def hats_of(part, after):
         ready = lax.optimization_barrier((info, *after))[0]
         return pl.pallas_call(
-            functools.partial(hat_kernel, (2 * by + which, half, tile_rows, angle_total)),
+            functools.partial(hat_kernel, (part, half, tile_rows, angle_total)),
             out_shape=jax.ShapeDtypeStruct((chunks, depth, pixels), jnp.bfloat16),
             in_specs=[smem],
             out_specs=vmem,
@@ -310,57 +317,60 @@
             name="hats",
         )(ready)
 
-    hats = {}
-    left_over = [(by, which) for which in (0, 1) for by in range(segments)]
-
-    def beside(moved, after, count=1):
-        names = [left_over.pop(0) for _ in range(min(count, len(left_over)))]
-        made = [hats_of(*name, after) for name in names]
+    hats = []
+
+    def beside(moved, after, count):
+        made = []
+        for _ in range(min(count, 2 * segments - len(hats))):
+            made.append(hats_of(len(hats), after))
+            hats.append(None)
         moved, made = lax.optimization_barrier((moved, made))
-        hats.update(zip(names, made))
+        hats[len(hats) - len(made) :] = made
         return moved
 
-    moved = [shifted(cut[turn], "tile", turn) for turn in range(1, tiles)]
-    pieces = jnp.stack([cut[0]] + beside(moved, cut))[None]
-    for bit in reversed(range(1, spots.bit_length() - 1)):
-        moved = beside(swapped(pieces, "angle", 1 << bit), (pieces,))
-        pieces = jnp.concatenate([pieces, moved])
+    def joint(turn, mask):
+        def index(spot, tile):
+            return (spot ^ mask) * tiles + (tile - turn) % tiles
+
+        pairs = [(at, index(at // tiles, at % tiles)) for at in range(spots * tiles)]
+        return lax.ppermute(cut[turn], ("angle", "tile"), pairs)
+
+    near = [(turn, mask) for mask in (0, *exchanges[0]) for turn in range(tiles)][1:]
+    moved = beside([joint(*pair) for pair in near], cut, 2)
+    pieces = jnp.stack([cut[0], *moved]).reshape(2, tiles, *cut[0].shape)
+    for index, masks in enumerate(exchanges[1:]):
+        moved = [swapped(pieces, "angle", mask) for mask in masks]
+        last = index == len(exchanges) - 2
+        moved = beside(moved, (pieces,), 2 * segments if last else 2)
+        pieces = jnp.concatenate([pieces, *moved])
     held_type = jnp.bfloat16 if slices % 16 == 0 else jnp.float32
-
-    def project(by, which, windows, sums, last=False):
+    parts = [pieces] + [shifted(pieces, "segment", by) for by in range(1, segments)]
+    sums = ()
+    for by, windows in enumerate(parts):
+        last = by == segments - 1
         value = pl.pallas_call(
-            functools.partial(project_kernel, (2 * by + which, local, angle_total, last)),
+            functools.partial(project_kernel, (by, 2, local, angle_total, last)),
             out_shape=jax.ShapeDtypeStruct(
                 (1, slices * tiles, ROWS_DEV * TCOLS)
                 if last
                 else (chunks, slices * tiles, pixels),
                 jnp.float32,
             ),
-            in_specs=[smem] + [vmem] * (2 + len(sums)),
+            in_specs=[smem] + [vmem] * (3 + len(sums)),
             out_specs=vmem,
             scratch_shapes=[
-                pltpu.VMEM((spots * local // 2, slices * tiles, outs * LANES), held_type),
-                pltpu.VMEM((chunks, slices * tiles, depth), jnp.bfloat16),
+                pltpu.VMEM((spots * local, slices * tiles, outs * LANES), held_type),
+                pltpu.VMEM((chunks, slices * tiles, 2 * depth), jnp.bfloat16),
             ],
             compiler_params=params,
             cost_estimate=pl.CostEstimate(
-                flops=32 * slices * tiles * chunks * depth * pixels,
+                flops=64 * slices * tiles * chunks * depth * pixels,
                 bytes_accessed=0,
                 transcendentals=0,
             ),
             name="project",
-        )(info, windows, hats[by, which], *sums)
-        return (value,)
-
-    crossed = swapped(pieces, "angle", 1)
-    sums = project(0, 0, pieces, ())
-    for by in range(1, segments):
-        sums = project(by, 0, shifted(pieces, "segment", by), sums)
-    crossed, sums = beside((crossed, sums), (pieces,), len(left_over))
-    others = [shifted(crossed, "segment", by) for by in range(1, segments)]
-    sums = project(0, 1, crossed, sums, segments == 1)
-    for by in range(1, segments):
-        sums = project(by, 1, others[by - 1], sums, by == segments - 1)
+        )(info, windows, *hats[2 * by : 2 * by + 2], *sums)
+        sums = (value,)
     return sums[0]
 
 

time: 28.5 us -> 26.5 us (0.930)
  waiting for transfers between devices: 4.69 us -> 3.17 us
  starting transfers between devices: 10.1 us -> 9.26 us
    ppermute x0 -> x3, starting transfers between devices: none -> 5.64 us  [joint(): return lax.ppermute(cut[turn], ('angle', 'tile'), pairs)]
    ppermute x3, starting transfers between devices: 7.01 us -> 3.55 us  [swapped(): lax.ppermute(value, axis, [(i, i ^ by) for i in range(lax.axis_size(axis))])]
    ppermute x3 -> x1, starting transfers between devices: 3.11 us -> 0.07 us  [shifted(): lax.ppermute(value, axis, [(i, (i - by) % size) for i in range(size)])]
    ppermute x3, waiting for transfers between devices: 3.94 us -> 1.62 us  [swapped(): lax.ppermute(value, axis, [(i, i ^ by) for i in range(lax.axis_size(axis))])]
    ppermute x0 -> x3, waiting for transfers between devices: none -> 1.55 us  [joint(): return lax.ppermute(cut[turn], ('angle', 'tile'), pairs)]
    ppermute x3 -> x1, waiting for transfers between devices: 0.74 us -> 0.01 us  [shifted(): lax.ppermute(value, axis, [(i, (i - by) % size) for i in range(size)])]
    pallas_call x8 -> x6, Pallas kernels: 10.8 us -> 11.1 us  [the longest x2 6.06 us: body(): pl.pallas_call(functools.partial(project_kernel, (by, 2, local, angle_tot...]
  transfers between devices with their start and end apart: 6 -> 7, of which waited for: 5 -> 4; matrix products, arithmetic and copies ran while one was open for 0% -> 0% of each run, Pallas kernels for 31% -> 29%
where the time goes in v2:
time: 26.5 us; the launch traced here: 26.3 us
  Pallas kernels  13 us (49%)
  starting transfers between devices  9.26 us (35%)
  waiting for transfers between devices  3.17 us (12%)
  between operations  0.73 us (3%)
    pallas_call x2, Pallas kernels, body(): pl.pallas_call(functools.partial(project_kernel, (by, 2, local, angle_tot...  6.06 us
    ppermute x3, starting transfers between devices, joint(): return lax.ppermute(cut[turn], ('angle', 'tile'), pairs)  5.64 us
    pallas_call x4, Pallas kernels, hats_of(): pl.pallas_call(functools.partial(hat_kernel, (part, half, tile_rows, angl...  5.05 us
    ppermute x3, starting transfers between devices, swapped(): lax.ppermute(value, axis, [(i, i ^ by) for i in range(lax.axis_size(axis))])  3.55 us
    pallas_call x1, Pallas kernels, body(): pl.pallas_call(functools.partial(filter_kernel, (tiles, outs, first_bin))...  1.92 us
    ppermute x3, waiting for transfers between devices, swapped(): lax.ppermute(value, axis, [(i, i ^ by) for i in range(lax.axis_size(axis))])  1.62 us
    ppermute x3, waiting for transfers between devices, joint(): return lax.ppermute(cut[turn], ('angle', 'tile'), pairs)  1.55 us
  transfers between devices with their start and end apart: 7, of which 4 were waited for; matrix products, arithmetic and copies ran while one was open for 0% of the time, Pallas kernels for 29%

profile of v2, /device:TPU:0, one launch (start us, length us, event | category | flops | bytes accessed | tf_op | source)
XLA Modules:
  0.0 26.3 jit_solution(8441550932983256740)
XLA Ops:
  0.7 1.9 %filter.1 = (bf16[32,384]{1,0:T(8,128)(2,1)S(1)}, bf16[32,384]{1,0:T(8,128)(2,1)S(1)}, f32[8,128]{1,0:T(8,128)S(1)}) custom-call(f32[1]{0:T(128)S(6)} %copy.5.width, s32[2,32]{1,0:T(2,128)} %bitcast.14, f32[16,8,128]{2,1,0:T(8,128)} %constant.2.clone.table, f32[2,16,4096]{2,1,0:T(8,128)} %rows_ref.1), custom_call_target="tpu_custom_call" | custom-call | tf_op jit(solution)/shard_map/filter/pallas_call | solution.py:282
  2.6 4.1 %collective-permute-start.1 = (bf16[32,384]{1,0:T(8,128)(2,1)S(1)}, bf16[32,384]{1,0:T(8,128)(2,1)S(1)}, u32[]{:S(2)}, u32[]{:S(2)}) collective-permute-start(bf16[32,384]{1,0:T(8,128)(2,1)S(1)} %get-tuple-element.21), channel_id=1, source_target_pairs={{0,8},{1,9},{2,10},{3,11},{4,12},{5,13},{6,14},{7,15},{8,0},{9,1},... | collective-permute-start | bytes 73736 | tf_op jit(solution)/shard_map/ppermute | solution.py:336
  6.7 1.3 %collective-permute-start.2 = (bf16[32,384]{1,0:T(8,128)(2,1)S(1)}, bf16[32,384]{1,0:T(8,128)(2,1)S(1)}, u32[]{:S(2)}, u32[]{:S(2)}) collective-permute-start(bf16[32,384]{1,0:T(8,128)(2,1)S(1)} %get-tuple-element.22), channel_id=1, source_target_pairs={{0,9},{1,8},{2,11},{3,10},{4,13},{5,12},{6,15},{7,14},{8,1},{9,0},... | collective-permute-start | bytes 73736 | tf_op jit(solution)/shard_map/ppermute | solution.py:336
  8.0 0.2 collective-permute-start
  8.2 1.3 %hats.5.refs_1_ = bf16[8,512,256]{2,1,0:T(8,128)(2,1)S(1)} custom-call(f32[8,128]{1,0:T(8,128)S(1)} %get-tuple-element.27.info), custom_call_target="tpu_custom_call" | custom-call | flops 16777216 | tf_op jit(solution)/shard_map/hats/pallas_call | solution.py:308
  9.5 1.3 %hats.4.refs_0_ = bf16[8,512,256]{2,1,0:T(8,128)(2,1)S(1)} custom-call(f32[8,128]{1,0:T(8,128)S(1)} %get-tuple-element.27.info), custom_call_target="tpu_custom_call" | custom-call | flops 16777216 | tf_op jit(solution)/shard_map/hats/pallas_call | solution.py:308
  10.8 0.0 collective-permute-done.1
  10.8 1.5 %collective-permute-done.2 = bf16[32,384]{1,0:T(8,128)(2,1)S(1)} collective-permute-done((bf16[32,384]{1,0:T(8,128)(2,1)S(1)}, bf16[32,384]{1,0:T(8,128)(2,1)S(1)}, u32[]{:S(2)}, u32[]{:S(2)}) %collective-permute-start.2) | collective-permute-done | bytes 24608 | tf_op jit(solution)/shard_map/ppermute | solution.py:336
  12.3 0.0 collective-permute-done
  12.3 2.6 %collective-permute-start.5 = (bf16[2,2,32,384]{3,2,1,0:T(8,128)(2,1)S(1)}, bf16[2,2,32,384]{3,2,1,0:T(8,128)(2,1)S(1)}, u32[]{:S(2)}, u32[]{:S(2)}) collective-permute-start(bf16[2,2,32,384]{3,2,1,0:T(8,128)(2,1)S(1)} %bitcast.7), channel_id=1, source_target_pairs={{0,6},{2,4},{4,2},{6,0},{8,14},{10,12},{12,10},{14,8},{1,7},{3,5},... | collective-permute-start | bytes 294920 | tf_op jit(solution)/shard_map/ppermute | solution.py:230
  14.9 0.5 %collective-permute-start.4 = (bf16[2,2,32,384]{3,2,1,0:T(8,128)(2,1)S(1)}, bf16[2,2,32,384]{3,2,1,0:T(8,128)(2,1)S(1)}, u32[]{:S(2)}, u32[]{:S(2)}) collective-permute-start(bf16[2,2,32,384]{3,2,1,0:T(8,128)(2,1)S(1)} %bitcast.8), channel_id=1, source_target_pairs={{0,2},{2,0},{4,6},{6,4},{8,10},{10,8},{12,14},{14,12},{1,3},{3,1},... | collective-permute-start | bytes 294920 | tf_op jit(solution)/shard_map/ppermute | solution.py:230
  15.4 0.4 %collective-permute-start.3 = (bf16[2,2,32,384]{3,2,1,0:T(8,128)(2,1)S(1)}, bf16[2,2,32,384]{3,2,1,0:T(8,128)(2,1)S(1)}, u32[]{:S(2)}, u32[]{:S(2)}) collective-permute-start(bf16[2,2,32,384]{3,2,1,0:T(8,128)(2,1)S(1)} %bitcast.9), channel_id=1, source_target_pairs={{0,4},{2,6},{4,0},{6,2},{8,12},{10,14},{12,8},{14,10},{1,5},{3,7},... | collective-permute-start | bytes 294920 | tf_op jit(solution)/shard_map/ppermute | solution.py:230
  15.9 1.3 %hats.7.refs_1_ = bf16[8,512,256]{2,1,0:T(8,128)(2,1)S(1)} custom-call(f32[8,128]{1,0:T(8,128)S(1)} %get-tuple-element.27.info), custom_call_target="tpu_custom_call" | custom-call | flops 16777216 | tf_op jit(solution)/shard_map/hats/pallas_call | solution.py:308
  17.2 1.3 %hats.6.refs_0_ = bf16[8,512,256]{2,1,0:T(8,128)(2,1)S(1)} custom-call(f32[8,128]{1,0:T(8,128)S(1)} %get-tuple-element.27.info), custom_call_target="tpu_custom_call" | custom-call | flops 16777216 | tf_op jit(solution)/shard_map/hats/pallas_call | solution.py:308
  18.4 0.6 %collective-permute-done.5 = bf16[2,2,32,384]{3,2,1,0:T(8,128)(2,1)S(1)} collective-permute-done((bf16[2,2,32,384]{3,2,1,0:T(8,128)(2,1)S(1)}, bf16[2,2,32,384]{3,2,1,0:T(8,128)(2,1)S(1)}, u32[]{:S(2)}, u32[]{:S(2)}) %collective-permute-start.5) | collective-permute-done | bytes 98336 | tf_op jit(solution)/shard_map/ppermute | solution.py:230
  19.0 0.8 %collective-permute-done.4 = bf16[2,2,32,384]{3,2,1,0:T(8,128)(2,1)S(1)} collective-permute-done((bf16[2,2,32,384]{3,2,1,0:T(8,128)(2,1)S(1)}, bf16[2,2,32,384]{3,2,1,0:T(8,128)(2,1)S(1)}, u32[]{:S(2)}, u32[]{:S(2)}) %collective-permute-start.4) | collective-permute-done | bytes 98336 | tf_op jit(solution)/shard_map/ppermute | solution.py:230
  19.8 0.3 %collective-permute-done.3 = bf16[2,2,32,384]{3,2,1,0:T(8,128)(2,1)S(1)} collective-permute-done((bf16[2,2,32,384]{3,2,1,0:T(8,128)(2,1)S(1)}, bf16[2,2,32,384]{3,2,1,0:T(8,128)(2,1)S(1)}, u32[]{:S(2)}, u32[]{:S(2)}) %collective-permute-start.3) | collective-permute-done | bytes 98336 | tf_op jit(solution)/shard_map/ppermute | solution.py:230
  20.1 0.1 pad_maximum_fusion.windows
  20.1 0.1 collective-permute-start.6
  20.2 2.6 %project.2.refs_2_ = f32[8,32,256]{2,1,0:T(8,128)S(1)} custom-call(f32[8,128]{1,0:T(8,128)S(1)} %get-tuple-element.27.info, bf16[8,2,32,384]{3,2,1,0:T(8,128)(2,1)S(1)} %pad_maximum_fusion.windows, bf16[8,512,256]{2,1,0:T(8,128)(2,1)S(1)} %hats.4.refs_0_, bf16[8,512,256]{2,1,0:T(8,128)(2,1)S(1)} %hats.5.refs_1_), custom_call_target="tpu_custom_call" | custom-call | flops 2147483648 | tf_op jit(solution)/shard_map/project/pallas_call | solution.py:351
  22.8 0.0 collective-permute-done.6.windows
  22.8 3.5 %project.3 = f32[1,32,2048]{2,1,0:T(8,128)} custom-call(f32[8,128]{1,0:T(8,128)S(1)} %get-tuple-element.27.info, bf16[8,2,32,384]{3,2,1,0:T(8,128)(2,1)S(1)} %collective-permute-done.6.windows, bf16[8,512,256]{2,1,0:T(8,128)(2,1)S(1)} %hats.6.refs_0_, bf16[8,512,256]{2,1,0:T(8,128)(2,1)S(1)} %hats.7.refs_1_, f32[8,32,256]{2,1,0:T(8,128)S(1)} %project.2.refs_2_), custom_call_target="tpu_custom_call" | custom-call | flops 2147483648 | tf_op jit(solution)/shard_map/project/pallas_call | solution.py:351
  (1 shorter events, 0.0 us)
Async XLA Ops:
  2.6 8.2 %collective-permute-start.1 = (bf16[32,384]{1,0:T(8,128)(2,1)S(1)}, bf16[32,384]{1,0:T(8,128)(2,1)S(1)}, u32[]{:S(2)}, u32[]{:S(2)}) collective-permute-start(bf16[32,384]{1,0:T(8,128)(2,1)S(1)} %get-tuple-element.21), channel_id=1, source_target_pairs={{0,8},{1,9},{2,10},{3,11},{4,12},{5,13},{6,14},{7,15},{8,0},{9,1},... | collective-permute-start | bytes 73736 | tf_op jit(solution)/shard_map/ppermute | solution.py:336
  6.7 5.6 %collective-permute-start.2 = (bf16[32,384]{1,0:T(8,128)(2,1)S(1)}, bf16[32,384]{1,0:T(8,128)(2,1)S(1)}, u32[]{:S(2)}, u32[]{:S(2)}) collective-permute-start(bf16[32,384]{1,0:T(8,128)(2,1)S(1)} %get-tuple-element.22), channel_id=1, source_target_pairs={{0,9},{1,8},{2,11},{3,10},{4,13},{5,12},{6,15},{7,14},{8,1},{9,0},... | collective-permute-start | bytes 73736 | tf_op jit(solution)/shard_map/ppermute | solution.py:336
  8.0 4.3 %collective-permute-start = (bf16[32,384]{1,0:T(8,128)(2,1)S(1)}, bf16[32,384]{1,0:T(8,128)(2,1)S(1)}, u32[]{:S(2)}, u32[]{:S(2)}) collective-permute-start(bf16[32,384]{1,0:T(8,128)(2,1)S(1)} %get-tuple-element.22), channel_id=1, source_target_pairs={{0,1},{1,0},{2,3},{3,2},{4,5},{5,4},{6,7},{7,6},{8,9},{9,8},{10,11... | collective-permute-start | bytes 73736 | tf_op jit(solution)/shard_map/ppermute | solution.py:336
  12.3 6.7 %collective-permute-start.5 = (bf16[2,2,32,384]{3,2,1,0:T(8,128)(2,1)S(1)}, bf16[2,2,32,384]{3,2,1,0:T(8,128)(2,1)S(1)}, u32[]{:S(2)}, u32[]{:S(2)}) collective-permute-start(bf16[2,2,32,384]{3,2,1,0:T(8,128)(2,1)S(1)} %bitcast.7), channel_id=1, source_target_pairs={{0,6},{2,4},{4,2},{6,0},{8,14},{10,12},{12,10},{14,8},{1,7},{3,5},... | collective-permute-start | bytes 294920 | tf_op jit(solution)/shard_map/ppermute | solution.py:230
  14.9 4.9 %collective-permute-start.4 = (bf16[2,2,32,384]{3,2,1,0:T(8,128)(2,1)S(1)}, bf16[2,2,32,384]{3,2,1,0:T(8,128)(2,1)S(1)}, u32[]{:S(2)}, u32[]{:S(2)}) collective-permute-start(bf16[2,2,32,384]{3,2,1,0:T(8,128)(2,1)S(1)} %bitcast.8), channel_id=1, source_target_pairs={{0,2},{2,0},{4,6},{6,4},{8,10},{10,8},{12,14},{14,12},{1,3},{3,1},... | collective-permute-start | bytes 294920 | tf_op jit(solution)/shard_map/ppermute | solution.py:230
  15.4 4.6 %collective-permute-start.3 = (bf16[2,2,32,384]{3,2,1,0:T(8,128)(2,1)S(1)}, bf16[2,2,32,384]{3,2,1,0:T(8,128)(2,1)S(1)}, u32[]{:S(2)}, u32[]{:S(2)}) collective-permute-start(bf16[2,2,32,384]{3,2,1,0:T(8,128)(2,1)S(1)} %bitcast.9), channel_id=1, source_target_pairs={{0,4},{2,6},{4,0},{6,2},{8,12},{10,14},{12,8},{14,10},{1,5},{3,7},... | collective-permute-start | bytes 294920 | tf_op jit(solution)/shard_map/ppermute | solution.py:230
  20.1 2.7 %collective-permute-start.6 = (bf16[8,2,32,384]{3,2,1,0:T(8,128)(2,1)S(1)}, bf16[8,2,32,384]{3,2,1,0:T(8,128)(2,1)S(1)}, u32[]{:S(2)}, u32[]{:S(2)}) collective-permute-start(bf16[8,2,32,384]{3,2,1,0:T(8,128)(2,1)S(1)} %pad_maximum_fusion.windows), channel_id=1, source_target_pairs={{0,16},{16,0},{1,17},{17,1},{2,18},{18,2},{3,19},{19,3},{4,20},{20... | collective-permute-start | bytes 1179656 | tf_op jit(solution)/shard_map/ppermute | solution.py:226

commit v3 on v2

--- a/solution.py
+++ b/solution.py
@@ -16,7 +16,7 @@
 LANES = 128
 LANE_BITS = 7
 CHUNK = 32
-DEPTH = 48
+DEPTH = 40
 SLOT = 64
 PER = LANES // SLOT
 
@@ -45,9 +45,12 @@
     )
 
 
-def filter_kernel(plan, width, blocks_ref, table, rows_ref, *refs):
+def filter_kernel(plan, width, blocks_ref, trig_table, code_table, rows_ref, *refs):
     tiles, outs, first_bin = plan
-    outputs, (info, blocks, padded, raw, smooth, arrived) = refs[:tiles], refs[tiles:]
+    outputs, (trig, codes, blocks, padded, raw, smooth, arrived) = (
+        refs[:tiles],
+        refs[tiles:],
+    )
     local, slices, bins = rows_ref.shape
     block_total = bins // LANES
     raw_wide = raw.shape[1]
@@ -56,15 +59,15 @@
     ahead = 2 * LANES
 
     place = lax.axis_index("segment") * lax.axis_size("angle") + lax.axis_index("angle")
+    sources = [(blocks_ref, blocks), (trig_table.at[place], trig), (code_table.at[place], codes)]
+    group = math.gcd(slices, 8)
+    for angle in range(local):
+        for row in range(0, slices, group):
+            into = padded.at[angle, pl.ds(row, group), pl.ds(ahead, bins)]
+            sources.append((rows_ref.at[angle, pl.ds(row, group)], into))
     copies = [
-        pltpu.make_async_copy(blocks_ref, blocks, arrived.at[local]),
-        pltpu.make_async_copy(table.at[place], info, arrived.at[local + 1]),
-    ]
-    copies += [
-        pltpu.make_async_copy(
-            rows_ref.at[angle], padded.at[angle, :, pl.ds(ahead, bins)], arrived.at[angle]
-        )
-        for angle in range(local)
+        pltpu.make_async_copy(source, into, arrived.at[index])
+        for index, (source, into) in enumerate(sources)
     ]
     for copy in copies:
         copy.start()
@@ -120,11 +123,11 @@
             outputs[turn][:, j * LANES : (j + 1) * LANES] = part.astype(jnp.bfloat16)
 
 
-def read(info, index):
-    return info[index >> LANE_BITS, index & (LANES - 1)]
-
-
-def hat_kernel(plan, info, hats):
+def read(table, index):
+    return table[index >> LANE_BITS, index & (LANES - 1)]
+
+
+def hat_kernel(plan, trig, codes, hats):
     part, half, tile_rows, angle_total = plan
     chunks, depth, pixels = hats.shape
     count = depth // SLOT
@@ -134,84 +137,79 @@
     depth_step = lax.broadcasted_iota(jnp.int32, (8, pixels), 0).astype(jnp.float32)
     y = (lane // CHUNK).astype(jnp.float32) + first_row
     x = (lane % CHUNK).astype(jnp.float32)
-    gap = jnp.zeros((SLOT - DEPTH, pixels), jnp.bfloat16)
+    rest = jnp.zeros((-DEPTH % 16, pixels), jnp.float32)
+    gap = jnp.zeros((SLOT - DEPTH - DEPTH % 16, pixels), jnp.bfloat16)
 
     def step(index, carry):
         angle = part * count + index
-        cosine, sine = read(info, angle), read(info, angle_total + angle)
+        cosine, sine = read(trig, angle), read(trig, angle_total + angle)
         at = pl.multiple_of(index * SLOT, SLOT)
+        start = y * sine + x * cosine - depth_step
         for chunk in range(chunks):
             left = chunk * CHUNK - (TCOLS - 1) / 2.0
-            low = read(info, 2 * angle_total + angle * chunks + chunk)
-            across = (x + left) * cosine + y * sine + (half - low) - depth_step
+            code = read(codes, angle * chunks + chunk)
+            low = ((code >> LANE_BITS) * SLOT + (code & (LANES - 1))).astype(jnp.float32)
+            across = start + (left * cosine + (half - low))
             rows = [jnp.maximum(0.0, 1.0 - jnp.abs(across - 8.0 * j)) for j in range(DEPTH // 8)]
-            rows = jnp.concatenate(rows, axis=0).astype(jnp.bfloat16)
-            hats[chunk, pl.ds(at, DEPTH), :] = rows
-            hats[chunk, pl.ds(at + DEPTH, SLOT - DEPTH), :] = gap
+            rows = jnp.concatenate([*rows, rest], axis=0).astype(jnp.bfloat16)
+            hats[chunk, pl.ds(at, rows.shape[0]), :] = rows
+            hats[chunk, pl.ds(at + rows.shape[0], gap.shape[0]), :] = gap
         return carry
 
-    lax.fori_loop(0, count, step, 0)
-
-
-def project_kernel(plan, info, windows, *refs):
-    part, hat_count, local, angle_total, last = plan
-    hats, before, (out, held, cut) = refs[:hat_count], refs[hat_count:-3], refs[-3:]
-    chunks, hat_depth, pixels = hats[0].shape
-    depth = hat_count * hat_depth
+    lax.fori_loop(0, count, step, 0, unroll=2)
+
+
+def project_kernel(plan, codes, windows, hats, *refs):
+    part, local, last = plan
+    before, (out, held) = refs[:-2], refs[-2:]
+    chunks, depth, pixels = hats.shape
     sources, tiles, height, wide = windows.shape
     slices = height // local
     count = depth // SLOT
-    lane_blocks = wide // LANES
+    spread = lax.broadcasted_iota(jnp.int32, (height, LANES), 1)
     for source in range(sources):
         for turn in range(tiles):
             piece = windows[source, turn].astype(held.dtype)
-            for angle in range(local):
-                held[source * local + angle, turn * slices : (turn + 1) * slices, :] = piece[
-                    angle * slices : (angle + 1) * slices
-                ]
+            pieces = [piece[:, at : at + LANES] for at in range(0, wide, LANES)]
+            halves = [pltpu.roll(value, SLOT, 1) for value in pieces]
+            for j in range(held.shape[1]):
+                if j % 2 == 0:
+                    value = pieces[j // 2]
+                else:
+                    value = jnp.where(spread < SLOT, halves[j // 2], halves[j // 2 + 1])
+                for angle in range(local):
+                    held[source * local + angle, j, turn * slices : (turn + 1) * slices, :] = (
+                        value[angle * slices : (angle + 1) * slices]
+                    )
     lane = lax.broadcasted_iota(jnp.int32, (slices * tiles, LANES), 1)
-
-    def step(pair, carry):
-        for chunk in range(chunks):
+    sums = []
+    for chunk in range(chunks):
+        cut = []
+        for first in range(0, count, PER):
             merged = None
             for spot in range(PER):
-                index = pair * PER + spot
-                low = read(info, 2 * angle_total + (part * count + index) * chunks + chunk)
-                low = low.astype(jnp.int32)
-                block = low >> LANE_BITS
-                past = low & (LANES - 1)
-                after = jnp.minimum(block + 1, lane_blocks - 1)
-                near = pl.ds(pl.multiple_of(block * LANES, LANES), LANES)
-                far = pl.ds(pl.multiple_of(after * LANES, LANES), LANES)
-                value = jnp.where(lane >= past, held[index, :, near], held[index, :, far])
-                turn_by = (spot * SLOT + LANES - past) & (LANES - 1)
-                value = pltpu.roll(value, turn_by, 1)
+                index = first + spot
+                code = read(codes, (part * count + index) * chunks + chunk)
+                turn_by = (spot * SLOT + LANES - (code & (LANES - 1))) & (LANES - 1)
+                value = pltpu.roll(held[index, code >> LANE_BITS], turn_by, 1)
                 merged = value if spot == 0 else jnp.where(lane < spot * SLOT, merged, value)
-            at = pl.ds(pl.multiple_of(pair * LANES, LANES), LANES)
-            cut[chunk, :, at] = merged.astype(jnp.bfloat16)
-        return carry
-
-    lax.fori_loop(0, count // PER, step, 0, unroll=4)
-    sums = []
-    for chunk in range(chunks):
-        value = before[0][chunk] if before else None
-        for index, hat in enumerate(hats):
-            lanes = slice(index * hat_depth, (index + 1) * hat_depth)
-            more = jnp.dot(cut[chunk, :, lanes], hat[chunk], preferred_element_type=jnp.float32)
-            value = more if value is None else value + more
+            cut.append(merged.astype(jnp.bfloat16))
+        value = jnp.dot(
+            jnp.concatenate(cut, axis=1), hats[chunk], preferred_element_type=jnp.float32
+        )
+        if before:
+            value = value + before[0][chunk]
         sums.append(value)
         if not last:
             out[chunk] = value
-    if not last:
-        return
-    mine = lax.axis_index("tile")
-    for pair in range(TCOLS // LANES):
-        near = sums[pair * (LANES // CHUNK) : (pair + 1) * (LANES // CHUNK)]
+        if not last or (chunk + 1) * CHUNK % LANES:
+            continue
+        mine = lax.axis_index("tile")
         for row in range(ROWS_DEV):
             value = jnp.concatenate(
-                [part[:, row * CHUNK : (row + 1) * CHUNK] for part in near], axis=1
+                [part[:, row * CHUNK : (row + 1) * CHUNK] for part in sums], axis=1
             )
-            at = row * TCOLS + pair * LANES
+            at = row * TCOLS + (chunk + 1) * CHUNK - LANES
             if slices % 8 == 0:
                 for turn in range(tiles):
                     tile = lax.rem(mine + turn, tiles)
@@ -219,6 +217,7 @@
                     out[0, into, at : at + LANES] = value[turn * slices : (turn + 1) * slices]
             else:
                 out[0, :, at : at + LANES] = pltpu.roll(value, mine * slices, 0)
+        sums = []
 
 
 def shifted(value, axis, by):
@@ -273,18 +272,24 @@
     top = where * ROWS_DEV - (tile_rows - 1) / 2.0
     rise = np.minimum(sine * top, sine * (top + (ROWS_DEV - 1)))
     lows = np.floor(edges + rise[..., None] + (half - 0.01)).astype(np.int32)
-    lows = lows.astype(np.float32).reshape(groups, -1)
-    table = np.concatenate([cosine.astype(np.float32), sine.astype(np.float32), lows], axis=1)
-    info_rows = -(-table.shape[1] // (8 * LANES)) * 8
-    table = np.pad(table, ((0, 0), (0, info_rows * LANES - table.shape[1])))
-    table = jnp.asarray(table.reshape(groups, info_rows, LANES))
-
-    *cut, info = pl.pallas_call(
+    blocks = np.minimum(lows // SLOT, PER * (outs - 1))
+    codes = (blocks << LANE_BITS) + lows - blocks * SLOT
+
+    def in_rows(values):
+        values = values.reshape(groups, -1)
+        rows = -(-values.shape[1] // (8 * LANES)) * 8
+        values = np.pad(values, ((0, 0), (0, rows * LANES - values.shape[1])))
+        return jnp.asarray(values.reshape(groups, rows, LANES))
+
+    trig_table = in_rows(np.concatenate([cosine, sine], axis=1).astype(np.float32))
+    code_table = in_rows(codes.astype(np.int32))
+
+    *cut, trig, codes = pl.pallas_call(
         functools.partial(filter_kernel, (tiles, outs, first_bin)),
         out_shape=[jax.ShapeDtypeStruct((height, outs * LANES), jnp.bfloat16)] * tiles
-        + [jax.ShapeDtypeStruct((info_rows, LANES), jnp.float32)],
-        in_specs=[smem] + [pl.BlockSpec(memory_space=pltpu.HBM)] * 3,
-        out_specs=[vmem] * (tiles + 1),
+        + [jax.ShapeDtypeStruct(v.shape[1:], v.dtype) for v in (trig_table, code_table)],
+        in_specs=[smem] + [pl.BlockSpec(memory_space=pltpu.HBM)] * 4,
+        out_specs=[vmem] * (tiles + 2),
         scratch_shapes=[
             pltpu.SMEM(window_block.T.shape, jnp.int32),
             pltpu.VMEM(
@@ -293,35 +298,38 @@
             ),
             pltpu.VMEM((height * tiles, (smooth_blocks + 2) * LANES), jnp.float32),
             pltpu.VMEM((height * tiles, smooth_blocks * LANES), jnp.float32),
-            pltpu.SemaphoreType.DMA((local + 2,)),
+            pltpu.SemaphoreType.DMA((local * slices // math.gcd(slices, 8) + 3,)),
         ],
         compiler_params=params,
         name="filter",
     )(
         paganin_width,
-        *(pltpu.with_memory_space_constraint(v, pltpu.HBM) for v in (window_block.T, table, sinogram)),
+        *(
+            pltpu.with_memory_space_constraint(value, pltpu.HBM)
+            for value in (window_block.T, trig_table, code_table, sinogram)
+        ),
     )
 
-    depth = spots * local // 2 * SLOT
+    depth = spots * local * SLOT
     def hats_of(part, after):
-        ready = lax.optimization_barrier((info, *after))[0]
+        ready = lax.optimization_barrier((trig, codes, *after))[:2]
         return pl.pallas_call(
             functools.partial(hat_kernel, (part, half, tile_rows, angle_total)),
             out_shape=jax.ShapeDtypeStruct((chunks, depth, pixels), jnp.bfloat16),
-            in_specs=[smem],
+            in_specs=[smem, smem],
             out_specs=vmem,
             compiler_params=params,
             cost_estimate=pl.CostEstimate(
                 flops=chunks * depth * pixels * 16, bytes_accessed=0, transcendentals=0
             ),
             name="hats",
-        )(ready)
+        )(*ready)
 
     hats = []
 
     def beside(moved, after, count):
         made = []
-        for _ in range(min(count, 2 * segments - len(hats))):
+        for _ in range(min(count, segments - len(hats))):
             made.append(hats_of(len(hats), after))
             hats.append(None)
         moved, made = lax.optimization_barrier((moved, made))
@@ -336,12 +344,12 @@
         return lax.ppermute(cut[turn], ("angle", "tile"), pairs)
 
     near = [(turn, mask) for mask in (0, *exchanges[0]) for turn in range(tiles)][1:]
-    moved = beside([joint(*pair) for pair in near], cut, 2)
+    moved = beside([joint(*pair) for pair in near], cut, 1)
     pieces = jnp.stack([cut[0], *moved]).reshape(2, tiles, *cut[0].shape)
     for index, masks in enumerate(exchanges[1:]):
         moved = [swapped(pieces, "angle", mask) for mask in masks]
         last = index == len(exchanges) - 2
-        moved = beside(moved, (pieces,), 2 * segments if last else 2)
+        moved = beside(moved, (pieces,), segments if last else 1)
         pieces = jnp.concatenate([pieces, *moved])
     held_type = jnp.bfloat16 if slices % 16 == 0 else jnp.float32
     parts = [pieces] + [shifted(pieces, "segment", by) for by in range(1, segments)]
@@ -349,27 +357,26 @@
     for by, windows in enumerate(parts):
         last = by == segments - 1
         value = pl.pallas_call(
-            functools.partial(project_kernel, (by, 2, local, angle_total, last)),
+            functools.partial(project_kernel, (by, local, last)),
             out_shape=jax.ShapeDtypeStruct(
                 (1, slices * tiles, ROWS_DEV * TCOLS)
                 if last
                 else (chunks, slices * tiles, pixels),
                 jnp.float32,
             ),
-            in_specs=[smem] + [vmem] * (3 + len(sums)),
+            in_specs=[smem] + [vmem] * (2 + len(sums)),
             out_specs=vmem,
             scratch_shapes=[
-                pltpu.VMEM((spots * local, slices * tiles, outs * LANES), held_type),
-                pltpu.VMEM((chunks, slices * tiles, 2 * depth), jnp.bfloat16),
+                pltpu.VMEM((spots * local, PER * (outs - 1) + 1, slices * tiles, LANES), held_type),
             ],
             compiler_params=params,
             cost_estimate=pl.CostEstimate(
-                flops=64 * slices * tiles * chunks * depth * pixels,
+                flops=32 * slices * tiles * chunks * depth * pixels,
                 bytes_accessed=0,
                 transcendentals=0,
             ),
             name="project",
-        )(info, windows, *hats[2 * by : 2 * by + 2], *sums)
+        )(codes, windows, hats[by], *sums)
         sums = (value,)
     return sums[0]
 

time: 26.5 us -> 24.8 us (0.936)
  Pallas kernels: 13 us -> 9.91 us
  waiting for transfers between devices: 3.17 us -> 4.6 us
    pallas_call x2, Pallas kernels: 6.06 us -> 4.26 us  [body(): pl.pallas_call(functools.partial(project_kernel, (by, local, last)), out_...]
    pallas_call x4 -> x2, Pallas kernels: 5.05 us -> 3.62 us  [hats_of(): pl.pallas_call(functools.partial(hat_kernel, (part, half, tile_rows, angl...]
    ppermute x3, waiting for transfers between devices: 1.55 us -> 2.29 us  [joint(): return lax.ppermute(cut[turn], ('angle', 'tile'), pairs)]
    ppermute x3, waiting for transfers between devices: 1.62 us -> 2.31 us  [swapped(): lax.ppermute(value, axis, [(i, i ^ by) for i in range(lax.axis_size(axis))])]
  transfers between devices with their start and end apart: 7 -> 7, of which waited for: 4 -> 4; matrix products, arithmetic and copies ran while one was open for 0% -> 0% of each run, Pallas kernels for 29% -> 22%
where the time goes in v3:
time: 24.8 us; the launch traced here: 24.6 us
  Pallas kernels  9.91 us (40%)
  starting transfers between devices  9.27 us (37%)
  waiting for transfers between devices  4.6 us (19%)
  between operations  0.72 us (3%)
    ppermute x3, starting transfers between devices, joint(): return lax.ppermute(cut[turn], ('angle', 'tile'), pairs)  5.64 us
    pallas_call x2, Pallas kernels, body(): pl.pallas_call(functools.partial(project_kernel, (by, local, last)), out_...  4.26 us
    pallas_call x2, Pallas kernels, hats_of(): pl.pallas_call(functools.partial(hat_kernel, (part, half, tile_rows, angl...  3.62 us
    ppermute x3, starting transfers between devices, swapped(): lax.ppermute(value, axis, [(i, i ^ by) for i in range(lax.axis_size(axis))])  3.55 us
    ppermute x3, waiting for transfers between devices, swapped(): lax.ppermute(value, axis, [(i, i ^ by) for i in range(lax.axis_size(axis))])  2.31 us
    ppermute x3, waiting for transfers between devices, joint(): return lax.ppermute(cut[turn], ('angle', 'tile'), pairs)  2.29 us
    pallas_call x1, Pallas kernels, body(): pl.pallas_call(functools.partial(filter_kernel, (tiles, outs, first_bin))...  2.03 us
  transfers between devices with their start and end apart: 7, of which 4 were waited for; matrix products, arithmetic and copies ran while one was open for 0% of the time, Pallas kernels for 22%

profile of v3, /device:TPU:0, one launch (start us, length us, event | category | flops | bytes accessed | tf_op | source)
XLA Modules:
  0.0 24.6 jit_solution(1318169139961610731)
XLA Ops:
  0.7 2.0 %filter.1 = (bf16[32,384]{1,0:T(8,128)(2,1)S(1)}, bf16[32,384]{1,0:T(8,128)(2,1)S(1)}, f32[8,128]{1,0:T(8,128)S(1)}, s32[8,128]{1,0:T(8,128)S(1)}) custom-call(f32[1]{0:T(128)S(6)} %copy.6.width, s32[2,32]{1,0:T(2,128)} %bitcast.14, f32[16,8,128]{2,1,0:T(8,128)} %constant.4.clone.trig_table, s32[16,8,128]{2,1,0:T(8,128)} %constant.5.clone.code_table, ...), custom_call_target="tpu_custom_call" | custom-call | tf_op jit(solution)/shard_map/filter/pallas_call | solution.py:287
  2.7 4.1 %collective-permute-start.1 = (bf16[32,384]{1,0:T(8,128)(2,1)S(1)}, bf16[32,384]{1,0:T(8,128)(2,1)S(1)}, u32[]{:S(2)}, u32[]{:S(2)}) collective-permute-start(bf16[32,384]{1,0:T(8,128)(2,1)S(1)} %get-tuple-element.22), channel_id=1, source_target_pairs={{0,8},{1,9},{2,10},{3,11},{4,12},{5,13},{6,14},{7,15},{8,0},{9,1},... | collective-permute-start | bytes 73736 | tf_op jit(solution)/shard_map/ppermute | solution.py:344
  6.8 1.3 %collective-permute-start.2 = (bf16[32,384]{1,0:T(8,128)(2,1)S(1)}, bf16[32,384]{1,0:T(8,128)(2,1)S(1)}, u32[]{:S(2)}, u32[]{:S(2)}) collective-permute-start(bf16[32,384]{1,0:T(8,128)(2,1)S(1)} %get-tuple-element.23), channel_id=1, source_target_pairs={{0,9},{1,8},{2,11},{3,10},{4,13},{5,12},{6,15},{7,14},{8,1},{9,0},... | collective-permute-start | bytes 73736 | tf_op jit(solution)/shard_map/ppermute | solution.py:344
  8.1 0.3 %collective-permute-start = (bf16[32,384]{1,0:T(8,128)(2,1)S(1)}, bf16[32,384]{1,0:T(8,128)(2,1)S(1)}, u32[]{:S(2)}, u32[]{:S(2)}) collective-permute-start(bf16[32,384]{1,0:T(8,128)(2,1)S(1)} %get-tuple-element.23), channel_id=1, source_target_pairs={{0,1},{1,0},{2,3},{3,2},{4,5},{5,4},{6,7},{7,6},{8,9},{9,8},{10,11... | collective-permute-start | bytes 73736 | tf_op jit(solution)/shard_map/ppermute | solution.py:344
  8.3 1.8 %hats.2 = bf16[8,1024,256]{2,1,0:T(8,128)(2,1)S(1)} custom-call(f32[8,128]{1,0:T(8,128)S(1)} %get-tuple-element.30.trig, s32[8,128]{1,0:T(8,128)S(1)} %get-tuple-element.31.codes), custom_call_target="tpu_custom_call" | custom-call | flops 33554432 | tf_op jit(solution)/shard_map/hats/pallas_call | solution.py:316
  10.1 0.0 collective-permute-done.1
  10.1 2.3 %collective-permute-done.2 = bf16[32,384]{1,0:T(8,128)(2,1)S(1)} collective-permute-done((bf16[32,384]{1,0:T(8,128)(2,1)S(1)}, bf16[32,384]{1,0:T(8,128)(2,1)S(1)}, u32[]{:S(2)}, u32[]{:S(2)}) %collective-permute-start.2) | collective-permute-done | bytes 24608 | tf_op jit(solution)/shard_map/ppermute | solution.py:344
  12.4 0.0 collective-permute-done
  12.4 2.6 %collective-permute-start.5 = (bf16[2,2,32,384]{3,2,1,0:T(8,128)(2,1)S(1)}, bf16[2,2,32,384]{3,2,1,0:T(8,128)(2,1)S(1)}, u32[]{:S(2)}, u32[]{:S(2)}) collective-permute-start(bf16[2,2,32,384]{3,2,1,0:T(8,128)(2,1)S(1)} %bitcast.7), channel_id=1, source_target_pairs={{0,6},{2,4},{4,2},{6,0},{8,14},{10,12},{12,10},{14,8},{1,7},{3,5},... | collective-permute-start | bytes 294920 | tf_op jit(solution)/shard_map/ppermute | solution.py:229
  15.0 0.5 %collective-permute-start.4 = (bf16[2,2,32,384]{3,2,1,0:T(8,128)(2,1)S(1)}, bf16[2,2,32,384]{3,2,1,0:T(8,128)(2,1)S(1)}, u32[]{:S(2)}, u32[]{:S(2)}) collective-permute-start(bf16[2,2,32,384]{3,2,1,0:T(8,128)(2,1)S(1)} %bitcast.8), channel_id=1, source_target_pairs={{0,2},{2,0},{4,6},{6,4},{8,10},{10,8},{12,14},{14,12},{1,3},{3,1},... | collective-permute-start | bytes 294920 | tf_op jit(solution)/shard_map/ppermute | solution.py:229
  15.5 0.5 %collective-permute-start.3 = (bf16[2,2,32,384]{3,2,1,0:T(8,128)(2,1)S(1)}, bf16[2,2,32,384]{3,2,1,0:T(8,128)(2,1)S(1)}, u32[]{:S(2)}, u32[]{:S(2)}) collective-permute-start(bf16[2,2,32,384]{3,2,1,0:T(8,128)(2,1)S(1)} %bitcast.9), channel_id=1, source_target_pairs={{0,4},{2,6},{4,0},{6,2},{8,12},{10,14},{12,8},{14,10},{1,5},{3,7},... | collective-permute-start | bytes 294920 | tf_op jit(solution)/shard_map/ppermute | solution.py:229
  16.0 1.8 %hats.3 = bf16[8,1024,256]{2,1,0:T(8,128)(2,1)S(1)} custom-call(f32[8,128]{1,0:T(8,128)S(1)} %get-tuple-element.30.trig, s32[8,128]{1,0:T(8,128)S(1)} %get-tuple-element.31.codes), custom_call_target="tpu_custom_call" | custom-call | flops 33554432 | tf_op jit(solution)/shard_map/hats/pallas_call | solution.py:316
  17.8 1.3 %collective-permute-done.5 = bf16[2,2,32,384]{3,2,1,0:T(8,128)(2,1)S(1)} collective-permute-done((bf16[2,2,32,384]{3,2,1,0:T(8,128)(2,1)S(1)}, bf16[2,2,32,384]{3,2,1,0:T(8,128)(2,1)S(1)}, u32[]{:S(2)}, u32[]{:S(2)}) %collective-permute-start.5) | collective-permute-done | bytes 98336 | tf_op jit(solution)/shard_map/ppermute | solution.py:229
  19.1 0.8 %collective-permute-done.4 = bf16[2,2,32,384]{3,2,1,0:T(8,128)(2,1)S(1)} collective-permute-done((bf16[2,2,32,384]{3,2,1,0:T(8,128)(2,1)S(1)}, bf16[2,2,32,384]{3,2,1,0:T(8,128)(2,1)S(1)}, u32[]{:S(2)}, u32[]{:S(2)}) %collective-permute-start.4) | collective-permute-done | bytes 98336 | tf_op jit(solution)/shard_map/ppermute | solution.py:229
  19.9 0.3 %collective-permute-done.3 = bf16[2,2,32,384]{3,2,1,0:T(8,128)(2,1)S(1)} collective-permute-done((bf16[2,2,32,384]{3,2,1,0:T(8,128)(2,1)S(1)}, bf16[2,2,32,384]{3,2,1,0:T(8,128)(2,1)S(1)}, u32[]{:S(2)}, u32[]{:S(2)}) %collective-permute-start.3) | collective-permute-done | bytes 98336 | tf_op jit(solution)/shard_map/ppermute | solution.py:229
  20.2 0.1 pad_maximum_fusion.windows
  20.2 0.1 collective-permute-start.6
  20.3 1.7 %project.2.refs_0_ = f32[8,32,256]{2,1,0:T(8,128)S(1)} custom-call(s32[8,128]{1,0:T(8,128)S(1)} %get-tuple-element.31.codes, bf16[8,2,32,384]{3,2,1,0:T(8,128)(2,1)S(1)} %pad_maximum_fusion.windows, bf16[8,1024,256]{2,1,0:T(8,128)(2,1)S(1)} %hats.2), custom_call_target="tpu_custom_call" | custom-call | flops 2147483648 | tf_op jit(solution)/shard_map/project/pallas_call | solution.py:359
  22.0 0.0 collective-permute-done.6.windows
  22.1 2.5 %project.3 = f32[1,32,2048]{2,1,0:T(8,128)} custom-call(s32[8,128]{1,0:T(8,128)S(1)} %get-tuple-element.31.codes, bf16[8,2,32,384]{3,2,1,0:T(8,128)(2,1)S(1)} %collective-permute-done.6.windows, bf16[8,1024,256]{2,1,0:T(8,128)(2,1)S(1)} %hats.3, f32[8,32,256]{2,1,0:T(8,128)S(1)} %project.2.refs_0_), custom_call_target="tpu_custom_call" | custom-call | flops 2147483648 | tf_op jit(solution)/shard_map/project/pallas_call | solution.py:359
  (1 shorter events, 0.0 us)
Async XLA Ops:
  2.7 7.4 %collective-permute-start.1 = (bf16[32,384]{1,0:T(8,128)(2,1)S(1)}, bf16[32,384]{1,0:T(8,128)(2,1)S(1)}, u32[]{:S(2)}, u32[]{:S(2)}) collective-permute-start(bf16[32,384]{1,0:T(8,128)(2,1)S(1)} %get-tuple-element.22), channel_id=1, source_target_pairs={{0,8},{1,9},{2,10},{3,11},{4,12},{5,13},{6,14},{7,15},{8,0},{9,1},... | collective-permute-start | bytes 73736 | tf_op jit(solution)/shard_map/ppermute | solution.py:344
  6.8 5.6 %collective-permute-start.2 = (bf16[32,384]{1,0:T(8,128)(2,1)S(1)}, bf16[32,384]{1,0:T(8,128)(2,1)S(1)}, u32[]{:S(2)}, u32[]{:S(2)}) collective-permute-start(bf16[32,384]{1,0:T(8,128)(2,1)S(1)} %get-tuple-element.23), channel_id=1, source_target_pairs={{0,9},{1,8},{2,11},{3,10},{4,13},{5,12},{6,15},{7,14},{8,1},{9,0},... | collective-permute-start | bytes 73736 | tf_op jit(solution)/shard_map/ppermute | solution.py:344
  8.1 4.3 %collective-permute-start = (bf16[32,384]{1,0:T(8,128)(2,1)S(1)}, bf16[32,384]{1,0:T(8,128)(2,1)S(1)}, u32[]{:S(2)}, u32[]{:S(2)}) collective-permute-start(bf16[32,384]{1,0:T(8,128)(2,1)S(1)} %get-tuple-element.23), channel_id=1, source_target_pairs={{0,1},{1,0},{2,3},{3,2},{4,5},{5,4},{6,7},{7,6},{8,9},{9,8},{10,11... | collective-permute-start | bytes 73736 | tf_op jit(solution)/shard_map/ppermute | solution.py:344
  12.4 6.7 %collective-permute-start.5 = (bf16[2,2,32,384]{3,2,1,0:T(8,128)(2,1)S(1)}, bf16[2,2,32,384]{3,2,1,0:T(8,128)(2,1)S(1)}, u32[]{:S(2)}, u32[]{:S(2)}) collective-permute-start(bf16[2,2,32,384]{3,2,1,0:T(8,128)(2,1)S(1)} %bitcast.7), channel_id=1, source_target_pairs={{0,6},{2,4},{4,2},{6,0},{8,14},{10,12},{12,10},{14,8},{1,7},{3,5},... | collective-permute-start | bytes 294920 | tf_op jit(solution)/shard_map/ppermute | solution.py:229
  15.0 4.9 %collective-permute-start.4 = (bf16[2,2,32,384]{3,2,1,0:T(8,128)(2,1)S(1)}, bf16[2,2,32,384]{3,2,1,0:T(8,128)(2,1)S(1)}, u32[]{:S(2)}, u32[]{:S(2)}) collective-permute-start(bf16[2,2,32,384]{3,2,1,0:T(8,128)(2,1)S(1)} %bitcast.8), channel_id=1, source_target_pairs={{0,2},{2,0},{4,6},{6,4},{8,10},{10,8},{12,14},{14,12},{1,3},{3,1},... | collective-permute-start | bytes 294920 | tf_op jit(solution)/shard_map/ppermute | solution.py:229
  15.5 4.6 %collective-permute-start.3 = (bf16[2,2,32,384]{3,2,1,0:T(8,128)(2,1)S(1)}, bf16[2,2,32,384]{3,2,1,0:T(8,128)(2,1)S(1)}, u32[]{:S(2)}, u32[]{:S(2)}) collective-permute-start(bf16[2,2,32,384]{3,2,1,0:T(8,128)(2,1)S(1)} %bitcast.9), channel_id=1, source_target_pairs={{0,4},{2,6},{4,0},{6,2},{8,12},{10,14},{12,8},{14,10},{1,5},{3,7},... | collective-permute-start | bytes 294920 | tf_op jit(solution)/shard_map/ppermute | solution.py:229
  20.2 1.8 %collective-permute-start.6 = (bf16[8,2,32,384]{3,2,1,0:T(8,128)(2,1)S(1)}, bf16[8,2,32,384]{3,2,1,0:T(8,128)(2,1)S(1)}, u32[]{:S(2)}, u32[]{:S(2)}) collective-permute-start(bf16[8,2,32,384]{3,2,1,0:T(8,128)(2,1)S(1)} %pad_maximum_fusion.windows), channel_id=1, source_target_pairs={{0,16},{16,0},{1,17},{17,1},{2,18},{18,2},{3,19},{19,3},{4,20},{20... | collective-permute-start | bytes 1179656 | tf_op jit(solution)/shard_map/ppermute | solution.py:225

commit v4 on v3

--- a/solution.py
+++ b/solution.py
@@ -46,7 +46,8 @@
 
 
 def filter_kernel(plan, width, blocks_ref, trig_table, code_table, rows_ref, *refs):
-    tiles, outs, first_bin = plan
+    tiles, outs, first_bin, packing = plan
+    full, rows_of_block, groups = packing
     outputs, (trig, codes, blocks, padded, raw, smooth, arrived) = (
         refs[:tiles],
         refs[tiles:],
@@ -59,12 +60,13 @@
     ahead = 2 * LANES
 
     place = lax.axis_index("segment") * lax.axis_size("angle") + lax.axis_index("angle")
-    sources = [(blocks_ref, blocks), (trig_table.at[place], trig), (code_table.at[place], codes)]
-    group = math.gcd(slices, 8)
-    for angle in range(local):
-        for row in range(0, slices, group):
-            into = padded.at[angle, pl.ds(row, group), pl.ds(ahead, bins)]
-            sources.append((rows_ref.at[angle, pl.ds(row, group)], into))
+    sources = [(rows_ref.at[i], padded.at[i, :, pl.ds(ahead, bins)]) for i in range(local)]
+    sources = [
+        *sources,
+        (blocks_ref, blocks),
+        (trig_table.at[place], trig),
+        (code_table.at[place], codes),
+    ]
     copies = [
         pltpu.make_async_copy(source, into, arrived.at[index])
         for index, (source, into) in enumerate(sources)
@@ -75,6 +77,12 @@
     padded[:, :, :ahead] = jnp.zeros((local, slices, ahead), jnp.float32)
     padded[:, :, ahead + bins :] = jnp.zeros((local, slices, behind), jnp.float32)
 
+    away = offsets(512, LANES, BAND + first_bin)
+    spread = jnp.abs(away)
+    squared = jnp.maximum(spread * spread, 1).astype(jnp.float32)
+    odd = jnp.logical_and(spread <= BAND, (spread & 1) == 1)
+    ramp = jnp.where(odd, -1.0 / (math.pi * math.pi * squared), 0.0)
+    ramp = split(jnp.where(away == 0, 0.25, ramp))
     decay = width[0]
     steps = (lax.broadcasted_iota(jnp.int32, (1, BAND), 1) + 1).astype(jnp.float32)
     total = 1.0 + 2.0 * jnp.sum(jnp.exp(-steps / decay), axis=1, keepdims=True)
@@ -84,12 +92,6 @@
         spread <= BAND, jnp.exp(-spread.astype(jnp.float32) / decay) / total, 0.0
     )
     paganin = split(paganin)
-    away = offsets(512, LANES, BAND + first_bin)
-    spread = jnp.abs(away)
-    squared = jnp.maximum(spread * spread, 1).astype(jnp.float32)
-    odd = jnp.logical_and(spread <= BAND, (spread & 1) == 1)
-    ramp = jnp.where(odd, -1.0 / (math.pi * math.pi * squared), 0.0)
-    ramp = split(jnp.where(away == 0, 0.25, ramp))
 
     for copy in copies:
         copy.wait()
@@ -120,7 +122,29 @@
     for j, value in enumerate(banded(smooth[...], ramp, lanes)):
         for turn in range(tiles):
             part = value[turn * height : (turn + 1) * height]
-            outputs[turn][:, j * LANES : (j + 1) * LANES] = part.astype(jnp.bfloat16)
+            if j == full:
+                part = pack(part, groups)
+            if part.shape[0] % 16:
+                rest = jnp.zeros((-part.shape[0] % 16, LANES), jnp.float32)
+                part = jnp.concatenate([part, rest], axis=0)
+            at = j * rows_of_block
+            outputs[turn][at : at + part.shape[0], :] = part.astype(jnp.bfloat16)
+
+
+def pack(value, groups):
+    rows, wide = value.shape[0] // groups, LANES // groups
+    lane = lax.broadcasted_iota(jnp.int32, (rows, LANES), 1)
+    packed = value[:rows]
+    for group in range(1, groups):
+        more = pltpu.roll(value[group * rows : (group + 1) * rows], group * wide, 1)
+        packed = jnp.where(lane < group * wide, packed, more)
+    return packed
+
+
+def unpack(value, groups):
+    wide = LANES // groups
+    rolled = [pltpu.roll(value, (LANES - group * wide) % LANES, 1) for group in range(groups)]
+    return jnp.concatenate(rolled, axis=0)
 
 
 def read(table, index):
@@ -160,17 +184,27 @@
 
 
 def project_kernel(plan, codes, windows, hats, *refs):
-    part, local, last = plan
+    part, local, last, tiles, height, packing = plan
+    full, rows_of_block, groups = packing
     before, (out, held) = refs[:-2], refs[-2:]
     chunks, depth, pixels = hats.shape
-    sources, tiles, height, wide = windows.shape
+    sources = windows.shape[0]
+    tail_first = tiles * full * rows_of_block
     slices = height // local
     count = depth // SLOT
     spread = lax.broadcasted_iota(jnp.int32, (height, LANES), 1)
     for source in range(sources):
+        if groups > 1:
+            tails = windows[source, tail_first:, :].astype(jnp.float32)
         for turn in range(tiles):
-            piece = windows[source, turn].astype(held.dtype)
-            pieces = [piece[:, at : at + LANES] for at in range(0, wide, LANES)]
+            pieces = []
+            for j in range(full):
+                rows = pl.ds((turn * full + j) * rows_of_block, rows_of_block)
+                pieces.append(windows[source, rows, :].astype(held.dtype)[:height])
+            if groups > 1:
+                tail = height // groups
+                tail = tails[turn * tail : (turn + 1) * tail]
+                pieces.append(unpack(tail, groups).astype(held.dtype))
             halves = [pltpu.roll(value, SLOT, 1) for value in pieces]
             for j in range(held.shape[1]):
                 if j % 2 == 0:
@@ -252,6 +286,14 @@
     params = pltpu.CompilerParams(vmem_limit_bytes=hat_bytes + 12 * 1024 * 1024)
     height = local * slices
     block_total = bins // LANES
+    used = last_bin + 1 - first_bin - (outs - 1) * LANES
+    row_groups = LANES // (1 << (used - 1).bit_length())
+    if height % (8 * row_groups):
+        row_groups = 1
+    full = outs if row_groups == 1 else outs - 1
+    rows_of_block = -(-height // 16) * 16
+    tail = 0 if row_groups == 1 else height // row_groups
+    packing = (full, rows_of_block, row_groups)
     bits = [1 << bit for bit in reversed(range(spots.bit_length() - 1))]
     exchanges = [(bits[0],)]
     for first in range(1, len(bits), 2):
@@ -285,8 +327,11 @@
     code_table = in_rows(codes.astype(np.int32))
 
     *cut, trig, codes = pl.pallas_call(
-        functools.partial(filter_kernel, (tiles, outs, first_bin)),
-        out_shape=[jax.ShapeDtypeStruct((height, outs * LANES), jnp.bfloat16)] * tiles
+        functools.partial(filter_kernel, (tiles, outs, first_bin, packing)),
+        out_shape=[
+            jax.ShapeDtypeStruct((full * rows_of_block + -(-tail // 16) * 16, LANES), jnp.bfloat16)
+        ]
+        * tiles
         + [jax.ShapeDtypeStruct(v.shape[1:], v.dtype) for v in (trig_table, code_table)],
         in_specs=[smem] + [pl.BlockSpec(memory_space=pltpu.HBM)] * 4,
         out_specs=[vmem] * (tiles + 2),
@@ -298,7 +343,7 @@
             ),
             pltpu.VMEM((height * tiles, (smooth_blocks + 2) * LANES), jnp.float32),
             pltpu.VMEM((height * tiles, smooth_blocks * LANES), jnp.float32),
-            pltpu.SemaphoreType.DMA((local * slices // math.gcd(slices, 8) + 3,)),
+            pltpu.SemaphoreType.DMA((local + 3,)),
         ],
         compiler_params=params,
         name="filter",
@@ -345,7 +390,14 @@
 
     near = [(turn, mask) for mask in (0, *exchanges[0]) for turn in range(tiles)][1:]
     moved = beside([joint(*pair) for pair in near], cut, 1)
-    pieces = jnp.stack([cut[0], *moved]).reshape(2, tiles, *cut[0].shape)
+    pieces = jnp.stack([cut[0], *moved])
+    whole = full * rows_of_block
+    if tail:
+        main = pieces[:, :whole].reshape(2, tiles * whole, LANES)
+        tails = pieces[:, whole : whole + tail].reshape(2, tiles * tail, LANES)
+        pieces = jnp.concatenate([main, tails], axis=1)
+    else:
+        pieces = pieces.reshape(2, tiles * whole, LANES)
     for index, masks in enumerate(exchanges[1:]):
         moved = [swapped(pieces, "angle", mask) for mask in masks]
         last = index == len(exchanges) - 2
@@ -357,7 +409,7 @@
     for by, windows in enumerate(parts):
         last = by == segments - 1
         value = pl.pallas_call(
-            functools.partial(project_kernel, (by, local, last)),
+            functools.partial(project_kernel, (by, local, last, tiles, height, packing)),
             out_shape=jax.ShapeDtypeStruct(
                 (1, slices * tiles, ROWS_DEV * TCOLS)
                 if last

time: 24.8 us -> 24.5 us (0.988)
  waiting for transfers between devices: 4.6 us -> 4.3 us
    ppermute x3, waiting for transfers between devices: 2.31 us -> 2.05 us  [swapped(): lax.ppermute(value, axis, [(i, i ^ by) for i in range(lax.axis_size(axis))])]
where the time goes in v4:
time: 24.5 us; the launch traced here: 24.3 us
  Pallas kernels  9.92 us (40%)
  starting transfers between devices  9.27 us (38%)
  waiting for transfers between devices  4.3 us (18%)
  between operations  0.74 us (3%)
    ppermute x3, starting transfers between devices, joint(): return lax.ppermute(cut[turn], ('angle', 'tile'), pairs)  5.64 us
    pallas_call x2, Pallas kernels, body(): pl.pallas_call(functools.partial(project_kernel, (by, local, last, tiles,...  4.3 us
    pallas_call x2, Pallas kernels, hats_of(): pl.pallas_call(functools.partial(hat_kernel, (part, half, tile_rows, angl...  3.62 us
    ppermute x3, starting transfers between devices, swapped(): lax.ppermute(value, axis, [(i, i ^ by) for i in range(lax.axis_size(axis))])  3.55 us
    ppermute x3, waiting for transfers between devices, joint(): return lax.ppermute(cut[turn], ('angle', 'tile'), pairs)  2.25 us
    ppermute x3, waiting for transfers between devices, swapped(): lax.ppermute(value, axis, [(i, i ^ by) for i in range(lax.axis_size(axis))])  2.05 us
    pallas_call x1, Pallas kernels, body(): pl.pallas_call(functools.partial(filter_kernel, (tiles, outs, first_bin,...  2 us
  transfers between devices with their start and end apart: 7, of which 4 were waited for; matrix products, arithmetic and copies ran while one was open for 0% of the time, Pallas kernels for 22%

profile of v4, /device:TPU:0, one launch (start us, length us, event | category | flops | bytes accessed | tf_op | source)
XLA Modules:
  0.0 24.3 jit_solution(6342656476940663375)
XLA Ops:
  0.7 2.0 %filter.1 = (bf16[80,128]{1,0:T(8,128)(2,1)S(1)}, bf16[80,128]{1,0:T(8,128)(2,1)S(1)}, f32[8,128]{1,0:T(8,128)S(1)}, s32[8,128]{1,0:T(8,128)S(1)}) custom-call(f32[1]{0:T(128)S(6)} %copy.6.width, s32[2,32]{1,0:T(2,128)} %bitcast.19, f32[16,8,128]{2,1,0:T(8,128)} %constant.4.clone.trig_table, s32[16,8,128]{2,1,0:T(8,128)} %constant.5.clone.code_table, ...), custom_call_target="tpu_custom_call" | custom-call | tf_op jit(solution)/shard_map/filter/pallas_call | solution.py:329
  2.7 4.1 %collective-permute-start.1 = (bf16[80,128]{1,0:T(8,128)(2,1)S(1)}, bf16[80,128]{1,0:T(8,128)(2,1)S(1)}, u32[]{:S(2)}, u32[]{:S(2)}) collective-permute-start(bf16[80,128]{1,0:T(8,128)(2,1)S(1)} %get-tuple-element.22), channel_id=1, source_target_pairs={{0,8},{1,9},{2,10},{3,11},{4,12},{5,13},{6,14},{7,15},{8,0},{9,1},... | collective-permute-start | bytes 61448 | tf_op jit(solution)/shard_map/ppermute | solution.py:389
  6.8 1.3 %collective-permute-start.2 = (bf16[80,128]{1,0:T(8,128)(2,1)S(1)}, bf16[80,128]{1,0:T(8,128)(2,1)S(1)}, u32[]{:S(2)}, u32[]{:S(2)}) collective-permute-start(bf16[80,128]{1,0:T(8,128)(2,1)S(1)} %get-tuple-element.23), channel_id=1, source_target_pairs={{0,9},{1,8},{2,11},{3,10},{4,13},{5,12},{6,15},{7,14},{8,1},{9,0},... | collective-permute-start | bytes 61448 | tf_op jit(solution)/shard_map/ppermute | solution.py:389
  8.1 0.2 %collective-permute-start = (bf16[80,128]{1,0:T(8,128)(2,1)S(1)}, bf16[80,128]{1,0:T(8,128)(2,1)S(1)}, u32[]{:S(2)}, u32[]{:S(2)}) collective-permute-start(bf16[80,128]{1,0:T(8,128)(2,1)S(1)} %get-tuple-element.23), channel_id=1, source_target_pairs={{0,1},{1,0},{2,3},{3,2},{4,5},{5,4},{6,7},{7,6},{8,9},{9,8},{10,11... | collective-permute-start | bytes 61448 | tf_op jit(solution)/shard_map/ppermute | solution.py:389
  8.3 1.8 %hats.2 = bf16[8,1024,256]{2,1,0:T(8,128)(2,1)S(1)} custom-call(f32[8,128]{1,0:T(8,128)S(1)} %get-tuple-element.30.trig, s32[8,128]{1,0:T(8,128)S(1)} %get-tuple-element.31.codes), custom_call_target="tpu_custom_call" | custom-call | flops 33554432 | tf_op jit(solution)/shard_map/hats/pallas_call | solution.py:361
  10.1 0.0 collective-permute-done.1
  10.1 2.2 %collective-permute-done.2 = bf16[80,128]{1,0:T(8,128)(2,1)S(1)} collective-permute-done((bf16[80,128]{1,0:T(8,128)(2,1)S(1)}, bf16[80,128]{1,0:T(8,128)(2,1)S(1)}, u32[]{:S(2)}, u32[]{:S(2)}) %collective-permute-start.2) | collective-permute-done | bytes 20512 | tf_op jit(solution)/shard_map/ppermute | solution.py:389
  12.3 0.0 collective-permute-done
  12.4 2.6 %collective-permute-start.5 = (bf16[2,144,128]{2,1,0:T(8,128)(2,1)S(1)}, bf16[2,144,128]{2,1,0:T(8,128)(2,1)S(1)}, u32[]{:S(2)}, u32[]{:S(2)}) collective-permute-start(bf16[2,144,128]{2,1,0:T(8,128)(2,1)S(1)} %pad_maximum_fusion.2), channel_id=1, source_target_pairs={{0,6},{2,4},{4,2},{6,0},{8,14},{10,12},{12,10},{14,8},{1,7},{3,5},... | collective-permute-start | bytes 221192 | tf_op jit(solution)/shard_map/ppermute | solution.py:263
  15.0 0.5 %collective-permute-start.4 = (bf16[2,144,128]{2,1,0:T(8,128)(2,1)S(1)}, bf16[2,144,128]{2,1,0:T(8,128)(2,1)S(1)}, u32[]{:S(2)}, u32[]{:S(2)}) collective-permute-start(bf16[2,144,128]{2,1,0:T(8,128)(2,1)S(1)} %pad_maximum_fusion.2), channel_id=1, source_target_pairs={{0,2},{2,0},{4,6},{6,4},{8,10},{10,8},{12,14},{14,12},{1,3},{3,1},... | collective-permute-start | bytes 221192 | tf_op jit(solution)/shard_map/ppermute | solution.py:263
  15.5 0.5 %collective-permute-start.3 = (bf16[2,144,128]{2,1,0:T(8,128)(2,1)S(1)}, bf16[2,144,128]{2,1,0:T(8,128)(2,1)S(1)}, u32[]{:S(2)}, u32[]{:S(2)}) collective-permute-start(bf16[2,144,128]{2,1,0:T(8,128)(2,1)S(1)} %pad_maximum_fusion.2), channel_id=1, source_target_pairs={{0,4},{2,6},{4,0},{6,2},{8,12},{10,14},{12,8},{14,10},{1,5},{3,7},... | collective-permute-start | bytes 221192 | tf_op jit(solution)/shard_map/ppermute | solution.py:263
  16.0 1.8 %hats.3 = bf16[8,1024,256]{2,1,0:T(8,128)(2,1)S(1)} custom-call(f32[8,128]{1,0:T(8,128)S(1)} %get-tuple-element.30.trig, s32[8,128]{1,0:T(8,128)S(1)} %get-tuple-element.31.codes), custom_call_target="tpu_custom_call" | custom-call | flops 33554432 | tf_op jit(solution)/shard_map/hats/pallas_call | solution.py:361
  17.8 0.6 %collective-permute-done.5 = bf16[2,144,128]{2,1,0:T(8,128)(2,1)S(1)} collective-permute-done((bf16[2,144,128]{2,1,0:T(8,128)(2,1)S(1)}, bf16[2,144,128]{2,1,0:T(8,128)(2,1)S(1)}, u32[]{:S(2)}, u32[]{:S(2)}) %collective-permute-start.5) | collective-permute-done | bytes 73760 | tf_op jit(solution)/shard_map/ppermute | solution.py:263
  18.4 0.9 %collective-permute-done.4 = bf16[2,144,128]{2,1,0:T(8,128)(2,1)S(1)} collective-permute-done((bf16[2,144,128]{2,1,0:T(8,128)(2,1)S(1)}, bf16[2,144,128]{2,1,0:T(8,128)(2,1)S(1)}, u32[]{:S(2)}, u32[]{:S(2)}) %collective-permute-start.4) | collective-permute-done | bytes 73760 | tf_op jit(solution)/shard_map/ppermute | solution.py:263
  19.3 0.5 %collective-permute-done.3 = bf16[2,144,128]{2,1,0:T(8,128)(2,1)S(1)} collective-permute-done((bf16[2,144,128]{2,1,0:T(8,128)(2,1)S(1)}, bf16[2,144,128]{2,1,0:T(8,128)(2,1)S(1)}, u32[]{:S(2)}, u32[]{:S(2)}) %collective-permute-start.3) | collective-permute-done | bytes 73760 | tf_op jit(solution)/shard_map/ppermute | solution.py:263
  19.9 0.1 collective-permute-start.6
  20.0 1.8 %project.2.refs_0_ = f32[8,32,256]{2,1,0:T(8,128)S(1)} custom-call(s32[8,128]{1,0:T(8,128)S(1)} %get-tuple-element.31.codes, bf16[8,144,128]{2,1,0:T(8,128)(2,1)S(1)} %pad_maximum_fusion.windows, bf16[8,1024,256]{2,1,0:T(8,128)(2,1)S(1)} %hats.2), custom_call_target="tpu_custom_call" | custom-call | flops 2147483648 | tf_op jit(solution)/shard_map/project/pallas_call | solution.py:411
  21.7 0.0 collective-permute-done.6.windows
  21.7 2.5 %project.3 = f32[1,32,2048]{2,1,0:T(8,128)} custom-call(s32[8,128]{1,0:T(8,128)S(1)} %get-tuple-element.31.codes, bf16[8,144,128]{2,1,0:T(8,128)(2,1)S(1)} %collective-permute-done.6.windows, bf16[8,1024,256]{2,1,0:T(8,128)(2,1)S(1)} %hats.3, f32[8,32,256]{2,1,0:T(8,128)S(1)} %project.2.refs_0_), custom_call_target="tpu_custom_call" | custom-call | flops 2147483648 | tf_op jit(solution)/shard_map/project/pallas_call | solution.py:411
  (5 shorter events, 0.1 us)
Async XLA Ops:
  2.7 7.4 %collective-permute-start.1 = (bf16[80,128]{1,0:T(8,128)(2,1)S(1)}, bf16[80,128]{1,0:T(8,128)(2,1)S(1)}, u32[]{:S(2)}, u32[]{:S(2)}) collective-permute-start(bf16[80,128]{1,0:T(8,128)(2,1)S(1)} %get-tuple-element.22), channel_id=1, source_target_pairs={{0,8},{1,9},{2,10},{3,11},{4,12},{5,13},{6,14},{7,15},{8,0},{9,1},... | collective-permute-start | bytes 61448 | tf_op jit(solution)/shard_map/ppermute | solution.py:389
  6.8 5.6 %collective-permute-start.2 = (bf16[80,128]{1,0:T(8,128)(2,1)S(1)}, bf16[80,128]{1,0:T(8,128)(2,1)S(1)}, u32[]{:S(2)}, u32[]{:S(2)}) collective-permute-start(bf16[80,128]{1,0:T(8,128)(2,1)S(1)} %get-tuple-element.23), channel_id=1, source_target_pairs={{0,9},{1,8},{2,11},{3,10},{4,13},{5,12},{6,15},{7,14},{8,1},{9,0},... | collective-permute-start | bytes 61448 | tf_op jit(solution)/shard_map/ppermute | solution.py:389
  8.1 4.3 %collective-permute-start = (bf16[80,128]{1,0:T(8,128)(2,1)S(1)}, bf16[80,128]{1,0:T(8,128)(2,1)S(1)}, u32[]{:S(2)}, u32[]{:S(2)}) collective-permute-start(bf16[80,128]{1,0:T(8,128)(2,1)S(1)} %get-tuple-element.23), channel_id=1, source_target_pairs={{0,1},{1,0},{2,3},{3,2},{4,5},{5,4},{6,7},{7,6},{8,9},{9,8},{10,11... | collective-permute-start | bytes 61448 | tf_op jit(solution)/shard_map/ppermute | solution.py:389
  12.4 6.0 %collective-permute-start.5 = (bf16[2,144,128]{2,1,0:T(8,128)(2,1)S(1)}, bf16[2,144,128]{2,1,0:T(8,128)(2,1)S(1)}, u32[]{:S(2)}, u32[]{:S(2)}) collective-permute-start(bf16[2,144,128]{2,1,0:T(8,128)(2,1)S(1)} %pad_maximum_fusion.2), channel_id=1, source_target_pairs={{0,6},{2,4},{4,2},{6,0},{8,14},{10,12},{12,10},{14,8},{1,7},{3,5},... | collective-permute-start | bytes 221192 | tf_op jit(solution)/shard_map/ppermute | solution.py:263
  15.0 4.4 %collective-permute-start.4 = (bf16[2,144,128]{2,1,0:T(8,128)(2,1)S(1)}, bf16[2,144,128]{2,1,0:T(8,128)(2,1)S(1)}, u32[]{:S(2)}, u32[]{:S(2)}) collective-permute-start(bf16[2,144,128]{2,1,0:T(8,128)(2,1)S(1)} %pad_maximum_fusion.2), channel_id=1, source_target_pairs={{0,2},{2,0},{4,6},{6,4},{8,10},{10,8},{12,14},{14,12},{1,3},{3,1},... | collective-permute-start | bytes 221192 | tf_op jit(solution)/shard_map/ppermute | solution.py:263
  15.5 4.4 %collective-permute-start.3 = (bf16[2,144,128]{2,1,0:T(8,128)(2,1)S(1)}, bf16[2,144,128]{2,1,0:T(8,128)(2,1)S(1)}, u32[]{:S(2)}, u32[]{:S(2)}) collective-permute-start(bf16[2,144,128]{2,1,0:T(8,128)(2,1)S(1)} %pad_maximum_fusion.2), channel_id=1, source_target_pairs={{0,4},{2,6},{4,0},{6,2},{8,12},{10,14},{12,8},{14,10},{1,5},{3,7},... | collective-permute-start | bytes 221192 | tf_op jit(solution)/shard_map/ppermute | solution.py:263
  19.9 1.8 %collective-permute-start.6 = (bf16[8,144,128]{2,1,0:T(8,128)(2,1)S(1)}, bf16[8,144,128]{2,1,0:T(8,128)(2,1)S(1)}, u32[]{:S(2)}, u32[]{:S(2)}) collective-permute-start(bf16[8,144,128]{2,1,0:T(8,128)(2,1)S(1)} %pad_maximum_fusion.windows), channel_id=1, source_target_pairs={{0,16},{16,0},{1,17},{17,1},{2,18},{18,2},{3,19},{19,3},{4,20},{20... | collective-permute-start | bytes 884744 | tf_op jit(solution)/shard_map/ppermute | solution.py:259

commit v5 on v4

--- a/solution.py
+++ b/solution.py
@@ -183,24 +183,26 @@
     lax.fori_loop(0, count, step, 0, unroll=2)
 
 
-def project_kernel(plan, codes, windows, hats, *refs):
-    part, local, last, tiles, height, packing = plan
+def project_kernel(plan, codes, *refs):
+    parts, sources, arrays, segments, local, last, tiles, height, packing = plan
     full, rows_of_block, groups = packing
-    before, (out, held) = refs[:-2], refs[-2:]
-    chunks, depth, pixels = hats.shape
-    sources = windows.shape[0]
+    windows, refs = refs[:arrays], refs[arrays:]
+    windows = [(window, source) for window in windows for source in range(window.shape[0])]
+    hats, before, (out, held) = refs[:segments], refs[segments:-2], refs[-2:]
+    chunks, depth, pixels = hats[0].shape
     tail_first = tiles * full * rows_of_block
     slices = height // local
-    count = depth // SLOT
+    count = sources * local
+    angle_count = depth // SLOT
     spread = lax.broadcasted_iota(jnp.int32, (height, LANES), 1)
-    for source in range(sources):
+    for at, (window, source) in enumerate(windows):
         if groups > 1:
-            tails = windows[source, tail_first:, :].astype(jnp.float32)
+            tails = window[source, tail_first:, :].astype(jnp.float32)
         for turn in range(tiles):
             pieces = []
             for j in range(full):
                 rows = pl.ds((turn * full + j) * rows_of_block, rows_of_block)
-                pieces.append(windows[source, rows, :].astype(held.dtype)[:height])
+                pieces.append(window[source, rows, :].astype(held.dtype)[:height])
             if groups > 1:
                 tail = height // groups
                 tail = tails[turn * tail : (turn + 1) * tail]
@@ -212,27 +214,31 @@
                 else:
                     value = jnp.where(spread < SLOT, halves[j // 2], halves[j // 2 + 1])
                 for angle in range(local):
-                    held[source * local + angle, j, turn * slices : (turn + 1) * slices, :] = (
-                        value[angle * slices : (angle + 1) * slices]
-                    )
+                    held[at * local + angle, j, turn * slices : (turn + 1) * slices, :] = value[
+                        angle * slices : (angle + 1) * slices
+                    ]
     lane = lax.broadcasted_iota(jnp.int32, (slices * tiles, LANES), 1)
     sums = []
     for chunk in range(chunks):
-        cut = []
-        for first in range(0, count, PER):
-            merged = None
-            for spot in range(PER):
-                index = first + spot
-                code = read(codes, (part * count + index) * chunks + chunk)
-                turn_by = (spot * SLOT + LANES - (code & (LANES - 1))) & (LANES - 1)
-                value = pltpu.roll(held[index, code >> LANE_BITS], turn_by, 1)
-                merged = value if spot == 0 else jnp.where(lane < spot * SLOT, merged, value)
-            cut.append(merged.astype(jnp.bfloat16))
-        value = jnp.dot(
-            jnp.concatenate(cut, axis=1), hats[chunk], preferred_element_type=jnp.float32
-        )
-        if before:
-            value = value + before[0][chunk]
+        value = before[0][chunk] if before else None
+        for at, (by, part) in enumerate(parts):
+            cut = []
+            for first in range(0, count, PER):
+                merged = None
+                for spot in range(PER):
+                    index = first + spot
+                    code = read(codes, (by * angle_count + part * count + index) * chunks + chunk)
+                    turn_by = (spot * SLOT + LANES - (code & (LANES - 1))) & (LANES - 1)
+                    piece = pltpu.roll(held[at * count + index, code >> LANE_BITS], turn_by, 1)
+                    merged = piece if spot == 0 else jnp.where(lane < spot * SLOT, merged, piece)
+                cut.append(merged.astype(jnp.bfloat16))
+            rows = pl.ds(part * count * SLOT, count * SLOT)
+            more = jnp.dot(
+                jnp.concatenate(cut, axis=1),
+                hats[by][chunk, rows, :],
+                preferred_element_type=jnp.float32,
+            )
+            value = more if value is None else value + more
         sums.append(value)
         if not last:
             out[chunk] = value
@@ -398,28 +404,36 @@
         pieces = jnp.concatenate([main, tails], axis=1)
     else:
         pieces = pieces.reshape(2, tiles * whole, LANES)
-    for index, masks in enumerate(exchanges[1:]):
-        moved = [swapped(pieces, "angle", mask) for mask in masks]
-        last = index == len(exchanges) - 2
-        moved = beside(moved, (pieces,), segments if last else 1)
+    for masks in exchanges[1:-1]:
+        moved = beside([swapped(pieces, "angle", mask) for mask in masks], (pieces,), 1)
         pieces = jnp.concatenate([pieces, *moved])
     held_type = jnp.bfloat16 if slices % 16 == 0 else jnp.float32
-    parts = [pieces] + [shifted(pieces, "segment", by) for by in range(1, segments)]
-    sums = ()
-    for by, windows in enumerate(parts):
-        last = by == segments - 1
-        value = pl.pallas_call(
-            functools.partial(project_kernel, (by, local, last, tiles, height, packing)),
+    sources = pieces.shape[0]
+
+    def project(parts, windows, sums, last=False):
+        return pl.pallas_call(
+            functools.partial(
+                project_kernel,
+                (parts, sources, len(windows), segments, local, last, tiles, height, packing),
+            ),
             out_shape=jax.ShapeDtypeStruct(
                 (1, slices * tiles, ROWS_DEV * TCOLS)
                 if last
                 else (chunks, slices * tiles, pixels),
                 jnp.float32,
             ),
-            in_specs=[smem] + [vmem] * (2 + len(sums)),
+            in_specs=[smem] + [vmem] * (len(windows) + segments + len(sums)),
             out_specs=vmem,
             scratch_shapes=[
-                pltpu.VMEM((spots * local, PER * (outs - 1) + 1, slices * tiles, LANES), held_type),
+                pltpu.VMEM(
+                    (
+                        len(parts) * sources * local,
+                        PER * (outs - 1) + 1,
+                        slices * tiles,
+                        LANES,
+                    ),
+                    held_type,
+                ),
             ],
             compiler_params=params,
             cost_estimate=pl.CostEstimate(
@@ -428,9 +442,32 @@
                 transcendentals=0,
             ),
             name="project",
-        )(codes, windows, hats[by], *sums)
-        sums = (value,)
-    return sums[0]
+        )(codes, *windows, *hats, *sums)
+
+    others = range(1, segments)
+    early = [pieces] + [shifted(pieces, "segment", by) for by in others]
+    moved = [swapped(pieces, "angle", mask) for mask in exchanges[-1]]
+    hats += [hats_of(part, (pieces,)) for part in range(len(hats), segments)]
+    count = len(moved)
+    if count > 1:
+        early, moved[-1] = lax.optimization_barrier((early, moved[-1]))
+    sums = project([(by, 0) for by in range(segments)], early, ())
+    if count > 1:
+        moved[:-1], sums = lax.optimization_barrier((moved[:-1], sums))
+    else:
+        moved, sums = lax.optimization_barrier((moved, sums))
+    ahead = [shifted(moved[-1], "segment", by) for by in others]
+    final = [(by, part) for by in others for part in range(1, count)]
+    if final:
+        rest = jnp.concatenate(moved[:-1])
+        late = [shifted(rest, "segment", by) for by in others]
+    own = [(0, part + 1) for part in range(count)]
+    first = [(by, count) for by in others]
+    if final:
+        sums = project(own + first, [*moved, *ahead], (sums,))
+        return project(final, late, (sums,), True)
+    sums = project(own, moved, (sums,))
+    return project(first, ahead, (sums,), True)
 
 
 def solution(mesh):

time: 24.5 us -> 24.1 us (0.984)
  waiting for transfers between devices: 4.3 us -> 2.96 us
  Pallas kernels: 9.92 us -> 10.8 us
    ppermute x3, waiting for transfers between devices: 2.05 us -> 0.7 us  [swapped(): lax.ppermute(value, axis, [(i, i ^ by) for i in range(lax.axis_size(axis))])]
    pallas_call x2 -> x3, Pallas kernels: 4.3 us -> 5.16 us  [project(): pl.pallas_call(functools.partial(project_kernel, (parts, sources, len(win...]
  transfers between devices with their start and end apart: 7 -> 9, of which waited for: 4 -> 3; matrix products, arithmetic and copies ran while one was open for 0% -> 0% of each run, Pallas kernels for 22% -> 28%
where the time goes in v5:
time: 24.1 us; the launch traced here: 23.9 us
  Pallas kernels  10.8 us (45%)
  starting transfers between devices  9.34 us (39%)
  waiting for transfers between devices  2.96 us (12%)
  between operations  0.77 us (3%)
    ppermute x3, starting transfers between devices, joint(): return lax.ppermute(cut[turn], ('angle', 'tile'), pairs)  5.64 us
    pallas_call x3, Pallas kernels, project(): pl.pallas_call(functools.partial(project_kernel, (parts, sources, len(win...  5.16 us
    pallas_call x2, Pallas kernels, hats_of(): pl.pallas_call(functools.partial(hat_kernel, (part, half, tile_rows, angl...  3.62 us
    ppermute x3, starting transfers between devices, swapped(): lax.ppermute(value, axis, [(i, i ^ by) for i in range(lax.axis_size(axis))])  3.55 us
    ppermute x3, waiting for transfers between devices, joint(): return lax.ppermute(cut[turn], ('angle', 'tile'), pairs)  2.25 us
    pallas_call x1, Pallas kernels, body(): pl.pallas_call(functools.partial(filter_kernel, (tiles, outs, first_bin,...  2 us
    ppermute x3, waiting for transfers between devices, swapped(): lax.ppermute(value, axis, [(i, i ^ by) for i in range(lax.axis_size(axis))])  0.7 us
  transfers between devices with their start and end apart: 9, of which 3 were waited for; matrix products, arithmetic and copies ran while one was open for 0% of the time, Pallas kernels for 28%

profile of v5, /device:TPU:0, one launch (start us, length us, event | category | flops | bytes accessed | tf_op | source)
XLA Modules:
  0.0 23.9 jit_solution(5360547292813748695)
XLA Ops:
  0.7 2.0 %filter.1 = (bf16[80,128]{1,0:T(8,128)(2,1)S(1)}, bf16[80,128]{1,0:T(8,128)(2,1)S(1)}, f32[8,128]{1,0:T(8,128)S(1)}, s32[8,128]{1,0:T(8,128)S(1)}) custom-call(f32[1]{0:T(128)S(6)} %copy.6.width, s32[2,32]{1,0:T(2,128)} %bitcast.17, f32[16,8,128]{2,1,0:T(8,128)} %constant.4.clone.trig_table, s32[16,8,128]{2,1,0:T(8,128)} %constant.5.clone.code_table, ...), custom_call_target="tpu_custom_call" | custom-call | tf_op jit(solution)/shard_map/filter/pallas_call | solution.py:335
  2.7 4.1 %collective-permute-start.1 = (bf16[80,128]{1,0:T(8,128)(2,1)S(1)}, bf16[80,128]{1,0:T(8,128)(2,1)S(1)}, u32[]{:S(2)}, u32[]{:S(2)}) collective-permute-start(bf16[80,128]{1,0:T(8,128)(2,1)S(1)} %get-tuple-element.24), channel_id=1, source_target_pairs={{0,8},{1,9},{2,10},{3,11},{4,12},{5,13},{6,14},{7,15},{8,0},{9,1},... | collective-permute-start | bytes 61448 | tf_op jit(solution)/shard_map/ppermute | solution.py:395
  6.8 1.3 %collective-permute-start.2 = (bf16[80,128]{1,0:T(8,128)(2,1)S(1)}, bf16[80,128]{1,0:T(8,128)(2,1)S(1)}, u32[]{:S(2)}, u32[]{:S(2)}) collective-permute-start(bf16[80,128]{1,0:T(8,128)(2,1)S(1)} %get-tuple-element.25), channel_id=1, source_target_pairs={{0,9},{1,8},{2,11},{3,10},{4,13},{5,12},{6,15},{7,14},{8,1},{9,0},... | collective-permute-start | bytes 61448 | tf_op jit(solution)/shard_map/ppermute | solution.py:395
  8.1 0.2 %collective-permute-start = (bf16[80,128]{1,0:T(8,128)(2,1)S(1)}, bf16[80,128]{1,0:T(8,128)(2,1)S(1)}, u32[]{:S(2)}, u32[]{:S(2)}) collective-permute-start(bf16[80,128]{1,0:T(8,128)(2,1)S(1)} %get-tuple-element.25), channel_id=1, source_target_pairs={{0,1},{1,0},{2,3},{3,2},{4,5},{5,4},{6,7},{7,6},{8,9},{9,8},{10,11... | collective-permute-start | bytes 61448 | tf_op jit(solution)/shard_map/ppermute | solution.py:395
  8.3 1.8 %hats.2.refs_2_.refs_4_.refs_1_ = bf16[8,1024,256]{2,1,0:T(8,128)(2,1)S(1)} custom-call(f32[8,128]{1,0:T(8,128)S(1)} %get-tuple-element.35.trig, s32[8,128]{1,0:T(8,128)S(1)} %get-tuple-element.36.codes), custom_call_target="tpu_custom_call" | custom-call | flops 33554432 | tf_op jit(solution)/shard_map/hats/pallas_call | solution.py:367
  10.1 0.0 collective-permute-done.1
  10.1 2.2 %collective-permute-done.2 = bf16[80,128]{1,0:T(8,128)(2,1)S(1)} collective-permute-done((bf16[80,128]{1,0:T(8,128)(2,1)S(1)}, bf16[80,128]{1,0:T(8,128)(2,1)S(1)}, u32[]{:S(2)}, u32[]{:S(2)}) %collective-permute-start.2) | collective-permute-done | bytes 20512 | tf_op jit(solution)/shard_map/ppermute | solution.py:395
  12.3 0.0 collective-permute-done
  12.4 2.6 %collective-permute-start.6 = (bf16[2,144,128]{2,1,0:T(8,128)(2,1)S(1)}, bf16[2,144,128]{2,1,0:T(8,128)(2,1)S(1)}, u32[]{:S(2)}, u32[]{:S(2)}) collective-permute-start(bf16[2,144,128]{2,1,0:T(8,128)(2,1)S(1)} %pad_maximum_fusion.2.refs_0_), channel_id=1, source_target_pairs={{0,6},{2,4},{4,2},{6,0},{8,14},{10,12},{12,10},{14,8},{1,7},{3,5},... | collective-permute-start | bytes 221192 | tf_op jit(solution)/shard_map/ppermute | solution.py:269
  15.0 0.0 collective-permute-start.5
  15.0 0.5 %collective-permute-start.4 = (bf16[2,144,128]{2,1,0:T(8,128)(2,1)S(1)}, bf16[2,144,128]{2,1,0:T(8,128)(2,1)S(1)}, u32[]{:S(2)}, u32[]{:S(2)}) collective-permute-start(bf16[2,144,128]{2,1,0:T(8,128)(2,1)S(1)} %pad_maximum_fusion.2.refs_0_), channel_id=1, source_target_pairs={{0,2},{2,0},{4,6},{6,4},{8,10},{10,8},{12,14},{14,12},{1,3},{3,1},... | collective-permute-start | bytes 221192 | tf_op jit(solution)/shard_map/ppermute | solution.py:269
  15.5 0.4 %collective-permute-start.3 = (bf16[2,144,128]{2,1,0:T(8,128)(2,1)S(1)}, bf16[2,144,128]{2,1,0:T(8,128)(2,1)S(1)}, u32[]{:S(2)}, u32[]{:S(2)}) collective-permute-start(bf16[2,144,128]{2,1,0:T(8,128)(2,1)S(1)} %pad_maximum_fusion.2.refs_0_), channel_id=1, source_target_pairs={{0,4},{2,6},{4,0},{6,2},{8,12},{10,14},{12,8},{14,10},{1,5},{3,7},... | collective-permute-start | bytes 221192 | tf_op jit(solution)/shard_map/ppermute | solution.py:269
  16.0 1.8 %hats.3.refs_3_.refs_5_.refs_2_ = bf16[8,1024,256]{2,1,0:T(8,128)(2,1)S(1)} custom-call(f32[8,128]{1,0:T(8,128)S(1)} %get-tuple-element.35.trig, s32[8,128]{1,0:T(8,128)S(1)} %get-tuple-element.36.codes), custom_call_target="tpu_custom_call" | custom-call | flops 33554432 | tf_op jit(solution)/shard_map/hats/pallas_call | solution.py:367
  17.8 0.0 collective-permute-done.6.refs_2_
  17.8 0.0 collective-permute-done.5.refs_1_
  17.8 0.1 collective-permute-start.8
  17.9 1.3 %project.3.refs_6_ = f32[8,32,256]{2,1,0:T(8,128)S(1)} custom-call(s32[8,128]{1,0:T(8,128)S(1)} %get-tuple-element.36.codes, bf16[2,144,128]{2,1,0:T(8,128)(2,1)S(1)} %pad_maximum_fusion.2.refs_0_, bf16[2,144,128]{2,1,0:T(8,128)(2,1)S(1)} %collective-permute-done.5.refs_1_, bf16[8,1024,256]{2,1,0:T(8,128)(2,1)S(1)} %hats.2.refs_2_.refs_4_.refs_1_, ...), custom_call_target="tpu_custom_call" | custom-call | flops 2147483648 | tf_op jit(solution)/shard_map/project/pallas_call | solution.py:414
  19.2 0.4 %collective-permute-done.4.refs_1_ = bf16[2,144,128]{2,1,0:T(8,128)(2,1)S(1)} collective-permute-done((bf16[2,144,128]{2,1,0:T(8,128)(2,1)S(1)}, bf16[2,144,128]{2,1,0:T(8,128)(2,1)S(1)}, u32[]{:S(2)}, u32[]{:S(2)}) %collective-permute-start.4) | collective-permute-done | bytes 73760 | tf_op jit(solution)/shard_map/ppermute | solution.py:269
  19.6 0.3 %collective-permute-done.3.refs_0_ = bf16[2,144,128]{2,1,0:T(8,128)(2,1)S(1)} collective-permute-done((bf16[2,144,128]{2,1,0:T(8,128)(2,1)S(1)}, bf16[2,144,128]{2,1,0:T(8,128)(2,1)S(1)}, u32[]{:S(2)}, u32[]{:S(2)}) %collective-permute-start.3) | collective-permute-done | bytes 73760 | tf_op jit(solution)/shard_map/ppermute | solution.py:269
  19.9 0.1 collective-permute-start.7
  20.0 0.0 collective-permute-done.8.refs_3_
  20.0 1.8 %project.4.refs_3_ = f32[8,32,256]{2,1,0:T(8,128)S(1)} custom-call(s32[8,128]{1,0:T(8,128)S(1)} %get-tuple-element.36.codes, bf16[2,144,128]{2,1,0:T(8,128)(2,1)S(1)} %collective-permute-done.3.refs_0_, bf16[2,144,128]{2,1,0:T(8,128)(2,1)S(1)} %collective-permute-done.4.refs_1_, bf16[2,144,128]{2,1,0:T(8,128)(2,1)S(1)} %collective-permute-done.6.refs_2_, ...), custom_call_target="tpu_custom_call" | custom-call | flops 2147483648 | tf_op jit(solution)/shard_map/project/pallas_call | solution.py:414
  21.8 0.0 collective-permute-done.7.refs_0_
  21.8 2.1 %project.5 = f32[1,32,2048]{2,1,0:T(8,128)} custom-call(s32[8,128]{1,0:T(8,128)S(1)} %get-tuple-element.36.codes, bf16[4,144,128]{2,1,0:T(8,128)(2,1)S(1)} %collective-permute-done.7.refs_0_, bf16[8,1024,256]{2,1,0:T(8,128)(2,1)S(1)} %hats.2.refs_2_.refs_4_.refs_1_, bf16[8,1024,256]{2,1,0:T(8,128)(2,1)S(1)} %hats.3.refs_3_.refs_5_.refs_2_, ...), custom_call_target="tpu_custom_call" | custom-call | flops 2147483648 | tf_op jit(solution)/shard_map/project/pallas_call | solution.py:414
  (5 shorter events, 0.0 us)
Async XLA Ops:
  2.7 7.4 %collective-permute-start.1 = (bf16[80,128]{1,0:T(8,128)(2,1)S(1)}, bf16[80,128]{1,0:T(8,128)(2,1)S(1)}, u32[]{:S(2)}, u32[]{:S(2)}) collective-permute-start(bf16[80,128]{1,0:T(8,128)(2,1)S(1)} %get-tuple-element.24), channel_id=1, source_target_pairs={{0,8},{1,9},{2,10},{3,11},{4,12},{5,13},{6,14},{7,15},{8,0},{9,1},... | collective-permute-start | bytes 61448 | tf_op jit(solution)/shard_map/ppermute | solution.py:395
  6.8 5.6 %collective-permute-start.2 = (bf16[80,128]{1,0:T(8,128)(2,1)S(1)}, bf16[80,128]{1,0:T(8,128)(2,1)S(1)}, u32[]{:S(2)}, u32[]{:S(2)}) collective-permute-start(bf16[80,128]{1,0:T(8,128)(2,1)S(1)} %get-tuple-element.25), channel_id=1, source_target_pairs={{0,9},{1,8},{2,11},{3,10},{4,13},{5,12},{6,15},{7,14},{8,1},{9,0},... | collective-permute-start | bytes 61448 | tf_op jit(solution)/shard_map/ppermute | solution.py:395
  8.1 4.3 %collective-permute-start = (bf16[80,128]{1,0:T(8,128)(2,1)S(1)}, bf16[80,128]{1,0:T(8,128)(2,1)S(1)}, u32[]{:S(2)}, u32[]{:S(2)}) collective-permute-start(bf16[80,128]{1,0:T(8,128)(2,1)S(1)} %get-tuple-element.25), channel_id=1, source_target_pairs={{0,1},{1,0},{2,3},{3,2},{4,5},{5,4},{6,7},{7,6},{8,9},{9,8},{10,11... | collective-permute-start | bytes 61448 | tf_op jit(solution)/shard_map/ppermute | solution.py:395
  12.4 5.4 %collective-permute-start.6 = (bf16[2,144,128]{2,1,0:T(8,128)(2,1)S(1)}, bf16[2,144,128]{2,1,0:T(8,128)(2,1)S(1)}, u32[]{:S(2)}, u32[]{:S(2)}) collective-permute-start(bf16[2,144,128]{2,1,0:T(8,128)(2,1)S(1)} %pad_maximum_fusion.2.refs_0_), channel_id=1, source_target_pairs={{0,6},{2,4},{4,2},{6,0},{8,14},{10,12},{12,10},{14,8},{1,7},{3,5},... | collective-permute-start | bytes 221192 | tf_op jit(solution)/shard_map/ppermute | solution.py:269
  15.0 2.9 %collective-permute-start.5 = (bf16[2,144,128]{2,1,0:T(8,128)(2,1)S(1)}, bf16[2,144,128]{2,1,0:T(8,128)(2,1)S(1)}, u32[]{:S(2)}, u32[]{:S(2)}) collective-permute-start(bf16[2,144,128]{2,1,0:T(8,128)(2,1)S(1)} %pad_maximum_fusion.2.refs_0_), channel_id=1, source_target_pairs={{0,16},{16,0},{1,17},{17,1},{2,18},{18,2},{3,19},{19,3},{4,20},{20... | collective-permute-start | bytes 221192 | tf_op jit(solution)/shard_map/ppermute | solution.py:265
  15.0 4.7 %collective-permute-start.4 = (bf16[2,144,128]{2,1,0:T(8,128)(2,1)S(1)}, bf16[2,144,128]{2,1,0:T(8,128)(2,1)S(1)}, u32[]{:S(2)}, u32[]{:S(2)}) collective-permute-start(bf16[2,144,128]{2,1,0:T(8,128)(2,1)S(1)} %pad_maximum_fusion.2.refs_0_), channel_id=1, source_target_pairs={{0,2},{2,0},{4,6},{6,4},{8,10},{10,8},{12,14},{14,12},{1,3},{3,1},... | collective-permute-start | bytes 221192 | tf_op jit(solution)/shard_map/ppermute | solution.py:269
  15.5 4.4 %collective-permute-start.3 = (bf16[2,144,128]{2,1,0:T(8,128)(2,1)S(1)}, bf16[2,144,128]{2,1,0:T(8,128)(2,1)S(1)}, u32[]{:S(2)}, u32[]{:S(2)}) collective-permute-start(bf16[2,144,128]{2,1,0:T(8,128)(2,1)S(1)} %pad_maximum_fusion.2.refs_0_), channel_id=1, source_target_pairs={{0,4},{2,6},{4,0},{6,2},{8,12},{10,14},{12,8},{14,10},{1,5},{3,7},... | collective-permute-start | bytes 221192 | tf_op jit(solution)/shard_map/ppermute | solution.py:269
  17.8 2.2 %collective-permute-start.8 = (bf16[2,144,128]{2,1,0:T(8,128)(2,1)S(1)}, bf16[2,144,128]{2,1,0:T(8,128)(2,1)S(1)}, u32[]{:S(2)}, u32[]{:S(2)}) collective-permute-start(bf16[2,144,128]{2,1,0:T(8,128)(2,1)S(1)} %collective-permute-done.6.refs_2_), channel_id=1, source_target_pairs={{0,16},{16,0},{1,17},{17,1},{2,18},{18,2},{3,19},{19,3},{4,20},{20... | collective-permute-start | bytes 221192 | tf_op jit(solution)/shard_map/ppermute | solution.py:265
  19.9 1.9 %collective-permute-start.7 = (bf16[4,144,128]{2,1,0:T(8,128)(2,1)S(1)}, bf16[4,144,128]{2,1,0:T(8,128)(2,1)S(1)}, u32[]{:S(2)}, u32[]{:S(2)}) collective-permute-start(bf16[4,144,128]{2,1,0:T(8,128)(2,1)S(1)} %pad_maximum_fusion), channel_id=1, source_target_pairs={{0,16},{16,0},{1,17},{17,1},{2,18},{18,2},{3,19},{19,3},{4,20},{20... | collective-permute-start | bytes 442376 | tf_op jit(solution)/shard_map/ppermute | solution.py:265

commit v6 on v5

--- a/solution.py
+++ b/solution.py
@@ -338,9 +338,9 @@
             jax.ShapeDtypeStruct((full * rows_of_block + -(-tail // 16) * 16, LANES), jnp.bfloat16)
         ]
         * tiles
-        + [jax.ShapeDtypeStruct(v.shape[1:], v.dtype) for v in (trig_table, code_table)],
+        + [pltpu.SMEM(v.shape[1:], v.dtype) for v in (trig_table, code_table)],
         in_specs=[smem] + [pl.BlockSpec(memory_space=pltpu.HBM)] * 4,
-        out_specs=[vmem] * (tiles + 2),
+        out_specs=[vmem] * tiles + [smem] * 2,
         scratch_shapes=[
             pltpu.SMEM(window_block.T.shape, jnp.int32),
             pltpu.VMEM(

time: 24.1 us -> 23 us (0.954)
  Pallas kernels: 10.8 us -> 7.71 us
  waiting for transfers between devices: 2.96 us -> 5.12 us
    pallas_call x3, Pallas kernels: 5.16 us -> 3.41 us  [project(): pl.pallas_call(functools.partial(project_kernel, (parts, sources, len(win...]
    ppermute x3, waiting for transfers between devices: 0.7 us -> 2.06 us  [swapped(): lax.ppermute(value, axis, [(i, i ^ by) for i in range(lax.axis_size(axis))])]
    pallas_call x2, Pallas kernels: 3.62 us -> 2.3 us  [hats_of(): pl.pallas_call(functools.partial(hat_kernel, (part, half, tile_rows, angl...]
    ppermute x3, waiting for transfers between devices: 2.25 us -> 2.88 us  [joint(): return lax.ppermute(cut[turn], ('angle', 'tile'), pairs)]
  transfers between devices with their start and end apart: 9 -> 9, of which waited for: 3 -> 5; matrix products, arithmetic and copies ran while one was open for 0% -> 0% of each run, Pallas kernels for 28% -> 18%
where the time goes in v6:
time: 23 us; the launch traced here: 22.9 us
  starting transfers between devices  9.27 us (40%)
  Pallas kernels  7.71 us (34%)
  waiting for transfers between devices  5.12 us (22%)
  between operations  0.74 us (3%)
    ppermute x3, starting transfers between devices, joint(): return lax.ppermute(cut[turn], ('angle', 'tile'), pairs)  5.64 us
    ppermute x3, starting transfers between devices, swapped(): lax.ppermute(value, axis, [(i, i ^ by) for i in range(lax.axis_size(axis))])  3.55 us
    pallas_call x3, Pallas kernels, project(): pl.pallas_call(functools.partial(project_kernel, (parts, sources, len(win...  3.41 us
    ppermute x3, waiting for transfers between devices, joint(): return lax.ppermute(cut[turn], ('angle', 'tile'), pairs)  2.88 us
    pallas_call x2, Pallas kernels, hats_of(): pl.pallas_call(functools.partial(hat_kernel, (part, half, tile_rows, angl...  2.3 us
    ppermute x3, waiting for transfers between devices, swapped(): lax.ppermute(value, axis, [(i, i ^ by) for i in range(lax.axis_size(axis))])  2.06 us
    pallas_call x1, Pallas kernels, body(): pl.pallas_call(functools.partial(filter_kernel, (tiles, outs, first_bin,...  2.01 us
  transfers between devices with their start and end apart: 9, of which 5 were waited for; matrix products, arithmetic and copies ran while one was open for 0% of the time, Pallas kernels for 18%

profile of v6, /device:TPU:0, one launch (start us, length us, event | category | flops | bytes accessed | tf_op | source)
XLA Modules:
  0.0 22.9 jit_solution(4469196153712728174)
XLA Ops:
  0.7 2.0 %filter.1 = (bf16[80,128]{1,0:T(8,128)(2,1)S(1)}, bf16[80,128]{1,0:T(8,128)(2,1)S(1)}, f32[8,128]{1,0:T(8,128)S(4)}, s32[8,128]{1,0:T(8,128)S(4)}) custom-call(f32[1]{0:T(128)S(6)} %copy.6.width, s32[2,32]{1,0:T(2,128)} %bitcast.17, f32[16,8,128]{2,1,0:T(8,128)} %constant.4.clone.trig_table, s32[16,8,128]{2,1,0:T(8,128)} %constant.5.clone.code_table, ...), custom_call_target="tpu_custom_call" | custom-call | tf_op jit(solution)/shard_map/filter/pallas_call | solution.py:335
  2.7 4.1 %collective-permute-start.1 = (bf16[80,128]{1,0:T(8,128)(2,1)S(1)}, bf16[80,128]{1,0:T(8,128)(2,1)S(1)}, u32[]{:S(2)}, u32[]{:S(2)}) collective-permute-start(bf16[80,128]{1,0:T(8,128)(2,1)S(1)} %get-tuple-element.24), channel_id=1, source_target_pairs={{0,8},{1,9},{2,10},{3,11},{4,12},{5,13},{6,14},{7,15},{8,0},{9,1},... | collective-permute-start | bytes 61448 | tf_op jit(solution)/shard_map/ppermute | solution.py:395
  6.8 1.3 %collective-permute-start.2 = (bf16[80,128]{1,0:T(8,128)(2,1)S(1)}, bf16[80,128]{1,0:T(8,128)(2,1)S(1)}, u32[]{:S(2)}, u32[]{:S(2)}) collective-permute-start(bf16[80,128]{1,0:T(8,128)(2,1)S(1)} %get-tuple-element.25), channel_id=1, source_target_pairs={{0,9},{1,8},{2,11},{3,10},{4,13},{5,12},{6,15},{7,14},{8,1},{9,0},... | collective-permute-start | bytes 61448 | tf_op jit(solution)/shard_map/ppermute | solution.py:395
  8.1 0.2 %collective-permute-start = (bf16[80,128]{1,0:T(8,128)(2,1)S(1)}, bf16[80,128]{1,0:T(8,128)(2,1)S(1)}, u32[]{:S(2)}, u32[]{:S(2)}) collective-permute-start(bf16[80,128]{1,0:T(8,128)(2,1)S(1)} %get-tuple-element.25), channel_id=1, source_target_pairs={{0,1},{1,0},{2,3},{3,2},{4,5},{5,4},{6,7},{7,6},{8,9},{9,8},{10,11... | collective-permute-start | bytes 61448 | tf_op jit(solution)/shard_map/ppermute | solution.py:395
  8.3 1.1 %hats.2.refs_2_.refs_4_.refs_1_ = bf16[8,1024,256]{2,1,0:T(8,128)(2,1)S(1)} custom-call(f32[8,128]{1,0:T(8,128)S(4)} %get-tuple-element.35.trig, s32[8,128]{1,0:T(8,128)S(4)} %get-tuple-element.36.codes), custom_call_target="tpu_custom_call" | custom-call | flops 33554432 | tf_op jit(solution)/shard_map/hats/pallas_call | solution.py:367
  9.5 0.0 collective-permute-done.1
  9.5 2.9 %collective-permute-done.2 = bf16[80,128]{1,0:T(8,128)(2,1)S(1)} collective-permute-done((bf16[80,128]{1,0:T(8,128)(2,1)S(1)}, bf16[80,128]{1,0:T(8,128)(2,1)S(1)}, u32[]{:S(2)}, u32[]{:S(2)}) %collective-permute-start.2) | collective-permute-done | bytes 20512 | tf_op jit(solution)/shard_map/ppermute | solution.py:395
  12.4 0.0 collective-permute-done
  12.4 2.6 %collective-permute-start.6 = (bf16[2,144,128]{2,1,0:T(8,128)(2,1)S(1)}, bf16[2,144,128]{2,1,0:T(8,128)(2,1)S(1)}, u32[]{:S(2)}, u32[]{:S(2)}) collective-permute-start(bf16[2,144,128]{2,1,0:T(8,128)(2,1)S(1)} %pad_maximum_fusion.2.refs_0_), channel_id=1, source_target_pairs={{0,6},{2,4},{4,2},{6,0},{8,14},{10,12},{12,10},{14,8},{1,7},{3,5},... | collective-permute-start | bytes 221192 | tf_op jit(solution)/shard_map/ppermute | solution.py:269
  15.0 0.0 collective-permute-start.5
  15.0 0.5 %collective-permute-start.4 = (bf16[2,144,128]{2,1,0:T(8,128)(2,1)S(1)}, bf16[2,144,128]{2,1,0:T(8,128)(2,1)S(1)}, u32[]{:S(2)}, u32[]{:S(2)}) collective-permute-start(bf16[2,144,128]{2,1,0:T(8,128)(2,1)S(1)} %pad_maximum_fusion.2.refs_0_), channel_id=1, source_target_pairs={{0,2},{2,0},{4,6},{6,4},{8,10},{10,8},{12,14},{14,12},{1,3},{3,1},... | collective-permute-start | bytes 221192 | tf_op jit(solution)/shard_map/ppermute | solution.py:269
  15.5 0.4 %collective-permute-start.3 = (bf16[2,144,128]{2,1,0:T(8,128)(2,1)S(1)}, bf16[2,144,128]{2,1,0:T(8,128)(2,1)S(1)}, u32[]{:S(2)}, u32[]{:S(2)}) collective-permute-start(bf16[2,144,128]{2,1,0:T(8,128)(2,1)S(1)} %pad_maximum_fusion.2.refs_0_), channel_id=1, source_target_pairs={{0,4},{2,6},{4,0},{6,2},{8,12},{10,14},{12,8},{14,10},{1,5},{3,7},... | collective-permute-start | bytes 221192 | tf_op jit(solution)/shard_map/ppermute | solution.py:269
  16.0 1.2 %hats.3.refs_3_.refs_5_.refs_2_ = bf16[8,1024,256]{2,1,0:T(8,128)(2,1)S(1)} custom-call(f32[8,128]{1,0:T(8,128)S(4)} %get-tuple-element.35.trig, s32[8,128]{1,0:T(8,128)S(4)} %get-tuple-element.36.codes), custom_call_target="tpu_custom_call" | custom-call | flops 33554432 | tf_op jit(solution)/shard_map/hats/pallas_call | solution.py:367
  17.1 0.6 %collective-permute-done.6.refs_2_ = bf16[2,144,128]{2,1,0:T(8,128)(2,1)S(1)} collective-permute-done((bf16[2,144,128]{2,1,0:T(8,128)(2,1)S(1)}, bf16[2,144,128]{2,1,0:T(8,128)(2,1)S(1)}, u32[]{:S(2)}, u32[]{:S(2)}) %collective-permute-start.6) | collective-permute-done | bytes 73760 | tf_op jit(solution)/shard_map/ppermute | solution.py:269
  17.7 0.0 collective-permute-done.5.refs_1_
  17.7 0.0 collective-permute-start.8
  17.7 0.7 %project.3.refs_6_ = f32[8,32,256]{2,1,0:T(8,128)S(1)} custom-call(s32[8,128]{1,0:T(8,128)S(4)} %get-tuple-element.36.codes, bf16[2,144,128]{2,1,0:T(8,128)(2,1)S(1)} %pad_maximum_fusion.2.refs_0_, bf16[2,144,128]{2,1,0:T(8,128)(2,1)S(1)} %collective-permute-done.5.refs_1_, bf16[8,1024,256]{2,1,0:T(8,128)(2,1)S(1)} %hats.2.refs_2_.refs_4_.refs_1_, ...), custom_call_target="tpu_custom_call" | custom-call | flops 2147483648 | tf_op jit(solution)/shard_map/project/pallas_call | solution.py:414
  18.5 1.2 %collective-permute-done.4.refs_1_ = bf16[2,144,128]{2,1,0:T(8,128)(2,1)S(1)} collective-permute-done((bf16[2,144,128]{2,1,0:T(8,128)(2,1)S(1)}, bf16[2,144,128]{2,1,0:T(8,128)(2,1)S(1)}, u32[]{:S(2)}, u32[]{:S(2)}) %collective-permute-start.4) | collective-permute-done | bytes 73760 | tf_op jit(solution)/shard_map/ppermute | solution.py:269
  19.7 0.3 %collective-permute-done.3.refs_0_ = bf16[2,144,128]{2,1,0:T(8,128)(2,1)S(1)} collective-permute-done((bf16[2,144,128]{2,1,0:T(8,128)(2,1)S(1)}, bf16[2,144,128]{2,1,0:T(8,128)(2,1)S(1)}, u32[]{:S(2)}, u32[]{:S(2)}) %collective-permute-start.3) | collective-permute-done | bytes 73760 | tf_op jit(solution)/shard_map/ppermute | solution.py:269
  19.9 0.1 collective-permute-start.7
  20.0 0.0 collective-permute-done.8.refs_3_
  20.0 1.2 %project.4.refs_3_ = f32[8,32,256]{2,1,0:T(8,128)S(1)} custom-call(s32[8,128]{1,0:T(8,128)S(4)} %get-tuple-element.36.codes, bf16[2,144,128]{2,1,0:T(8,128)(2,1)S(1)} %collective-permute-done.3.refs_0_, bf16[2,144,128]{2,1,0:T(8,128)(2,1)S(1)} %collective-permute-done.4.refs_1_, bf16[2,144,128]{2,1,0:T(8,128)(2,1)S(1)} %collective-permute-done.6.refs_2_, ...), custom_call_target="tpu_custom_call" | custom-call | flops 2147483648 | tf_op jit(solution)/shard_map/project/pallas_call | solution.py:414
  21.2 0.2 collective-permute-done.7.refs_0_
  21.4 1.5 %project.5 = f32[1,32,2048]{2,1,0:T(8,128)} custom-call(s32[8,128]{1,0:T(8,128)S(4)} %get-tuple-element.36.codes, bf16[4,144,128]{2,1,0:T(8,128)(2,1)S(1)} %collective-permute-done.7.refs_0_, bf16[8,1024,256]{2,1,0:T(8,128)(2,1)S(1)} %hats.2.refs_2_.refs_4_.refs_1_, bf16[8,1024,256]{2,1,0:T(8,128)(2,1)S(1)} %hats.3.refs_3_.refs_5_.refs_2_, ...), custom_call_target="tpu_custom_call" | custom-call | flops 2147483648 | tf_op jit(solution)/shard_map/project/pallas_call | solution.py:414
  (5 shorter events, 0.0 us)
Async XLA Ops:
  2.7 6.8 %collective-permute-start.1 = (bf16[80,128]{1,0:T(8,128)(2,1)S(1)}, bf16[80,128]{1,0:T(8,128)(2,1)S(1)}, u32[]{:S(2)}, u32[]{:S(2)}) collective-permute-start(bf16[80,128]{1,0:T(8,128)(2,1)S(1)} %get-tuple-element.24), channel_id=1, source_target_pairs={{0,8},{1,9},{2,10},{3,11},{4,12},{5,13},{6,14},{7,15},{8,0},{9,1},... | collective-permute-start | bytes 61448 | tf_op jit(solution)/shard_map/ppermute | solution.py:395
  6.8 5.6 %collective-permute-start.2 = (bf16[80,128]{1,0:T(8,128)(2,1)S(1)}, bf16[80,128]{1,0:T(8,128)(2,1)S(1)}, u32[]{:S(2)}, u32[]{:S(2)}) collective-permute-start(bf16[80,128]{1,0:T(8,128)(2,1)S(1)} %get-tuple-element.25), channel_id=1, source_target_pairs={{0,9},{1,8},{2,11},{3,10},{4,13},{5,12},{6,15},{7,14},{8,1},{9,0},... | collective-permute-start | bytes 61448 | tf_op jit(solution)/shard_map/ppermute | solution.py:395
  8.1 4.3 %collective-permute-start = (bf16[80,128]{1,0:T(8,128)(2,1)S(1)}, bf16[80,128]{1,0:T(8,128)(2,1)S(1)}, u32[]{:S(2)}, u32[]{:S(2)}) collective-permute-start(bf16[80,128]{1,0:T(8,128)(2,1)S(1)} %get-tuple-element.25), channel_id=1, source_target_pairs={{0,1},{1,0},{2,3},{3,2},{4,5},{5,4},{6,7},{7,6},{8,9},{9,8},{10,11... | collective-permute-start | bytes 61448 | tf_op jit(solution)/shard_map/ppermute | solution.py:395
  12.4 5.3 %collective-permute-start.6 = (bf16[2,144,128]{2,1,0:T(8,128)(2,1)S(1)}, bf16[2,144,128]{2,1,0:T(8,128)(2,1)S(1)}, u32[]{:S(2)}, u32[]{:S(2)}) collective-permute-start(bf16[2,144,128]{2,1,0:T(8,128)(2,1)S(1)} %pad_maximum_fusion.2.refs_0_), channel_id=1, source_target_pairs={{0,6},{2,4},{4,2},{6,0},{8,14},{10,12},{12,10},{14,8},{1,7},{3,5},... | collective-permute-start | bytes 221192 | tf_op jit(solution)/shard_map/ppermute | solution.py:269
  15.0 2.7 %collective-permute-start.5 = (bf16[2,144,128]{2,1,0:T(8,128)(2,1)S(1)}, bf16[2,144,128]{2,1,0:T(8,128)(2,1)S(1)}, u32[]{:S(2)}, u32[]{:S(2)}) collective-permute-start(bf16[2,144,128]{2,1,0:T(8,128)(2,1)S(1)} %pad_maximum_fusion.2.refs_0_), channel_id=1, source_target_pairs={{0,16},{16,0},{1,17},{17,1},{2,18},{18,2},{3,19},{19,3},{4,20},{20... | collective-permute-start | bytes 221192 | tf_op jit(solution)/shard_map/ppermute | solution.py:265
  15.0 4.7 %collective-permute-start.4 = (bf16[2,144,128]{2,1,0:T(8,128)(2,1)S(1)}, bf16[2,144,128]{2,1,0:T(8,128)(2,1)S(1)}, u32[]{:S(2)}, u32[]{:S(2)}) collective-permute-start(bf16[2,144,128]{2,1,0:T(8,128)(2,1)S(1)} %pad_maximum_fusion.2.refs_0_), channel_id=1, source_target_pairs={{0,2},{2,0},{4,6},{6,4},{8,10},{10,8},{12,14},{14,12},{1,3},{3,1},... | collective-permute-start | bytes 221192 | tf_op jit(solution)/shard_map/ppermute | solution.py:269
  15.5 4.4 %collective-permute-start.3 = (bf16[2,144,128]{2,1,0:T(8,128)(2,1)S(1)}, bf16[2,144,128]{2,1,0:T(8,128)(2,1)S(1)}, u32[]{:S(2)}, u32[]{:S(2)}) collective-permute-start(bf16[2,144,128]{2,1,0:T(8,128)(2,1)S(1)} %pad_maximum_fusion.2.refs_0_), channel_id=1, source_target_pairs={{0,4},{2,6},{4,0},{6,2},{8,12},{10,14},{12,8},{14,10},{1,5},{3,7},... | collective-permute-start | bytes 221192 | tf_op jit(solution)/shard_map/ppermute | solution.py:269
  17.7 2.3 %collective-permute-start.8 = (bf16[2,144,128]{2,1,0:T(8,128)(2,1)S(1)}, bf16[2,144,128]{2,1,0:T(8,128)(2,1)S(1)}, u32[]{:S(2)}, u32[]{:S(2)}) collective-permute-start(bf16[2,144,128]{2,1,0:T(8,128)(2,1)S(1)} %collective-permute-done.6.refs_2_), channel_id=1, source_target_pairs={{0,16},{16,0},{1,17},{17,1},{2,18},{18,2},{3,19},{19,3},{4,20},{20... | collective-permute-start | bytes 221192 | tf_op jit(solution)/shard_map/ppermute | solution.py:265
  19.9 1.4 %collective-permute-start.7 = (bf16[4,144,128]{2,1,0:T(8,128)(2,1)S(1)}, bf16[4,144,128]{2,1,0:T(8,128)(2,1)S(1)}, u32[]{:S(2)}, u32[]{:S(2)}) collective-permute-start(bf16[4,144,128]{2,1,0:T(8,128)(2,1)S(1)} %pad_maximum_fusion), channel_id=1, source_target_pairs={{0,16},{16,0},{1,17},{17,1},{2,18},{18,2},{3,19},{19,3},{4,20},{20... | collective-permute-start | bytes 442376 | tf_op jit(solution)/shard_map/ppermute | solution.py:265

commit v7 on v6

--- a/solution.py
+++ b/solution.py
@@ -45,10 +45,10 @@
     )
 
 
-def filter_kernel(plan, width, blocks_ref, trig_table, code_table, rows_ref, *refs):
-    tiles, outs, first_bin, packing = plan
+def filter_kernel(plan, width, blocks_ref, trig_table, code_table, ramp_ref, rows_ref, *refs):
+    tiles, outs, packing = plan
     full, rows_of_block, groups = packing
-    outputs, (trig, codes, blocks, padded, raw, smooth, arrived) = (
+    outputs, (trig, codes, blocks, ramp, padded, raw, smooth, arrived) = (
         refs[:tiles],
         refs[tiles:],
     )
@@ -64,6 +64,7 @@
     sources = [
         *sources,
         (blocks_ref, blocks),
+        (ramp_ref, ramp),
         (trig_table.at[place], trig),
         (code_table.at[place], codes),
     ]
@@ -77,21 +78,26 @@
     padded[:, :, :ahead] = jnp.zeros((local, slices, ahead), jnp.float32)
     padded[:, :, ahead + bins :] = jnp.zeros((local, slices, behind), jnp.float32)
 
-    away = offsets(512, LANES, BAND + first_bin)
-    spread = jnp.abs(away)
-    squared = jnp.maximum(spread * spread, 1).astype(jnp.float32)
-    odd = jnp.logical_and(spread <= BAND, (spread & 1) == 1)
-    ramp = jnp.where(odd, -1.0 / (math.pi * math.pi * squared), 0.0)
-    ramp = split(jnp.where(away == 0, 0.25, ramp))
-    decay = width[0]
+    rate = 1.0 / width[0]
     steps = (lax.broadcasted_iota(jnp.int32, (1, BAND), 1) + 1).astype(jnp.float32)
-    total = 1.0 + 2.0 * jnp.sum(jnp.exp(-steps / decay), axis=1, keepdims=True)
-    away = offsets(2 * 256, 256, BAND)
-    spread = jnp.abs(away)
-    paganin = jnp.where(
-        spread <= BAND, jnp.exp(-spread.astype(jnp.float32) / decay) / total, 0.0
-    )
-    paganin = split(paganin)
+    total = 1.0 + 2.0 * jnp.sum(jnp.exp(-steps * rate), axis=1, keepdims=True)
+    share = 1.0 / total
+    near = []
+    for shift in (LANES, 0, -LANES):
+        spread = jnp.abs(offsets(LANES, LANES, shift))
+        taps = jnp.exp(-spread.astype(jnp.float32) * rate) * share
+        near.append(split(jnp.where(spread <= BAND, taps, 0.0)))
+    none = jnp.zeros((LANES, LANES), jnp.bfloat16)
+    paganin = [
+        jnp.concatenate(
+            [
+                jnp.concatenate([*(taps[part] for taps in near), none], axis=0),
+                jnp.concatenate([none, *(taps[part] for taps in near)], axis=0),
+            ],
+            axis=1,
+        )
+        for part in range(2)
+    ]
 
     for copy in copies:
         copy.wait()
@@ -119,7 +125,7 @@
             lanes = slice(j * LANES, (j + 1) * LANES)
             smooth[at, lanes] = jnp.where(inside, smooth[at, lanes], 0.0)
     lanes = range(0, outs * LANES, LANES)
-    for j, value in enumerate(banded(smooth[...], ramp, lanes)):
+    for j, value in enumerate(banded(smooth[...], (ramp[0], ramp[1]), lanes)):
         for turn in range(tiles):
             part = value[turn * height : (turn + 1) * height]
             if j == full:
@@ -332,24 +338,33 @@
     trig_table = in_rows(np.concatenate([cosine, sine], axis=1).astype(np.float32))
     code_table = in_rows(codes.astype(np.int32))
 
+    away = np.arange(4 * LANES)[:, None] - np.arange(LANES) - BAND - first_bin
+    odd = (np.abs(away) <= BAND) & (away % 2 == 1)
+    ramp = np.where(odd, -1.0 / (math.pi**2 * np.maximum(away**2, 1)), 0.0)
+    ramp = np.where(away == 0, 0.25, ramp)
+    high = ramp.astype(jnp.bfloat16)
+    low = (ramp - high.astype(np.float64)).astype(jnp.bfloat16)
+    ramp_table = jnp.asarray(np.stack([high, low]))
+
     *cut, trig, codes = pl.pallas_call(
-        functools.partial(filter_kernel, (tiles, outs, first_bin, packing)),
+        functools.partial(filter_kernel, (tiles, outs, packing)),
         out_shape=[
             jax.ShapeDtypeStruct((full * rows_of_block + -(-tail // 16) * 16, LANES), jnp.bfloat16)
         ]
         * tiles
         + [pltpu.SMEM(v.shape[1:], v.dtype) for v in (trig_table, code_table)],
-        in_specs=[smem] + [pl.BlockSpec(memory_space=pltpu.HBM)] * 4,
+        in_specs=[smem] + [pl.BlockSpec(memory_space=pltpu.HBM)] * 5,
         out_specs=[vmem] * tiles + [smem] * 2,
         scratch_shapes=[
             pltpu.SMEM(window_block.T.shape, jnp.int32),
+            pltpu.VMEM(ramp_table.shape, ramp_table.dtype),
             pltpu.VMEM(
                 (local, slices, (block_total - WIN // LANES + smooth_blocks + 2) * LANES),
                 jnp.float32,
             ),
             pltpu.VMEM((height * tiles, (smooth_blocks + 2) * LANES), jnp.float32),
             pltpu.VMEM((height * tiles, smooth_blocks * LANES), jnp.float32),
-            pltpu.SemaphoreType.DMA((local + 3,)),
+            pltpu.SemaphoreType.DMA((local + 4,)),
         ],
         compiler_params=params,
         name="filter",
@@ -357,7 +372,7 @@
         paganin_width,
         *(
             pltpu.with_memory_space_constraint(value, pltpu.HBM)
-            for value in (window_block.T, trig_table, code_table, sinogram)
+            for value in (window_block.T, trig_table, code_table, ramp_table, sinogram)
         ),
     )
 

time: 23 us -> 23.1 us (level)
  no operation moved by 1% of the time
where the time goes in v7:
time: 23.1 us; the launch traced here: 23 us
  starting transfers between devices  9.27 us (40%)
  Pallas kernels  7.79 us (34%)
  waiting for transfers between devices  5.12 us (22%)
  between operations  0.74 us (3%)
    ppermute x3, starting transfers between devices, joint(): return lax.ppermute(cut[turn], ('angle', 'tile'), pairs)  5.64 us
    ppermute x3, starting transfers between devices, swapped(): lax.ppermute(value, axis, [(i, i ^ by) for i in range(lax.axis_size(axis))])  3.55 us
    pallas_call x3, Pallas kernels, project(): pl.pallas_call(functools.partial(project_kernel, (parts, sources, len(win...  3.41 us
    ppermute x3, waiting for transfers between devices, joint(): return lax.ppermute(cut[turn], ('angle', 'tile'), pairs)  2.88 us
    pallas_call x2, Pallas kernels, hats_of(): pl.pallas_call(functools.partial(hat_kernel, (part, half, tile_rows, angl...  2.3 us
    pallas_call x1, Pallas kernels, body(): pl.pallas_call(functools.partial(filter_kernel, (tiles, outs, packing)),...  2.09 us
    ppermute x3, waiting for transfers between devices, swapped(): lax.ppermute(value, axis, [(i, i ^ by) for i in range(lax.axis_size(axis))])  2.05 us
  transfers between devices with their start and end apart: 9, of which 5 were waited for; matrix products, arithmetic and copies ran while one was open for 0% of the time, Pallas kernels for 18%

profile of v7, /device:TPU:0, one launch (start us, length us, event | category | flops | bytes accessed | tf_op | source)
XLA Modules:
  0.0 23.0 jit_solution(15210050396209840850)
XLA Ops:
  0.7 2.1 %filter.1 = (bf16[80,128]{1,0:T(8,128)(2,1)S(1)}, bf16[80,128]{1,0:T(8,128)(2,1)S(1)}, f32[8,128]{1,0:T(8,128)S(4)}, s32[8,128]{1,0:T(8,128)S(4)}) custom-call(f32[1]{0:T(128)S(6)} %copy.7.width, s32[2,32]{1,0:T(2,128)} %bitcast.17, f32[16,8,128]{2,1,0:T(8,128)} %constant.6.clone.trig_table, s32[16,8,128]{2,1,0:T(8,128)} %constant.7.clone.code_table, ...), custom_call_target="tpu_custom_call" | custom-call | tf_op jit(solution)/shard_map/filter/pallas_call | solution.py:349
  2.7 4.1 %collective-permute-start.1 = (bf16[80,128]{1,0:T(8,128)(2,1)S(1)}, bf16[80,128]{1,0:T(8,128)(2,1)S(1)}, u32[]{:S(2)}, u32[]{:S(2)}) collective-permute-start(bf16[80,128]{1,0:T(8,128)(2,1)S(1)} %get-tuple-element.24), channel_id=1, source_target_pairs={{0,8},{1,9},{2,10},{3,11},{4,12},{5,13},{6,14},{7,15},{8,0},{9,1},... | collective-permute-start | bytes 61448 | tf_op jit(solution)/shard_map/ppermute | solution.py:410
  6.9 1.3 %collective-permute-start.2 = (bf16[80,128]{1,0:T(8,128)(2,1)S(1)}, bf16[80,128]{1,0:T(8,128)(2,1)S(1)}, u32[]{:S(2)}, u32[]{:S(2)}) collective-permute-start(bf16[80,128]{1,0:T(8,128)(2,1)S(1)} %get-tuple-element.25), channel_id=1, source_target_pairs={{0,9},{1,8},{2,11},{3,10},{4,13},{5,12},{6,15},{7,14},{8,1},{9,0},... | collective-permute-start | bytes 61448 | tf_op jit(solution)/shard_map/ppermute | solution.py:410
  8.1 0.3 %collective-permute-start = (bf16[80,128]{1,0:T(8,128)(2,1)S(1)}, bf16[80,128]{1,0:T(8,128)(2,1)S(1)}, u32[]{:S(2)}, u32[]{:S(2)}) collective-permute-start(bf16[80,128]{1,0:T(8,128)(2,1)S(1)} %get-tuple-element.25), channel_id=1, source_target_pairs={{0,1},{1,0},{2,3},{3,2},{4,5},{5,4},{6,7},{7,6},{8,9},{9,8},{10,11... | collective-permute-start | bytes 61448 | tf_op jit(solution)/shard_map/ppermute | solution.py:410
  8.4 1.1 %hats.2.refs_2_.refs_4_.refs_1_ = bf16[8,1024,256]{2,1,0:T(8,128)(2,1)S(1)} custom-call(f32[8,128]{1,0:T(8,128)S(4)} %get-tuple-element.35.trig, s32[8,128]{1,0:T(8,128)S(4)} %get-tuple-element.36.codes), custom_call_target="tpu_custom_call" | custom-call | flops 33554432 | tf_op jit(solution)/shard_map/hats/pallas_call | solution.py:382
  9.5 0.0 collective-permute-done.1
  9.6 2.9 %collective-permute-done.2 = bf16[80,128]{1,0:T(8,128)(2,1)S(1)} collective-permute-done((bf16[80,128]{1,0:T(8,128)(2,1)S(1)}, bf16[80,128]{1,0:T(8,128)(2,1)S(1)}, u32[]{:S(2)}, u32[]{:S(2)}) %collective-permute-start.2) | collective-permute-done | bytes 20512 | tf_op jit(solution)/shard_map/ppermute | solution.py:410
  12.4 0.0 collective-permute-done
  12.5 2.6 %collective-permute-start.6 = (bf16[2,144,128]{2,1,0:T(8,128)(2,1)S(1)}, bf16[2,144,128]{2,1,0:T(8,128)(2,1)S(1)}, u32[]{:S(2)}, u32[]{:S(2)}) collective-permute-start(bf16[2,144,128]{2,1,0:T(8,128)(2,1)S(1)} %pad_maximum_fusion.2.refs_0_), channel_id=1, source_target_pairs={{0,6},{2,4},{4,2},{6,0},{8,14},{10,12},{12,10},{14,8},{1,7},{3,5},... | collective-permute-start | bytes 221192 | tf_op jit(solution)/shard_map/ppermute | solution.py:275
  15.1 0.0 collective-permute-start.5
  15.1 0.5 %collective-permute-start.4 = (bf16[2,144,128]{2,1,0:T(8,128)(2,1)S(1)}, bf16[2,144,128]{2,1,0:T(8,128)(2,1)S(1)}, u32[]{:S(2)}, u32[]{:S(2)}) collective-permute-start(bf16[2,144,128]{2,1,0:T(8,128)(2,1)S(1)} %pad_maximum_fusion.2.refs_0_), channel_id=1, source_target_pairs={{0,2},{2,0},{4,6},{6,4},{8,10},{10,8},{12,14},{14,12},{1,3},{3,1},... | collective-permute-start | bytes 221192 | tf_op jit(solution)/shard_map/ppermute | solution.py:275
  15.6 0.4 %collective-permute-start.3 = (bf16[2,144,128]{2,1,0:T(8,128)(2,1)S(1)}, bf16[2,144,128]{2,1,0:T(8,128)(2,1)S(1)}, u32[]{:S(2)}, u32[]{:S(2)}) collective-permute-start(bf16[2,144,128]{2,1,0:T(8,128)(2,1)S(1)} %pad_maximum_fusion.2.refs_0_), channel_id=1, source_target_pairs={{0,4},{2,6},{4,0},{6,2},{8,12},{10,14},{12,8},{14,10},{1,5},{3,7},... | collective-permute-start | bytes 221192 | tf_op jit(solution)/shard_map/ppermute | solution.py:275
  16.0 1.2 %hats.3.refs_3_.refs_5_.refs_2_ = bf16[8,1024,256]{2,1,0:T(8,128)(2,1)S(1)} custom-call(f32[8,128]{1,0:T(8,128)S(4)} %get-tuple-element.35.trig, s32[8,128]{1,0:T(8,128)S(4)} %get-tuple-element.36.codes), custom_call_target="tpu_custom_call" | custom-call | flops 33554432 | tf_op jit(solution)/shard_map/hats/pallas_call | solution.py:382
  17.2 0.6 %collective-permute-done.6.refs_2_ = bf16[2,144,128]{2,1,0:T(8,128)(2,1)S(1)} collective-permute-done((bf16[2,144,128]{2,1,0:T(8,128)(2,1)S(1)}, bf16[2,144,128]{2,1,0:T(8,128)(2,1)S(1)}, u32[]{:S(2)}, u32[]{:S(2)}) %collective-permute-start.6) | collective-permute-done | bytes 73760 | tf_op jit(solution)/shard_map/ppermute | solution.py:275
  17.8 0.0 collective-permute-done.5.refs_1_
  17.8 0.0 collective-permute-start.8
  17.8 0.7 %project.3.refs_6_ = f32[8,32,256]{2,1,0:T(8,128)S(1)} custom-call(s32[8,128]{1,0:T(8,128)S(4)} %get-tuple-element.36.codes, bf16[2,144,128]{2,1,0:T(8,128)(2,1)S(1)} %pad_maximum_fusion.2.refs_0_, bf16[2,144,128]{2,1,0:T(8,128)(2,1)S(1)} %collective-permute-done.5.refs_1_, bf16[8,1024,256]{2,1,0:T(8,128)(2,1)S(1)} %hats.2.refs_2_.refs_4_.refs_1_, ...), custom_call_target="tpu_custom_call" | custom-call | flops 2147483648 | tf_op jit(solution)/shard_map/project/pallas_call | solution.py:429
  18.5 1.2 %collective-permute-done.4.refs_1_ = bf16[2,144,128]{2,1,0:T(8,128)(2,1)S(1)} collective-permute-done((bf16[2,144,128]{2,1,0:T(8,128)(2,1)S(1)}, bf16[2,144,128]{2,1,0:T(8,128)(2,1)S(1)}, u32[]{:S(2)}, u32[]{:S(2)}) %collective-permute-start.4) | collective-permute-done | bytes 73760 | tf_op jit(solution)/shard_map/ppermute | solution.py:275
  19.7 0.3 %collective-permute-done.3.refs_0_ = bf16[2,144,128]{2,1,0:T(8,128)(2,1)S(1)} collective-permute-done((bf16[2,144,128]{2,1,0:T(8,128)(2,1)S(1)}, bf16[2,144,128]{2,1,0:T(8,128)(2,1)S(1)}, u32[]{:S(2)}, u32[]{:S(2)}) %collective-permute-start.3) | collective-permute-done | bytes 73760 | tf_op jit(solution)/shard_map/ppermute | solution.py:275
  20.0 0.1 collective-permute-start.7
  20.1 0.0 collective-permute-done.8.refs_3_
  20.1 1.2 %project.4.refs_3_ = f32[8,32,256]{2,1,0:T(8,128)S(1)} custom-call(s32[8,128]{1,0:T(8,128)S(4)} %get-tuple-element.36.codes, bf16[2,144,128]{2,1,0:T(8,128)(2,1)S(1)} %collective-permute-done.3.refs_0_, bf16[2,144,128]{2,1,0:T(8,128)(2,1)S(1)} %collective-permute-done.4.refs_1_, bf16[2,144,128]{2,1,0:T(8,128)(2,1)S(1)} %collective-permute-done.6.refs_2_, ...), custom_call_target="tpu_custom_call" | custom-call | flops 2147483648 | tf_op jit(solution)/shard_map/project/pallas_call | solution.py:429
  21.3 0.2 collective-permute-done.7.refs_0_
  21.5 1.5 %project.5 = f32[1,32,2048]{2,1,0:T(8,128)} custom-call(s32[8,128]{1,0:T(8,128)S(4)} %get-tuple-element.36.codes, bf16[4,144,128]{2,1,0:T(8,128)(2,1)S(1)} %collective-permute-done.7.refs_0_, bf16[8,1024,256]{2,1,0:T(8,128)(2,1)S(1)} %hats.2.refs_2_.refs_4_.refs_1_, bf16[8,1024,256]{2,1,0:T(8,128)(2,1)S(1)} %hats.3.refs_3_.refs_5_.refs_2_, ...), custom_call_target="tpu_custom_call" | custom-call | flops 2147483648 | tf_op jit(solution)/shard_map/project/pallas_call | solution.py:429
  (5 shorter events, 0.0 us)
Async XLA Ops:
  2.7 6.8 %collective-permute-start.1 = (bf16[80,128]{1,0:T(8,128)(2,1)S(1)}, bf16[80,128]{1,0:T(8,128)(2,1)S(1)}, u32[]{:S(2)}, u32[]{:S(2)}) collective-permute-start(bf16[80,128]{1,0:T(8,128)(2,1)S(1)} %get-tuple-element.24), channel_id=1, source_target_pairs={{0,8},{1,9},{2,10},{3,11},{4,12},{5,13},{6,14},{7,15},{8,0},{9,1},... | collective-permute-start | bytes 61448 | tf_op jit(solution)/shard_map/ppermute | solution.py:410
  6.9 5.6 %collective-permute-start.2 = (bf16[80,128]{1,0:T(8,128)(2,1)S(1)}, bf16[80,128]{1,0:T(8,128)(2,1)S(1)}, u32[]{:S(2)}, u32[]{:S(2)}) collective-permute-start(bf16[80,128]{1,0:T(8,128)(2,1)S(1)} %get-tuple-element.25), channel_id=1, source_target_pairs={{0,9},{1,8},{2,11},{3,10},{4,13},{5,12},{6,15},{7,14},{8,1},{9,0},... | collective-permute-start | bytes 61448 | tf_op jit(solution)/shard_map/ppermute | solution.py:410
  8.1 4.3 %collective-permute-start = (bf16[80,128]{1,0:T(8,128)(2,1)S(1)}, bf16[80,128]{1,0:T(8,128)(2,1)S(1)}, u32[]{:S(2)}, u32[]{:S(2)}) collective-permute-start(bf16[80,128]{1,0:T(8,128)(2,1)S(1)} %get-tuple-element.25), channel_id=1, source_target_pairs={{0,1},{1,0},{2,3},{3,2},{4,5},{5,4},{6,7},{7,6},{8,9},{9,8},{10,11... | collective-permute-start | bytes 61448 | tf_op jit(solution)/shard_map/ppermute | solution.py:410
  12.5 5.3 %collective-permute-start.6 = (bf16[2,144,128]{2,1,0:T(8,128)(2,1)S(1)}, bf16[2,144,128]{2,1,0:T(8,128)(2,1)S(1)}, u32[]{:S(2)}, u32[]{:S(2)}) collective-permute-start(bf16[2,144,128]{2,1,0:T(8,128)(2,1)S(1)} %pad_maximum_fusion.2.refs_0_), channel_id=1, source_target_pairs={{0,6},{2,4},{4,2},{6,0},{8,14},{10,12},{12,10},{14,8},{1,7},{3,5},... | collective-permute-start | bytes 221192 | tf_op jit(solution)/shard_map/ppermute | solution.py:275
  15.1 2.8 %collective-permute-start.5 = (bf16[2,144,128]{2,1,0:T(8,128)(2,1)S(1)}, bf16[2,144,128]{2,1,0:T(8,128)(2,1)S(1)}, u32[]{:S(2)}, u32[]{:S(2)}) collective-permute-start(bf16[2,144,128]{2,1,0:T(8,128)(2,1)S(1)} %pad_maximum_fusion.2.refs_0_), channel_id=1, source_target_pairs={{0,16},{16,0},{1,17},{17,1},{2,18},{18,2},{3,19},{19,3},{4,20},{20... | collective-permute-start | bytes 221192 | tf_op jit(solution)/shard_map/ppermute | solution.py:271
  15.1 4.7 %collective-permute-start.4 = (bf16[2,144,128]{2,1,0:T(8,128)(2,1)S(1)}, bf16[2,144,128]{2,1,0:T(8,128)(2,1)S(1)}, u32[]{:S(2)}, u32[]{:S(2)}) collective-permute-start(bf16[2,144,128]{2,1,0:T(8,128)(2,1)S(1)} %pad_maximum_fusion.2.refs_0_), channel_id=1, source_target_pairs={{0,2},{2,0},{4,6},{6,4},{8,10},{10,8},{12,14},{14,12},{1,3},{3,1},... | collective-permute-start | bytes 221192 | tf_op jit(solution)/shard_map/ppermute | solution.py:275
  15.6 4.4 %collective-permute-start.3 = (bf16[2,144,128]{2,1,0:T(8,128)(2,1)S(1)}, bf16[2,144,128]{2,1,0:T(8,128)(2,1)S(1)}, u32[]{:S(2)}, u32[]{:S(2)}) collective-permute-start(bf16[2,144,128]{2,1,0:T(8,128)(2,1)S(1)} %pad_maximum_fusion.2.refs_0_), channel_id=1, source_target_pairs={{0,4},{2,6},{4,0},{6,2},{8,12},{10,14},{12,8},{14,10},{1,5},{3,7},... | collective-permute-start | bytes 221192 | tf_op jit(solution)/shard_map/ppermute | solution.py:275
  17.8 2.3 %collective-permute-start.8 = (bf16[2,144,128]{2,1,0:T(8,128)(2,1)S(1)}, bf16[2,144,128]{2,1,0:T(8,128)(2,1)S(1)}, u32[]{:S(2)}, u32[]{:S(2)}) collective-permute-start(bf16[2,144,128]{2,1,0:T(8,128)(2,1)S(1)} %collective-permute-done.6.refs_2_), channel_id=1, source_target_pairs={{0,16},{16,0},{1,17},{17,1},{2,18},{18,2},{3,19},{19,3},{4,20},{20... | collective-permute-start | bytes 221192 | tf_op jit(solution)/shard_map/ppermute | solution.py:271
  20.0 1.4 %collective-permute-start.7 = (bf16[4,144,128]{2,1,0:T(8,128)(2,1)S(1)}, bf16[4,144,128]{2,1,0:T(8,128)(2,1)S(1)}, u32[]{:S(2)}, u32[]{:S(2)}) collective-permute-start(bf16[4,144,128]{2,1,0:T(8,128)(2,1)S(1)} %pad_maximum_fusion), channel_id=1, source_target_pairs={{0,16},{16,0},{1,17},{17,1},{2,18},{18,2},{3,19},{19,3},{4,20},{20... | collective-permute-start | bytes 442376 | tf_op jit(solution)/shard_map/ppermute | solution.py:271

commit v8 on v6

--- a/solution.py
+++ b/solution.py
@@ -188,7 +188,12 @@
     full, rows_of_block, groups = packing
     windows, refs = refs[:arrays], refs[arrays:]
     windows = [(window, source) for window in windows for source in range(window.shape[0])]
-    hats, before, (out, held) = refs[:segments], refs[segments:-2], refs[-2:]
+    scratch = 3 if last else 1
+    hats, before = refs[:segments], refs[segments : -1 - scratch]
+    out, held = refs[-1 - scratch], refs[-scratch]
+    if last:
+        ready, sent = refs[-2:]
+        copies = []
     chunks, depth, pixels = hats[0].shape
     tail_first = tiles * full * rows_of_block
     slices = height // local
@@ -254,10 +259,20 @@
                 for turn in range(tiles):
                     tile = lax.rem(mine + turn, tiles)
                     into = pl.ds(pl.multiple_of(tile * slices, slices), slices)
-                    out[0, into, at : at + LANES] = value[turn * slices : (turn + 1) * slices]
+                    ready[into, at : at + LANES] = value[turn * slices : (turn + 1) * slices]
             else:
-                out[0, :, at : at + LANES] = pltpu.roll(value, mine * slices, 0)
+                ready[:, at : at + LANES] = pltpu.roll(value, mine * slices, 0)
+            lanes = pl.ds(at, LANES)
+            copies.append(
+                pltpu.make_async_copy(
+                    ready.at[:, lanes], out.at[0, :, lanes], sent.at[len(copies)]
+                )
+            )
+            copies[-1].start()
         sums = []
+    if last:
+        for copy in copies:
+            copy.wait()
 
 
 def shifted(value, axis, by):
@@ -410,6 +425,11 @@
     held_type = jnp.bfloat16 if slices % 16 == 0 else jnp.float32
     sources = pieces.shape[0]
 
+    sending = [
+        pltpu.VMEM((slices * tiles, ROWS_DEV * TCOLS), jnp.float32),
+        pltpu.SemaphoreType.DMA((ROWS_DEV * TCOLS // LANES,)),
+    ]
+
     def project(parts, windows, sums, last=False):
         return pl.pallas_call(
             functools.partial(
@@ -423,7 +443,7 @@
                 jnp.float32,
             ),
             in_specs=[smem] + [vmem] * (len(windows) + segments + len(sums)),
-            out_specs=vmem,
+            out_specs=pl.BlockSpec(memory_space=pltpu.HBM) if last else vmem,
             scratch_shapes=[
                 pltpu.VMEM(
                     (
@@ -434,6 +454,7 @@
                     ),
                     held_type,
                 ),
+                *(sending if last else []),
             ],
             compiler_params=params,
             cost_estimate=pl.CostEstimate(

time: 23 us -> 23.1 us (level)
  no operation moved by 1% of the time
where the time goes in v8:
time: 23.1 us; the launch traced here: 22.9 us
  starting transfers between devices  9.27 us (40%)
  Pallas kernels  7.76 us (34%)
  waiting for transfers between devices  5.12 us (22%)
  between operations  0.74 us (3%)
    ppermute x3, starting transfers between devices, joint(): return lax.ppermute(cut[turn], ('angle', 'tile'), pairs)  5.64 us
    ppermute x3, starting transfers between devices, swapped(): lax.ppermute(value, axis, [(i, i ^ by) for i in range(lax.axis_size(axis))])  3.55 us
    pallas_call x3, Pallas kernels, project(): pl.pallas_call(functools.partial(project_kernel, (parts, sources, len(win...  3.46 us
    ppermute x3, waiting for transfers between devices, joint(): return lax.ppermute(cut[turn], ('angle', 'tile'), pairs)  2.88 us
    pallas_call x2, Pallas kernels, hats_of(): pl.pallas_call(functools.partial(hat_kernel, (part, half, tile_rows, angl...  2.3 us
    ppermute x3, waiting for transfers between devices, swapped(): lax.ppermute(value, axis, [(i, i ^ by) for i in range(lax.axis_size(axis))])  2.06 us
    pallas_call x1, Pallas kernels, body(): pl.pallas_call(functools.partial(filter_kernel, (tiles, outs, first_bin,...  2.01 us
  transfers between devices with their start and end apart: 9, of which 5 were waited for; matrix products, arithmetic and copies ran while one was open for 0% of the time, Pallas kernels for 18%

profile of v8, /device:TPU:0, one launch (start us, length us, event | category | flops | bytes accessed | tf_op | source)
XLA Modules:
  0.0 22.9 jit_solution(12094382736145183363)
XLA Ops:
  0.7 2.0 %filter.1 = (bf16[80,128]{1,0:T(8,128)(2,1)S(1)}, bf16[80,128]{1,0:T(8,128)(2,1)S(1)}, f32[8,128]{1,0:T(8,128)S(4)}, s32[8,128]{1,0:T(8,128)S(4)}) custom-call(f32[1]{0:T(128)S(6)} %copy.6.width, s32[2,32]{1,0:T(2,128)} %bitcast.17, f32[16,8,128]{2,1,0:T(8,128)} %constant.4.clone.trig_table, s32[16,8,128]{2,1,0:T(8,128)} %constant.5.clone.code_table, ...), custom_call_target="tpu_custom_call" | custom-call | tf_op jit(solution)/shard_map/filter/pallas_call | solution.py:350
  2.7 4.1 %collective-permute-start.1 = (bf16[80,128]{1,0:T(8,128)(2,1)S(1)}, bf16[80,128]{1,0:T(8,128)(2,1)S(1)}, u32[]{:S(2)}, u32[]{:S(2)}) collective-permute-start(bf16[80,128]{1,0:T(8,128)(2,1)S(1)} %get-tuple-element.24), channel_id=1, source_target_pairs={{0,8},{1,9},{2,10},{3,11},{4,12},{5,13},{6,14},{7,15},{8,0},{9,1},... | collective-permute-start | bytes 61448 | tf_op jit(solution)/shard_map/ppermute | solution.py:410
  6.8 1.3 %collective-permute-start.2 = (bf16[80,128]{1,0:T(8,128)(2,1)S(1)}, bf16[80,128]{1,0:T(8,128)(2,1)S(1)}, u32[]{:S(2)}, u32[]{:S(2)}) collective-permute-start(bf16[80,128]{1,0:T(8,128)(2,1)S(1)} %get-tuple-element.25), channel_id=1, source_target_pairs={{0,9},{1,8},{2,11},{3,10},{4,13},{5,12},{6,15},{7,14},{8,1},{9,0},... | collective-permute-start | bytes 61448 | tf_op jit(solution)/shard_map/ppermute | solution.py:410
  8.1 0.2 %collective-permute-start = (bf16[80,128]{1,0:T(8,128)(2,1)S(1)}, bf16[80,128]{1,0:T(8,128)(2,1)S(1)}, u32[]{:S(2)}, u32[]{:S(2)}) collective-permute-start(bf16[80,128]{1,0:T(8,128)(2,1)S(1)} %get-tuple-element.25), channel_id=1, source_target_pairs={{0,1},{1,0},{2,3},{3,2},{4,5},{5,4},{6,7},{7,6},{8,9},{9,8},{10,11... | collective-permute-start | bytes 61448 | tf_op jit(solution)/shard_map/ppermute | solution.py:410
  8.3 1.1 %hats.2.refs_2_.refs_4_.refs_1_ = bf16[8,1024,256]{2,1,0:T(8,128)(2,1)S(1)} custom-call(f32[8,128]{1,0:T(8,128)S(4)} %get-tuple-element.35.trig, s32[8,128]{1,0:T(8,128)S(4)} %get-tuple-element.36.codes), custom_call_target="tpu_custom_call" | custom-call | flops 33554432 | tf_op jit(solution)/shard_map/hats/pallas_call | solution.py:382
  9.5 0.0 collective-permute-done.1
  9.5 2.9 %collective-permute-done.2 = bf16[80,128]{1,0:T(8,128)(2,1)S(1)} collective-permute-done((bf16[80,128]{1,0:T(8,128)(2,1)S(1)}, bf16[80,128]{1,0:T(8,128)(2,1)S(1)}, u32[]{:S(2)}, u32[]{:S(2)}) %collective-permute-start.2) | collective-permute-done | bytes 20512 | tf_op jit(solution)/shard_map/ppermute | solution.py:410
  12.4 0.0 collective-permute-done
  12.4 2.6 %collective-permute-start.6 = (bf16[2,144,128]{2,1,0:T(8,128)(2,1)S(1)}, bf16[2,144,128]{2,1,0:T(8,128)(2,1)S(1)}, u32[]{:S(2)}, u32[]{:S(2)}) collective-permute-start(bf16[2,144,128]{2,1,0:T(8,128)(2,1)S(1)} %pad_maximum_fusion.2.refs_0_), channel_id=1, source_target_pairs={{0,6},{2,4},{4,2},{6,0},{8,14},{10,12},{12,10},{14,8},{1,7},{3,5},... | collective-permute-start | bytes 221192 | tf_op jit(solution)/shard_map/ppermute | solution.py:284
  15.0 0.0 collective-permute-start.5
  15.0 0.5 %collective-permute-start.4 = (bf16[2,144,128]{2,1,0:T(8,128)(2,1)S(1)}, bf16[2,144,128]{2,1,0:T(8,128)(2,1)S(1)}, u32[]{:S(2)}, u32[]{:S(2)}) collective-permute-start(bf16[2,144,128]{2,1,0:T(8,128)(2,1)S(1)} %pad_maximum_fusion.2.refs_0_), channel_id=1, source_target_pairs={{0,2},{2,0},{4,6},{6,4},{8,10},{10,8},{12,14},{14,12},{1,3},{3,1},... | collective-permute-start | bytes 221192 | tf_op jit(solution)/shard_map/ppermute | solution.py:284
  15.5 0.4 %collective-permute-start.3 = (bf16[2,144,128]{2,1,0:T(8,128)(2,1)S(1)}, bf16[2,144,128]{2,1,0:T(8,128)(2,1)S(1)}, u32[]{:S(2)}, u32[]{:S(2)}) collective-permute-start(bf16[2,144,128]{2,1,0:T(8,128)(2,1)S(1)} %pad_maximum_fusion.2.refs_0_), channel_id=1, source_target_pairs={{0,4},{2,6},{4,0},{6,2},{8,12},{10,14},{12,8},{14,10},{1,5},{3,7},... | collective-permute-start | bytes 221192 | tf_op jit(solution)/shard_map/ppermute | solution.py:284
  16.0 1.2 %hats.3.refs_3_.refs_5_.refs_2_ = bf16[8,1024,256]{2,1,0:T(8,128)(2,1)S(1)} custom-call(f32[8,128]{1,0:T(8,128)S(4)} %get-tuple-element.35.trig, s32[8,128]{1,0:T(8,128)S(4)} %get-tuple-element.36.codes), custom_call_target="tpu_custom_call" | custom-call | flops 33554432 | tf_op jit(solution)/shard_map/hats/pallas_call | solution.py:382
  17.1 0.6 %collective-permute-done.6.refs_2_ = bf16[2,144,128]{2,1,0:T(8,128)(2,1)S(1)} collective-permute-done((bf16[2,144,128]{2,1,0:T(8,128)(2,1)S(1)}, bf16[2,144,128]{2,1,0:T(8,128)(2,1)S(1)}, u32[]{:S(2)}, u32[]{:S(2)}) %collective-permute-start.6) | collective-permute-done | bytes 73760 | tf_op jit(solution)/shard_map/ppermute | solution.py:284
  17.7 0.0 collective-permute-done.5.refs_1_
  17.7 0.0 collective-permute-start.8
  17.7 0.7 %project.3.refs_6_ = f32[8,32,256]{2,1,0:T(8,128)S(1)} custom-call(s32[8,128]{1,0:T(8,128)S(4)} %get-tuple-element.36.codes, bf16[2,144,128]{2,1,0:T(8,128)(2,1)S(1)} %pad_maximum_fusion.2.refs_0_, bf16[2,144,128]{2,1,0:T(8,128)(2,1)S(1)} %collective-permute-done.5.refs_1_, bf16[8,1024,256]{2,1,0:T(8,128)(2,1)S(1)} %hats.2.refs_2_.refs_4_.refs_1_, ...), custom_call_target="tpu_custom_call" | custom-call | flops 2147483648 | tf_op jit(solution)/shard_map/project/pallas_call | solution.py:434
  18.5 1.2 %collective-permute-done.4.refs_1_ = bf16[2,144,128]{2,1,0:T(8,128)(2,1)S(1)} collective-permute-done((bf16[2,144,128]{2,1,0:T(8,128)(2,1)S(1)}, bf16[2,144,128]{2,1,0:T(8,128)(2,1)S(1)}, u32[]{:S(2)}, u32[]{:S(2)}) %collective-permute-start.4) | collective-permute-done | bytes 73760 | tf_op jit(solution)/shard_map/ppermute | solution.py:284
  19.7 0.3 %collective-permute-done.3.refs_0_ = bf16[2,144,128]{2,1,0:T(8,128)(2,1)S(1)} collective-permute-done((bf16[2,144,128]{2,1,0:T(8,128)(2,1)S(1)}, bf16[2,144,128]{2,1,0:T(8,128)(2,1)S(1)}, u32[]{:S(2)}, u32[]{:S(2)}) %collective-permute-start.3) | collective-permute-done | bytes 73760 | tf_op jit(solution)/shard_map/ppermute | solution.py:284
  19.9 0.1 collective-permute-start.7
  20.0 0.0 collective-permute-done.8.refs_3_
  20.0 1.2 %project.4.refs_3_ = f32[8,32,256]{2,1,0:T(8,128)S(1)} custom-call(s32[8,128]{1,0:T(8,128)S(4)} %get-tuple-element.36.codes, bf16[2,144,128]{2,1,0:T(8,128)(2,1)S(1)} %collective-permute-done.3.refs_0_, bf16[2,144,128]{2,1,0:T(8,128)(2,1)S(1)} %collective-permute-done.4.refs_1_, bf16[2,144,128]{2,1,0:T(8,128)(2,1)S(1)} %collective-permute-done.6.refs_2_, ...), custom_call_target="tpu_custom_call" | custom-call | flops 2147483648 | tf_op jit(solution)/shard_map/project/pallas_call | solution.py:434
  21.2 0.2 collective-permute-done.7.refs_0_
  21.4 1.6 %project.5 = f32[1,32,2048]{2,1,0:T(8,128)} custom-call(s32[8,128]{1,0:T(8,128)S(4)} %get-tuple-element.36.codes, bf16[4,144,128]{2,1,0:T(8,128)(2,1)S(1)} %collective-permute-done.7.refs_0_, bf16[8,1024,256]{2,1,0:T(8,128)(2,1)S(1)} %hats.2.refs_2_.refs_4_.refs_1_, bf16[8,1024,256]{2,1,0:T(8,128)(2,1)S(1)} %hats.3.refs_3_.refs_5_.refs_2_, ...), custom_call_target="tpu_custom_call" | custom-call | flops 2147483648 | tf_op jit(solution)/shard_map/project/pallas_call | solution.py:434
  (5 shorter events, 0.0 us)
Async XLA Ops:
  2.7 6.8 %collective-permute-start.1 = (bf16[80,128]{1,0:T(8,128)(2,1)S(1)}, bf16[80,128]{1,0:T(8,128)(2,1)S(1)}, u32[]{:S(2)}, u32[]{:S(2)}) collective-permute-start(bf16[80,128]{1,0:T(8,128)(2,1)S(1)} %get-tuple-element.24), channel_id=1, source_target_pairs={{0,8},{1,9},{2,10},{3,11},{4,12},{5,13},{6,14},{7,15},{8,0},{9,1},... | collective-permute-start | bytes 61448 | tf_op jit(solution)/shard_map/ppermute | solution.py:410
  6.8 5.6 %collective-permute-start.2 = (bf16[80,128]{1,0:T(8,128)(2,1)S(1)}, bf16[80,128]{1,0:T(8,128)(2,1)S(1)}, u32[]{:S(2)}, u32[]{:S(2)}) collective-permute-start(bf16[80,128]{1,0:T(8,128)(2,1)S(1)} %get-tuple-element.25), channel_id=1, source_target_pairs={{0,9},{1,8},{2,11},{3,10},{4,13},{5,12},{6,15},{7,14},{8,1},{9,0},... | collective-permute-start | bytes 61448 | tf_op jit(solution)/shard_map/ppermute | solution.py:410
  8.1 4.3 %collective-permute-start = (bf16[80,128]{1,0:T(8,128)(2,1)S(1)}, bf16[80,128]{1,0:T(8,128)(2,1)S(1)}, u32[]{:S(2)}, u32[]{:S(2)}) collective-permute-start(bf16[80,128]{1,0:T(8,128)(2,1)S(1)} %get-tuple-element.25), channel_id=1, source_target_pairs={{0,1},{1,0},{2,3},{3,2},{4,5},{5,4},{6,7},{7,6},{8,9},{9,8},{10,11... | collective-permute-start | bytes 61448 | tf_op jit(solution)/shard_map/ppermute | solution.py:410
  12.4 5.3 %collective-permute-start.6 = (bf16[2,144,128]{2,1,0:T(8,128)(2,1)S(1)}, bf16[2,144,128]{2,1,0:T(8,128)(2,1)S(1)}, u32[]{:S(2)}, u32[]{:S(2)}) collective-permute-start(bf16[2,144,128]{2,1,0:T(8,128)(2,1)S(1)} %pad_maximum_fusion.2.refs_0_), channel_id=1, source_target_pairs={{0,6},{2,4},{4,2},{6,0},{8,14},{10,12},{12,10},{14,8},{1,7},{3,5},... | collective-permute-start | bytes 221192 | tf_op jit(solution)/shard_map/ppermute | solution.py:284
  15.0 2.8 %collective-permute-start.5 = (bf16[2,144,128]{2,1,0:T(8,128)(2,1)S(1)}, bf16[2,144,128]{2,1,0:T(8,128)(2,1)S(1)}, u32[]{:S(2)}, u32[]{:S(2)}) collective-permute-start(bf16[2,144,128]{2,1,0:T(8,128)(2,1)S(1)} %pad_maximum_fusion.2.refs_0_), channel_id=1, source_target_pairs={{0,16},{16,0},{1,17},{17,1},{2,18},{18,2},{3,19},{19,3},{4,20},{20... | collective-permute-start | bytes 221192 | tf_op jit(solution)/shard_map/ppermute | solution.py:280
  15.0 4.7 %collective-permute-start.4 = (bf16[2,144,128]{2,1,0:T(8,128)(2,1)S(1)}, bf16[2,144,128]{2,1,0:T(8,128)(2,1)S(1)}, u32[]{:S(2)}, u32[]{:S(2)}) collective-permute-start(bf16[2,144,128]{2,1,0:T(8,128)(2,1)S(1)} %pad_maximum_fusion.2.refs_0_), channel_id=1, source_target_pairs={{0,2},{2,0},{4,6},{6,4},{8,10},{10,8},{12,14},{14,12},{1,3},{3,1},... | collective-permute-start | bytes 221192 | tf_op jit(solution)/shard_map/ppermute | solution.py:284
  15.5 4.4 %collective-permute-start.3 = (bf16[2,144,128]{2,1,0:T(8,128)(2,1)S(1)}, bf16[2,144,128]{2,1,0:T(8,128)(2,1)S(1)}, u32[]{:S(2)}, u32[]{:S(2)}) collective-permute-start(bf16[2,144,128]{2,1,0:T(8,128)(2,1)S(1)} %pad_maximum_fusion.2.refs_0_), channel_id=1, source_target_pairs={{0,4},{2,6},{4,0},{6,2},{8,12},{10,14},{12,8},{14,10},{1,5},{3,7},... | collective-permute-start | bytes 221192 | tf_op jit(solution)/shard_map/ppermute | solution.py:284
  17.7 2.3 %collective-permute-start.8 = (bf16[2,144,128]{2,1,0:T(8,128)(2,1)S(1)}, bf16[2,144,128]{2,1,0:T(8,128)(2,1)S(1)}, u32[]{:S(2)}, u32[]{:S(2)}) collective-permute-start(bf16[2,144,128]{2,1,0:T(8,128)(2,1)S(1)} %collective-permute-done.6.refs_2_), channel_id=1, source_target_pairs={{0,16},{16,0},{1,17},{17,1},{2,18},{18,2},{3,19},{19,3},{4,20},{20... | collective-permute-start | bytes 221192 | tf_op jit(solution)/shard_map/ppermute | solution.py:280
  19.9 1.4 %collective-permute-start.7 = (bf16[4,144,128]{2,1,0:T(8,128)(2,1)S(1)}, bf16[4,144,128]{2,1,0:T(8,128)(2,1)S(1)}, u32[]{:S(2)}, u32[]{:S(2)}) collective-permute-start(bf16[4,144,128]{2,1,0:T(8,128)(2,1)S(1)} %pad_maximum_fusion), channel_id=1, source_target_pairs={{0,16},{16,0},{1,17},{17,1},{2,18},{18,2},{3,19},{19,3},{4,20},{20... | collective-permute-start | bytes 442376 | tf_op jit(solution)/shard_map/ppermute | solution.py:280

commit v9 on v8

--- a/solution.py
+++ b/solution.py
@@ -26,14 +26,24 @@
     return high, (value - high.astype(jnp.float32)).astype(jnp.bfloat16)
 
 
-def banded(value, taps, starts):
+def banded(blocks, taps, starts):
     tap_high, tap_low = taps
+    count = tap_high.shape[0] // LANES
     dot = functools.partial(jnp.dot, preferred_element_type=jnp.float32)
-    cut = [value[:, start : start + tap_high.shape[0]] for start in starts]
-    high, low = split(jnp.concatenate(cut, axis=0))
+    parts = [split(block) for block in blocks]
+    high, low = (
+        jnp.concatenate(
+            [
+                jnp.concatenate([part[which] for part in parts[at : at + count]], axis=1)
+                for at in starts
+            ],
+            axis=0,
+        )
+        for which in range(2)
+    )
     both = dot(jnp.concatenate([high, low], axis=0), tap_high)
     result = both[: high.shape[0]] + (both[high.shape[0] :] + dot(high, tap_low))
-    rows = value.shape[0]
+    rows = blocks[0].shape[0]
     return [result[index * rows : (index + 1) * rows] for index in range(len(starts))]
 
 
@@ -46,16 +56,15 @@
 
 
 def filter_kernel(plan, width, blocks_ref, trig_table, code_table, rows_ref, *refs):
-    tiles, outs, first_bin, packing = plan
+    tiles, outs, first_bin, smooth_blocks, packing = plan
     full, rows_of_block, groups = packing
-    outputs, (trig, codes, blocks, padded, raw, smooth, arrived) = (
+    outputs, (trig, codes, blocks, padded, arrived) = (
         refs[:tiles],
         refs[tiles:],
     )
     local, slices, bins = rows_ref.shape
     block_total = bins // LANES
-    raw_wide = raw.shape[1]
-    smooth_blocks = smooth.shape[1] // LANES
+    raw_wide = (smooth_blocks + 2) * LANES
     height = local * slices
     ahead = 2 * LANES
 
@@ -97,29 +106,30 @@
         copy.wait()
     first = place * local
     mine = lax.axis_index("tile")
-    starts = []
+    starts, raw = [], []
     for turn in range(tiles):
         tile = lax.rem(mine - turn + tiles, tiles)
         for angle in range(local):
             start = blocks[tile, first + angle]
             starts.append(start)
-            at = (turn * local + angle) * slices
             lanes = pl.ds(pl.multiple_of(start * LANES, LANES), raw_wide)
-            raw[at : at + slices, :] = padded[angle, :, lanes]
-    pairs = range(0, smooth_blocks * LANES, 256)
-    for at, value in zip(pairs, banded(raw[...], paganin, pairs)):
-        smooth[:, at : at + 256] = value
-    for index, start in enumerate(starts):
-        at = slice(index * slices, (index + 1) * slices)
-        for j in range(smooth_blocks):
-            if 1 <= j <= WIN // LANES:
-                continue
+            raw.append(padded[angle, :, lanes])
+    raw = jnp.concatenate(raw, axis=0)
+    raw = [raw[:, at : at + LANES] for at in range(0, raw_wide, LANES)]
+    smooth = []
+    for pair in banded(raw, paganin, range(0, smooth_blocks, 2)):
+        smooth += [pair[:, :LANES], pair[:, LANES:]]
+    for j in range(smooth_blocks):
+        if 1 <= j <= WIN // LANES:
+            continue
+        kept = []
+        for index, start in enumerate(starts):
             block = start - 1 + j
             inside = jnp.logical_and(block >= 0, block < block_total)
-            lanes = slice(j * LANES, (j + 1) * LANES)
-            smooth[at, lanes] = jnp.where(inside, smooth[at, lanes], 0.0)
-    lanes = range(0, outs * LANES, LANES)
-    for j, value in enumerate(banded(smooth[...], ramp, lanes)):
+            value = smooth[j][index * slices : (index + 1) * slices]
+            kept.append(jnp.where(inside, value, 0.0))
+        smooth[j] = jnp.concatenate(kept, axis=0)
+    for j, value in enumerate(banded(smooth, ramp, range(outs))):
         for turn in range(tiles):
             part = value[turn * height : (turn + 1) * height]
             if j == full:
@@ -348,7 +358,7 @@
     code_table = in_rows(codes.astype(np.int32))
 
     *cut, trig, codes = pl.pallas_call(
-        functools.partial(filter_kernel, (tiles, outs, first_bin, packing)),
+        functools.partial(filter_kernel, (tiles, outs, first_bin, smooth_blocks, packing)),
         out_shape=[
             jax.ShapeDtypeStruct((full * rows_of_block + -(-tail // 16) * 16, LANES), jnp.bfloat16)
         ]
@@ -362,8 +372,6 @@
                 (local, slices, (block_total - WIN // LANES + smooth_blocks + 2) * LANES),
                 jnp.float32,
             ),
-            pltpu.VMEM((height * tiles, (smooth_blocks + 2) * LANES), jnp.float32),
-            pltpu.VMEM((height * tiles, smooth_blocks * LANES), jnp.float32),
             pltpu.SemaphoreType.DMA((local + 3,)),
         ],
         compiler_params=params,

time: 23.1 us -> 23.1 us (level)
  no operation moved by 1% of the time
where the time goes in v9:
time: 23.1 us; the launch traced here: 22.9 us
  starting transfers between devices  9.27 us (40%)
  Pallas kernels  7.77 us (34%)
  waiting for transfers between devices  5.11 us (22%)
  between operations  0.74 us (3%)
    ppermute x3, starting transfers between devices, joint(): return lax.ppermute(cut[turn], ('angle', 'tile'), pairs)  5.64 us
    ppermute x3, starting transfers between devices, swapped(): lax.ppermute(value, axis, [(i, i ^ by) for i in range(lax.axis_size(axis))])  3.55 us
    pallas_call x3, Pallas kernels, project(): pl.pallas_call(functools.partial(project_kernel, (parts, sources, len(win...  3.46 us
    ppermute x3, waiting for transfers between devices, joint(): return lax.ppermute(cut[turn], ('angle', 'tile'), pairs)  2.88 us
    pallas_call x2, Pallas kernels, hats_of(): pl.pallas_call(functools.partial(hat_kernel, (part, half, tile_rows, angl...  2.3 us
    ppermute x3, waiting for transfers between devices, swapped(): lax.ppermute(value, axis, [(i, i ^ by) for i in range(lax.axis_size(axis))])  2.05 us
    pallas_call x1, Pallas kernels, body(): pl.pallas_call(functools.partial(filter_kernel, (tiles, outs, first_bin,...  2.01 us
  transfers between devices with their start and end apart: 9, of which 5 were waited for; matrix products, arithmetic and copies ran while one was open for 0% of the time, Pallas kernels for 18%

profile of v9, /device:TPU:0, one launch (start us, length us, event | category | flops | bytes accessed | tf_op | source)
XLA Modules:
  0.0 22.9 jit_solution(12094382736145183363)
XLA Ops:
  0.7 2.0 %filter.1 = (bf16[80,128]{1,0:T(8,128)(2,1)S(1)}, bf16[80,128]{1,0:T(8,128)(2,1)S(1)}, f32[8,128]{1,0:T(8,128)S(4)}, s32[8,128]{1,0:T(8,128)S(4)}) custom-call(f32[1]{0:T(128)S(6)} %copy.6.width, s32[2,32]{1,0:T(2,128)} %bitcast.17, f32[16,8,128]{2,1,0:T(8,128)} %constant.4.clone.trig_table, s32[16,8,128]{2,1,0:T(8,128)} %constant.5.clone.code_table, ...), custom_call_target="tpu_custom_call" | custom-call | tf_op jit(solution)/shard_map/filter/pallas_call | solution.py:360
  2.7 4.1 %collective-permute-start.1 = (bf16[80,128]{1,0:T(8,128)(2,1)S(1)}, bf16[80,128]{1,0:T(8,128)(2,1)S(1)}, u32[]{:S(2)}, u32[]{:S(2)}) collective-permute-start(bf16[80,128]{1,0:T(8,128)(2,1)S(1)} %get-tuple-element.24), channel_id=1, source_target_pairs={{0,8},{1,9},{2,10},{3,11},{4,12},{5,13},{6,14},{7,15},{8,0},{9,1},... | collective-permute-start | bytes 61448 | tf_op jit(solution)/shard_map/ppermute | solution.py:418
  6.8 1.3 %collective-permute-start.2 = (bf16[80,128]{1,0:T(8,128)(2,1)S(1)}, bf16[80,128]{1,0:T(8,128)(2,1)S(1)}, u32[]{:S(2)}, u32[]{:S(2)}) collective-permute-start(bf16[80,128]{1,0:T(8,128)(2,1)S(1)} %get-tuple-element.25), channel_id=1, source_target_pairs={{0,9},{1,8},{2,11},{3,10},{4,13},{5,12},{6,15},{7,14},{8,1},{9,0},... | collective-permute-start | bytes 61448 | tf_op jit(solution)/shard_map/ppermute | solution.py:418
  8.1 0.2 %collective-permute-start = (bf16[80,128]{1,0:T(8,128)(2,1)S(1)}, bf16[80,128]{1,0:T(8,128)(2,1)S(1)}, u32[]{:S(2)}, u32[]{:S(2)}) collective-permute-start(bf16[80,128]{1,0:T(8,128)(2,1)S(1)} %get-tuple-element.25), channel_id=1, source_target_pairs={{0,1},{1,0},{2,3},{3,2},{4,5},{5,4},{6,7},{7,6},{8,9},{9,8},{10,11... | collective-permute-start | bytes 61448 | tf_op jit(solution)/shard_map/ppermute | solution.py:418
  8.3 1.1 %hats.2.refs_2_.refs_4_.refs_1_ = bf16[8,1024,256]{2,1,0:T(8,128)(2,1)S(1)} custom-call(f32[8,128]{1,0:T(8,128)S(4)} %get-tuple-element.35.trig, s32[8,128]{1,0:T(8,128)S(4)} %get-tuple-element.36.codes), custom_call_target="tpu_custom_call" | custom-call | flops 33554432 | tf_op jit(solution)/shard_map/hats/pallas_call | solution.py:390
  9.5 0.0 collective-permute-done.1
  9.5 2.9 %collective-permute-done.2 = bf16[80,128]{1,0:T(8,128)(2,1)S(1)} collective-permute-done((bf16[80,128]{1,0:T(8,128)(2,1)S(1)}, bf16[80,128]{1,0:T(8,128)(2,1)S(1)}, u32[]{:S(2)}, u32[]{:S(2)}) %collective-permute-start.2) | collective-permute-done | bytes 20512 | tf_op jit(solution)/shard_map/ppermute | solution.py:418
  12.4 0.0 collective-permute-done
  12.4 2.6 %collective-permute-start.6 = (bf16[2,144,128]{2,1,0:T(8,128)(2,1)S(1)}, bf16[2,144,128]{2,1,0:T(8,128)(2,1)S(1)}, u32[]{:S(2)}, u32[]{:S(2)}) collective-permute-start(bf16[2,144,128]{2,1,0:T(8,128)(2,1)S(1)} %pad_maximum_fusion.2.refs_0_), channel_id=1, source_target_pairs={{0,6},{2,4},{4,2},{6,0},{8,14},{10,12},{12,10},{14,8},{1,7},{3,5},... | collective-permute-start | bytes 221192 | tf_op jit(solution)/shard_map/ppermute | solution.py:294
  15.0 0.0 collective-permute-start.5
  15.0 0.5 %collective-permute-start.4 = (bf16[2,144,128]{2,1,0:T(8,128)(2,1)S(1)}, bf16[2,144,128]{2,1,0:T(8,128)(2,1)S(1)}, u32[]{:S(2)}, u32[]{:S(2)}) collective-permute-start(bf16[2,144,128]{2,1,0:T(8,128)(2,1)S(1)} %pad_maximum_fusion.2.refs_0_), channel_id=1, source_target_pairs={{0,2},{2,0},{4,6},{6,4},{8,10},{10,8},{12,14},{14,12},{1,3},{3,1},... | collective-permute-start | bytes 221192 | tf_op jit(solution)/shard_map/ppermute | solution.py:294
  15.5 0.5 %collective-permute-start.3 = (bf16[2,144,128]{2,1,0:T(8,128)(2,1)S(1)}, bf16[2,144,128]{2,1,0:T(8,128)(2,1)S(1)}, u32[]{:S(2)}, u32[]{:S(2)}) collective-permute-start(bf16[2,144,128]{2,1,0:T(8,128)(2,1)S(1)} %pad_maximum_fusion.2.refs_0_), channel_id=1, source_target_pairs={{0,4},{2,6},{4,0},{6,2},{8,12},{10,14},{12,8},{14,10},{1,5},{3,7},... | collective-permute-start | bytes 221192 | tf_op jit(solution)/shard_map/ppermute | solution.py:294
  16.0 1.2 %hats.3.refs_3_.refs_5_.refs_2_ = bf16[8,1024,256]{2,1,0:T(8,128)(2,1)S(1)} custom-call(f32[8,128]{1,0:T(8,128)S(4)} %get-tuple-element.35.trig, s32[8,128]{1,0:T(8,128)S(4)} %get-tuple-element.36.codes), custom_call_target="tpu_custom_call" | custom-call | flops 33554432 | tf_op jit(solution)/shard_map/hats/pallas_call | solution.py:390
  17.1 0.6 %collective-permute-done.6.refs_2_ = bf16[2,144,128]{2,1,0:T(8,128)(2,1)S(1)} collective-permute-done((bf16[2,144,128]{2,1,0:T(8,128)(2,1)S(1)}, bf16[2,144,128]{2,1,0:T(8,128)(2,1)S(1)}, u32[]{:S(2)}, u32[]{:S(2)}) %collective-permute-start.6) | collective-permute-done | bytes 73760 | tf_op jit(solution)/shard_map/ppermute | solution.py:294
  17.7 0.0 collective-permute-done.5.refs_1_
  17.7 0.0 collective-permute-start.8
  17.7 0.7 %project.3.refs_6_ = f32[8,32,256]{2,1,0:T(8,128)S(1)} custom-call(s32[8,128]{1,0:T(8,128)S(4)} %get-tuple-element.36.codes, bf16[2,144,128]{2,1,0:T(8,128)(2,1)S(1)} %pad_maximum_fusion.2.refs_0_, bf16[2,144,128]{2,1,0:T(8,128)(2,1)S(1)} %collective-permute-done.5.refs_1_, bf16[8,1024,256]{2,1,0:T(8,128)(2,1)S(1)} %hats.2.refs_2_.refs_4_.refs_1_, ...), custom_call_target="tpu_custom_call" | custom-call | flops 2147483648 | tf_op jit(solution)/shard_map/project/pallas_call | solution.py:442
  18.5 1.2 %collective-permute-done.4.refs_1_ = bf16[2,144,128]{2,1,0:T(8,128)(2,1)S(1)} collective-permute-done((bf16[2,144,128]{2,1,0:T(8,128)(2,1)S(1)}, bf16[2,144,128]{2,1,0:T(8,128)(2,1)S(1)}, u32[]{:S(2)}, u32[]{:S(2)}) %collective-permute-start.4) | collective-permute-done | bytes 73760 | tf_op jit(solution)/shard_map/ppermute | solution.py:294
  19.7 0.3 %collective-permute-done.3.refs_0_ = bf16[2,144,128]{2,1,0:T(8,128)(2,1)S(1)} collective-permute-done((bf16[2,144,128]{2,1,0:T(8,128)(2,1)S(1)}, bf16[2,144,128]{2,1,0:T(8,128)(2,1)S(1)}, u32[]{:S(2)}, u32[]{:S(2)}) %collective-permute-start.3) | collective-permute-done | bytes 73760 | tf_op jit(solution)/shard_map/ppermute | solution.py:294
  19.9 0.1 collective-permute-start.7
  20.0 0.0 collective-permute-done.8.refs_3_
  20.0 1.2 %project.4.refs_3_ = f32[8,32,256]{2,1,0:T(8,128)S(1)} custom-call(s32[8,128]{1,0:T(8,128)S(4)} %get-tuple-element.36.codes, bf16[2,144,128]{2,1,0:T(8,128)(2,1)S(1)} %collective-permute-done.3.refs_0_, bf16[2,144,128]{2,1,0:T(8,128)(2,1)S(1)} %collective-permute-done.4.refs_1_, bf16[2,144,128]{2,1,0:T(8,128)(2,1)S(1)} %collective-permute-done.6.refs_2_, ...), custom_call_target="tpu_custom_call" | custom-call | flops 2147483648 | tf_op jit(solution)/shard_map/project/pallas_call | solution.py:442
  21.2 0.2 collective-permute-done.7.refs_0_
  21.4 1.6 %project.5 = f32[1,32,2048]{2,1,0:T(8,128)} custom-call(s32[8,128]{1,0:T(8,128)S(4)} %get-tuple-element.36.codes, bf16[4,144,128]{2,1,0:T(8,128)(2,1)S(1)} %collective-permute-done.7.refs_0_, bf16[8,1024,256]{2,1,0:T(8,128)(2,1)S(1)} %hats.2.refs_2_.refs_4_.refs_1_, bf16[8,1024,256]{2,1,0:T(8,128)(2,1)S(1)} %hats.3.refs_3_.refs_5_.refs_2_, ...), custom_call_target="tpu_custom_call" | custom-call | flops 2147483648 | tf_op jit(solution)/shard_map/project/pallas_call | solution.py:442
  (5 shorter events, 0.0 us)
Async XLA Ops:
  2.7 6.8 %collective-permute-start.1 = (bf16[80,128]{1,0:T(8,128)(2,1)S(1)}, bf16[80,128]{1,0:T(8,128)(2,1)S(1)}, u32[]{:S(2)}, u32[]{:S(2)}) collective-permute-start(bf16[80,128]{1,0:T(8,128)(2,1)S(1)} %get-tuple-element.24), channel_id=1, source_target_pairs={{0,8},{1,9},{2,10},{3,11},{4,12},{5,13},{6,14},{7,15},{8,0},{9,1},... | collective-permute-start | bytes 61448 | tf_op jit(solution)/shard_map/ppermute | solution.py:418
  6.8 5.6 %collective-permute-start.2 = (bf16[80,128]{1,0:T(8,128)(2,1)S(1)}, bf16[80,128]{1,0:T(8,128)(2,1)S(1)}, u32[]{:S(2)}, u32[]{:S(2)}) collective-permute-start(bf16[80,128]{1,0:T(8,128)(2,1)S(1)} %get-tuple-element.25), channel_id=1, source_target_pairs={{0,9},{1,8},{2,11},{3,10},{4,13},{5,12},{6,15},{7,14},{8,1},{9,0},... | collective-permute-start | bytes 61448 | tf_op jit(solution)/shard_map/ppermute | solution.py:418
  8.1 4.3 %collective-permute-start = (bf16[80,128]{1,0:T(8,128)(2,1)S(1)}, bf16[80,128]{1,0:T(8,128)(2,1)S(1)}, u32[]{:S(2)}, u32[]{:S(2)}) collective-permute-start(bf16[80,128]{1,0:T(8,128)(2,1)S(1)} %get-tuple-element.25), channel_id=1, source_target_pairs={{0,1},{1,0},{2,3},{3,2},{4,5},{5,4},{6,7},{7,6},{8,9},{9,8},{10,11... | collective-permute-start | bytes 61448 | tf_op jit(solution)/shard_map/ppermute | solution.py:418
  12.4 5.3 %collective-permute-start.6 = (bf16[2,144,128]{2,1,0:T(8,128)(2,1)S(1)}, bf16[2,144,128]{2,1,0:T(8,128)(2,1)S(1)}, u32[]{:S(2)}, u32[]{:S(2)}) collective-permute-start(bf16[2,144,128]{2,1,0:T(8,128)(2,1)S(1)} %pad_maximum_fusion.2.refs_0_), channel_id=1, source_target_pairs={{0,6},{2,4},{4,2},{6,0},{8,14},{10,12},{12,10},{14,8},{1,7},{3,5},... | collective-permute-start | bytes 221192 | tf_op jit(solution)/shard_map/ppermute | solution.py:294
  15.0 2.8 %collective-permute-start.5 = (bf16[2,144,128]{2,1,0:T(8,128)(2,1)S(1)}, bf16[2,144,128]{2,1,0:T(8,128)(2,1)S(1)}, u32[]{:S(2)}, u32[]{:S(2)}) collective-permute-start(bf16[2,144,128]{2,1,0:T(8,128)(2,1)S(1)} %pad_maximum_fusion.2.refs_0_), channel_id=1, source_target_pairs={{0,16},{16,0},{1,17},{17,1},{2,18},{18,2},{3,19},{19,3},{4,20},{20... | collective-permute-start | bytes 221192 | tf_op jit(solution)/shard_map/ppermute | solution.py:290
  15.0 4.7 %collective-permute-start.4 = (bf16[2,144,128]{2,1,0:T(8,128)(2,1)S(1)}, bf16[2,144,128]{2,1,0:T(8,128)(2,1)S(1)}, u32[]{:S(2)}, u32[]{:S(2)}) collective-permute-start(bf16[2,144,128]{2,1,0:T(8,128)(2,1)S(1)} %pad_maximum_fusion.2.refs_0_), channel_id=1, source_target_pairs={{0,2},{2,0},{4,6},{6,4},{8,10},{10,8},{12,14},{14,12},{1,3},{3,1},... | collective-permute-start | bytes 221192 | tf_op jit(solution)/shard_map/ppermute | solution.py:294
  15.5 4.4 %collective-permute-start.3 = (bf16[2,144,128]{2,1,0:T(8,128)(2,1)S(1)}, bf16[2,144,128]{2,1,0:T(8,128)(2,1)S(1)}, u32[]{:S(2)}, u32[]{:S(2)}) collective-permute-start(bf16[2,144,128]{2,1,0:T(8,128)(2,1)S(1)} %pad_maximum_fusion.2.refs_0_), channel_id=1, source_target_pairs={{0,4},{2,6},{4,0},{6,2},{8,12},{10,14},{12,8},{14,10},{1,5},{3,7},... | collective-permute-start | bytes 221192 | tf_op jit(solution)/shard_map/ppermute | solution.py:294
  17.7 2.3 %collective-permute-start.8 = (bf16[2,144,128]{2,1,0:T(8,128)(2,1)S(1)}, bf16[2,144,128]{2,1,0:T(8,128)(2,1)S(1)}, u32[]{:S(2)}, u32[]{:S(2)}) collective-permute-start(bf16[2,144,128]{2,1,0:T(8,128)(2,1)S(1)} %collective-permute-done.6.refs_2_), channel_id=1, source_target_pairs={{0,16},{16,0},{1,17},{17,1},{2,18},{18,2},{3,19},{19,3},{4,20},{20... | collective-permute-start | bytes 221192 | tf_op jit(solution)/shard_map/ppermute | solution.py:290
  19.9 1.4 %collective-permute-start.7 = (bf16[4,144,128]{2,1,0:T(8,128)(2,1)S(1)}, bf16[4,144,128]{2,1,0:T(8,128)(2,1)S(1)}, u32[]{:S(2)}, u32[]{:S(2)}) collective-permute-start(bf16[4,144,128]{2,1,0:T(8,128)(2,1)S(1)} %pad_maximum_fusion), channel_id=1, source_target_pairs={{0,16},{16,0},{1,17},{17,1},{2,18},{18,2},{3,19},{19,3},{4,20},{20... | collective-permute-start | bytes 442376 | tf_op jit(solution)/shard_map/ppermute | solution.py:290

commit v10 on v9

--- a/solution.py
+++ b/solution.py
@@ -191,6 +191,26 @@
         return carry
 
     lax.fori_loop(0, count, step, 0, unroll=2)
+
+
+def by_rows(sums):
+    sides = len(sums)
+    lane = lax.broadcasted_iota(jnp.int32, (sums[0].shape[0], LANES), 1)
+    rows = []
+    for first in range(0, sums[0].shape[1], LANES):
+        turned = [
+            value[:, first : first + LANES]
+            if side == 0
+            else pltpu.roll(value[:, first : first + LANES], side * CHUNK, 1)
+            for side, value in enumerate(sums)
+        ]
+        for row in range(sides):
+            merged = turned[-row % sides]
+            for place in range(1, sides):
+                more = turned[(place - row) % sides]
+                merged = jnp.where(lane < place * CHUNK, merged, more)
+            rows.append(pltpu.roll(merged, LANES - row * CHUNK, 1) if row else merged)
+    return rows
 
 
 def project_kernel(plan, codes, *refs):
@@ -260,10 +280,7 @@
         if not last or (chunk + 1) * CHUNK % LANES:
             continue
         mine = lax.axis_index("tile")
-        for row in range(ROWS_DEV):
-            value = jnp.concatenate(
-                [part[:, row * CHUNK : (row + 1) * CHUNK] for part in sums], axis=1
-            )
+        for row, value in enumerate(by_rows(sums)):
             at = row * TCOLS + (chunk + 1) * CHUNK - LANES
             if slices % 8 == 0:
                 for turn in range(tiles):

time: 23.1 us -> 23.1 us (level)
  no operation moved by 1% of the time
where the time goes in v10:
time: 23.1 us; the launch traced here: 23 us
  starting transfers between devices  9.27 us (40%)
  Pallas kernels  7.82 us (34%)
  waiting for transfers between devices  5.12 us (22%)
  between operations  0.74 us (3%)
    ppermute x3, starting transfers between devices, joint(): return lax.ppermute(cut[turn], ('angle', 'tile'), pairs)  5.64 us
    ppermute x3, starting transfers between devices, swapped(): lax.ppermute(value, axis, [(i, i ^ by) for i in range(lax.axis_size(axis))])  3.55 us
    pallas_call x3, Pallas kernels, project(): pl.pallas_call(functools.partial(project_kernel, (parts, sources, len(win...  3.51 us
    ppermute x3, waiting for transfers between devices, joint(): return lax.ppermute(cut[turn], ('angle', 'tile'), pairs)  2.88 us
    pallas_call x2, Pallas kernels, hats_of(): pl.pallas_call(functools.partial(hat_kernel, (part, half, tile_rows, angl...  2.3 us
    ppermute x3, waiting for transfers between devices, swapped(): lax.ppermute(value, axis, [(i, i ^ by) for i in range(lax.axis_size(axis))])  2.05 us
    pallas_call x1, Pallas kernels, body(): pl.pallas_call(functools.partial(filter_kernel, (tiles, outs, first_bin,...  2.01 us
  transfers between devices with their start and end apart: 9, of which 5 were waited for; matrix products, arithmetic and copies ran while one was open for 0% of the time, Pallas kernels for 18%

profile of v10, /device:TPU:0, one launch (start us, length us, event | category | flops | bytes accessed | tf_op | source)
XLA Modules:
  0.0 23.0 jit_solution(10763836706837853388)
XLA Ops:
  0.7 2.0 %filter.1 = (bf16[80,128]{1,0:T(8,128)(2,1)S(1)}, bf16[80,128]{1,0:T(8,128)(2,1)S(1)}, f32[8,128]{1,0:T(8,128)S(4)}, s32[8,128]{1,0:T(8,128)S(4)}) custom-call(f32[1]{0:T(128)S(6)} %copy.6.width, s32[2,32]{1,0:T(2,128)} %bitcast.17, f32[16,8,128]{2,1,0:T(8,128)} %constant.4.clone.trig_table, s32[16,8,128]{2,1,0:T(8,128)} %constant.5.clone.code_table, ...), custom_call_target="tpu_custom_call" | custom-call | tf_op jit(solution)/shard_map/filter/pallas_call | solution.py:377
  2.7 4.1 %collective-permute-start.1 = (bf16[80,128]{1,0:T(8,128)(2,1)S(1)}, bf16[80,128]{1,0:T(8,128)(2,1)S(1)}, u32[]{:S(2)}, u32[]{:S(2)}) collective-permute-start(bf16[80,128]{1,0:T(8,128)(2,1)S(1)} %get-tuple-element.24), channel_id=1, source_target_pairs={{0,8},{1,9},{2,10},{3,11},{4,12},{5,13},{6,14},{7,15},{8,0},{9,1},... | collective-permute-start | bytes 61448 | tf_op jit(solution)/shard_map/ppermute | solution.py:435
  6.8 1.3 %collective-permute-start.2 = (bf16[80,128]{1,0:T(8,128)(2,1)S(1)}, bf16[80,128]{1,0:T(8,128)(2,1)S(1)}, u32[]{:S(2)}, u32[]{:S(2)}) collective-permute-start(bf16[80,128]{1,0:T(8,128)(2,1)S(1)} %get-tuple-element.25), channel_id=1, source_target_pairs={{0,9},{1,8},{2,11},{3,10},{4,13},{5,12},{6,15},{7,14},{8,1},{9,0},... | collective-permute-start | bytes 61448 | tf_op jit(solution)/shard_map/ppermute | solution.py:435
  8.1 0.2 %collective-permute-start = (bf16[80,128]{1,0:T(8,128)(2,1)S(1)}, bf16[80,128]{1,0:T(8,128)(2,1)S(1)}, u32[]{:S(2)}, u32[]{:S(2)}) collective-permute-start(bf16[80,128]{1,0:T(8,128)(2,1)S(1)} %get-tuple-element.25), channel_id=1, source_target_pairs={{0,1},{1,0},{2,3},{3,2},{4,5},{5,4},{6,7},{7,6},{8,9},{9,8},{10,11... | collective-permute-start | bytes 61448 | tf_op jit(solution)/shard_map/ppermute | solution.py:435
  8.3 1.1 %hats.2.refs_2_.refs_4_.refs_1_ = bf16[8,1024,256]{2,1,0:T(8,128)(2,1)S(1)} custom-call(f32[8,128]{1,0:T(8,128)S(4)} %get-tuple-element.35.trig, s32[8,128]{1,0:T(8,128)S(4)} %get-tuple-element.36.codes), custom_call_target="tpu_custom_call" | custom-call | flops 33554432 | tf_op jit(solution)/shard_map/hats/pallas_call | solution.py:407
  9.5 0.0 collective-permute-done.1
  9.5 2.9 %collective-permute-done.2 = bf16[80,128]{1,0:T(8,128)(2,1)S(1)} collective-permute-done((bf16[80,128]{1,0:T(8,128)(2,1)S(1)}, bf16[80,128]{1,0:T(8,128)(2,1)S(1)}, u32[]{:S(2)}, u32[]{:S(2)}) %collective-permute-start.2) | collective-permute-done | bytes 20512 | tf_op jit(solution)/shard_map/ppermute | solution.py:435
  12.4 0.0 collective-permute-done
  12.4 2.6 %collective-permute-start.6 = (bf16[2,144,128]{2,1,0:T(8,128)(2,1)S(1)}, bf16[2,144,128]{2,1,0:T(8,128)(2,1)S(1)}, u32[]{:S(2)}, u32[]{:S(2)}) collective-permute-start(bf16[2,144,128]{2,1,0:T(8,128)(2,1)S(1)} %pad_maximum_fusion.2.refs_0_), channel_id=1, source_target_pairs={{0,6},{2,4},{4,2},{6,0},{8,14},{10,12},{12,10},{14,8},{1,7},{3,5},... | collective-permute-start | bytes 221192 | tf_op jit(solution)/shard_map/ppermute | solution.py:311
  15.0 0.0 collective-permute-start.5
  15.0 0.5 %collective-permute-start.4 = (bf16[2,144,128]{2,1,0:T(8,128)(2,1)S(1)}, bf16[2,144,128]{2,1,0:T(8,128)(2,1)S(1)}, u32[]{:S(2)}, u32[]{:S(2)}) collective-permute-start(bf16[2,144,128]{2,1,0:T(8,128)(2,1)S(1)} %pad_maximum_fusion.2.refs_0_), channel_id=1, source_target_pairs={{0,2},{2,0},{4,6},{6,4},{8,10},{10,8},{12,14},{14,12},{1,3},{3,1},... | collective-permute-start | bytes 221192 | tf_op jit(solution)/shard_map/ppermute | solution.py:311
  15.5 0.5 %collective-permute-start.3 = (bf16[2,144,128]{2,1,0:T(8,128)(2,1)S(1)}, bf16[2,144,128]{2,1,0:T(8,128)(2,1)S(1)}, u32[]{:S(2)}, u32[]{:S(2)}) collective-permute-start(bf16[2,144,128]{2,1,0:T(8,128)(2,1)S(1)} %pad_maximum_fusion.2.refs_0_), channel_id=1, source_target_pairs={{0,4},{2,6},{4,0},{6,2},{8,12},{10,14},{12,8},{14,10},{1,5},{3,7},... | collective-permute-start | bytes 221192 | tf_op jit(solution)/shard_map/ppermute | solution.py:311
  16.0 1.2 %hats.3.refs_3_.refs_5_.refs_2_ = bf16[8,1024,256]{2,1,0:T(8,128)(2,1)S(1)} custom-call(f32[8,128]{1,0:T(8,128)S(4)} %get-tuple-element.35.trig, s32[8,128]{1,0:T(8,128)S(4)} %get-tuple-element.36.codes), custom_call_target="tpu_custom_call" | custom-call | flops 33554432 | tf_op jit(solution)/shard_map/hats/pallas_call | solution.py:407
  17.1 0.6 %collective-permute-done.6.refs_2_ = bf16[2,144,128]{2,1,0:T(8,128)(2,1)S(1)} collective-permute-done((bf16[2,144,128]{2,1,0:T(8,128)(2,1)S(1)}, bf16[2,144,128]{2,1,0:T(8,128)(2,1)S(1)}, u32[]{:S(2)}, u32[]{:S(2)}) %collective-permute-start.6) | collective-permute-done | bytes 73760 | tf_op jit(solution)/shard_map/ppermute | solution.py:311
  17.7 0.0 collective-permute-done.5.refs_1_
  17.7 0.0 collective-permute-start.8
  17.7 0.7 %project.3.refs_6_ = f32[8,32,256]{2,1,0:T(8,128)S(1)} custom-call(s32[8,128]{1,0:T(8,128)S(4)} %get-tuple-element.36.codes, bf16[2,144,128]{2,1,0:T(8,128)(2,1)S(1)} %pad_maximum_fusion.2.refs_0_, bf16[2,144,128]{2,1,0:T(8,128)(2,1)S(1)} %collective-permute-done.5.refs_1_, bf16[8,1024,256]{2,1,0:T(8,128)(2,1)S(1)} %hats.2.refs_2_.refs_4_.refs_1_, ...), custom_call_target="tpu_custom_call" | custom-call | flops 2147483648 | tf_op jit(solution)/shard_map/project/pallas_call | solution.py:459
  18.5 1.2 %collective-permute-done.4.refs_1_ = bf16[2,144,128]{2,1,0:T(8,128)(2,1)S(1)} collective-permute-done((bf16[2,144,128]{2,1,0:T(8,128)(2,1)S(1)}, bf16[2,144,128]{2,1,0:T(8,128)(2,1)S(1)}, u32[]{:S(2)}, u32[]{:S(2)}) %collective-permute-start.4) | collective-permute-done | bytes 73760 | tf_op jit(solution)/shard_map/ppermute | solution.py:311
  19.7 0.3 %collective-permute-done.3.refs_0_ = bf16[2,144,128]{2,1,0:T(8,128)(2,1)S(1)} collective-permute-done((bf16[2,144,128]{2,1,0:T(8,128)(2,1)S(1)}, bf16[2,144,128]{2,1,0:T(8,128)(2,1)S(1)}, u32[]{:S(2)}, u32[]{:S(2)}) %collective-permute-start.3) | collective-permute-done | bytes 73760 | tf_op jit(solution)/shard_map/ppermute | solution.py:311
  19.9 0.1 collective-permute-start.7
  20.0 0.0 collective-permute-done.8.refs_3_
  20.0 1.2 %project.4.refs_3_ = f32[8,32,256]{2,1,0:T(8,128)S(1)} custom-call(s32[8,128]{1,0:T(8,128)S(4)} %get-tuple-element.36.codes, bf16[2,144,128]{2,1,0:T(8,128)(2,1)S(1)} %collective-permute-done.3.refs_0_, bf16[2,144,128]{2,1,0:T(8,128)(2,1)S(1)} %collective-permute-done.4.refs_1_, bf16[2,144,128]{2,1,0:T(8,128)(2,1)S(1)} %collective-permute-done.6.refs_2_, ...), custom_call_target="tpu_custom_call" | custom-call | flops 2147483648 | tf_op jit(solution)/shard_map/project/pallas_call | solution.py:459
  21.2 0.2 collective-permute-done.7.refs_0_
  21.4 1.6 %project.5 = f32[1,32,2048]{2,1,0:T(8,128)} custom-call(s32[8,128]{1,0:T(8,128)S(4)} %get-tuple-element.36.codes, bf16[4,144,128]{2,1,0:T(8,128)(2,1)S(1)} %collective-permute-done.7.refs_0_, bf16[8,1024,256]{2,1,0:T(8,128)(2,1)S(1)} %hats.2.refs_2_.refs_4_.refs_1_, bf16[8,1024,256]{2,1,0:T(8,128)(2,1)S(1)} %hats.3.refs_3_.refs_5_.refs_2_, ...), custom_call_target="tpu_custom_call" | custom-call | flops 2147483648 | tf_op jit(solution)/shard_map/project/pallas_call | solution.py:459
  (5 shorter events, 0.0 us)
Async XLA Ops:
  2.7 6.8 %collective-permute-start.1 = (bf16[80,128]{1,0:T(8,128)(2,1)S(1)}, bf16[80,128]{1,0:T(8,128)(2,1)S(1)}, u32[]{:S(2)}, u32[]{:S(2)}) collective-permute-start(bf16[80,128]{1,0:T(8,128)(2,1)S(1)} %get-tuple-element.24), channel_id=1, source_target_pairs={{0,8},{1,9},{2,10},{3,11},{4,12},{5,13},{6,14},{7,15},{8,0},{9,1},... | collective-permute-start | bytes 61448 | tf_op jit(solution)/shard_map/ppermute | solution.py:435
  6.8 5.6 %collective-permute-start.2 = (bf16[80,128]{1,0:T(8,128)(2,1)S(1)}, bf16[80,128]{1,0:T(8,128)(2,1)S(1)}, u32[]{:S(2)}, u32[]{:S(2)}) collective-permute-start(bf16[80,128]{1,0:T(8,128)(2,1)S(1)} %get-tuple-element.25), channel_id=1, source_target_pairs={{0,9},{1,8},{2,11},{3,10},{4,13},{5,12},{6,15},{7,14},{8,1},{9,0},... | collective-permute-start | bytes 61448 | tf_op jit(solution)/shard_map/ppermute | solution.py:435
  8.1 4.3 %collective-permute-start = (bf16[80,128]{1,0:T(8,128)(2,1)S(1)}, bf16[80,128]{1,0:T(8,128)(2,1)S(1)}, u32[]{:S(2)}, u32[]{:S(2)}) collective-permute-start(bf16[80,128]{1,0:T(8,128)(2,1)S(1)} %get-tuple-element.25), channel_id=1, source_target_pairs={{0,1},{1,0},{2,3},{3,2},{4,5},{5,4},{6,7},{7,6},{8,9},{9,8},{10,11... | collective-permute-start | bytes 61448 | tf_op jit(solution)/shard_map/ppermute | solution.py:435
  12.4 5.3 %collective-permute-start.6 = (bf16[2,144,128]{2,1,0:T(8,128)(2,1)S(1)}, bf16[2,144,128]{2,1,0:T(8,128)(2,1)S(1)}, u32[]{:S(2)}, u32[]{:S(2)}) collective-permute-start(bf16[2,144,128]{2,1,0:T(8,128)(2,1)S(1)} %pad_maximum_fusion.2.refs_0_), channel_id=1, source_target_pairs={{0,6},{2,4},{4,2},{6,0},{8,14},{10,12},{12,10},{14,8},{1,7},{3,5},... | collective-permute-start | bytes 221192 | tf_op jit(solution)/shard_map/ppermute | solution.py:311
  15.0 2.8 %collective-permute-start.5 = (bf16[2,144,128]{2,1,0:T(8,128)(2,1)S(1)}, bf16[2,144,128]{2,1,0:T(8,128)(2,1)S(1)}, u32[]{:S(2)}, u32[]{:S(2)}) collective-permute-start(bf16[2,144,128]{2,1,0:T(8,128)(2,1)S(1)} %pad_maximum_fusion.2.refs_0_), channel_id=1, source_target_pairs={{0,16},{16,0},{1,17},{17,1},{2,18},{18,2},{3,19},{19,3},{4,20},{20... | collective-permute-start | bytes 221192 | tf_op jit(solution)/shard_map/ppermute | solution.py:307
  15.0 4.7 %collective-permute-start.4 = (bf16[2,144,128]{2,1,0:T(8,128)(2,1)S(1)}, bf16[2,144,128]{2,1,0:T(8,128)(2,1)S(1)}, u32[]{:S(2)}, u32[]{:S(2)}) collective-permute-start(bf16[2,144,128]{2,1,0:T(8,128)(2,1)S(1)} %pad_maximum_fusion.2.refs_0_), channel_id=1, source_target_pairs={{0,2},{2,0},{4,6},{6,4},{8,10},{10,8},{12,14},{14,12},{1,3},{3,1},... | collective-permute-start | bytes 221192 | tf_op jit(solution)/shard_map/ppermute | solution.py:311
  15.5 4.4 %collective-permute-start.3 = (bf16[2,144,128]{2,1,0:T(8,128)(2,1)S(1)}, bf16[2,144,128]{2,1,0:T(8,128)(2,1)S(1)}, u32[]{:S(2)}, u32[]{:S(2)}) collective-permute-start(bf16[2,144,128]{2,1,0:T(8,128)(2,1)S(1)} %pad_maximum_fusion.2.refs_0_), channel_id=1, source_target_pairs={{0,4},{2,6},{4,0},{6,2},{8,12},{10,14},{12,8},{14,10},{1,5},{3,7},... | collective-permute-start | bytes 221192 | tf_op jit(solution)/shard_map/ppermute | solution.py:311
  17.7 2.3 %collective-permute-start.8 = (bf16[2,144,128]{2,1,0:T(8,128)(2,1)S(1)}, bf16[2,144,128]{2,1,0:T(8,128)(2,1)S(1)}, u32[]{:S(2)}, u32[]{:S(2)}) collective-permute-start(bf16[2,144,128]{2,1,0:T(8,128)(2,1)S(1)} %collective-permute-done.6.refs_2_), channel_id=1, source_target_pairs={{0,16},{16,0},{1,17},{17,1},{2,18},{18,2},{3,19},{19,3},{4,20},{20... | collective-permute-start | bytes 221192 | tf_op jit(solution)/shard_map/ppermute | solution.py:307
  19.9 1.4 %collective-permute-start.7 = (bf16[4,144,128]{2,1,0:T(8,128)(2,1)S(1)}, bf16[4,144,128]{2,1,0:T(8,128)(2,1)S(1)}, u32[]{:S(2)}, u32[]{:S(2)}) collective-permute-start(bf16[4,144,128]{2,1,0:T(8,128)(2,1)S(1)} %pad_maximum_fusion), channel_id=1, source_target_pairs={{0,16},{16,0},{1,17},{17,1},{2,18},{18,2},{3,19},{19,3},{4,20},{20... | collective-permute-start | bytes 442376 | tf_op jit(solution)/shard_map/ppermute | solution.py:307

commit v11 on v9

--- a/solution.py
+++ b/solution.py
@@ -474,24 +474,24 @@
         )(codes, *windows, *hats, *sums)
 
     others = range(1, segments)
-    early = [pieces] + [shifted(pieces, "segment", by) for by in others]
-    moved = [swapped(pieces, "angle", mask) for mask in exchanges[-1]]
+    moved = [swapped(pieces, "angle", mask) for mask in reversed(exchanges[-1])][::-1]
     hats += [hats_of(part, (pieces,)) for part in range(len(hats), segments)]
     count = len(moved)
     if count > 1:
-        early, moved[-1] = lax.optimization_barrier((early, moved[-1]))
-    sums = project([(by, 0) for by in range(segments)], early, ())
+        pieces, moved[-1] = lax.optimization_barrier((pieces, moved[-1]))
+    sums = project([(0, 0)], [pieces], ())
     if count > 1:
         moved[:-1], sums = lax.optimization_barrier((moved[:-1], sums))
     else:
         moved, sums = lax.optimization_barrier((moved, sums))
-    ahead = [shifted(moved[-1], "segment", by) for by in others]
+    ahead = jnp.concatenate([pieces, moved[-1]])
+    ahead = [shifted(ahead, "segment", by) for by in others]
     final = [(by, part) for by in others for part in range(1, count)]
     if final:
         rest = jnp.concatenate(moved[:-1])
         late = [shifted(rest, "segment", by) for by in others]
     own = [(0, part + 1) for part in range(count)]
-    first = [(by, count) for by in others]
+    first = [(by, part) for by in others for part in (0, count)]
     if final:
         sums = project(own + first, [*moved, *ahead], (sums,))
         return project(final, late, (sums,), True)

time: 23.1 us -> 23.1 us (level)
  transfers between devices with their start and end apart: 9 -> 8, of which waited for: 5 -> 4; matrix products, arithmetic and copies ran while one was open for 0% -> 0% of each run, Pallas kernels for 18% -> 18%
where the time goes in v11:
time: 23.1 us; the launch traced here: 23 us
  starting transfers between devices  9.34 us (40%)
  Pallas kernels  7.74 us (34%)
  waiting for transfers between devices  5.07 us (22%)
  between operations  0.76 us (3%)
    ppermute x3, starting transfers between devices, joint(): return lax.ppermute(cut[turn], ('angle', 'tile'), pairs)  5.64 us
    ppermute x3, starting transfers between devices, swapped(): lax.ppermute(value, axis, [(i, i ^ by) for i in range(lax.axis_size(axis))])  3.55 us
    pallas_call x3, Pallas kernels, project(): pl.pallas_call(functools.partial(project_kernel, (parts, sources, len(win...  3.44 us
    ppermute x3, waiting for transfers between devices, joint(): return lax.ppermute(cut[turn], ('angle', 'tile'), pairs)  2.88 us
    pallas_call x2, Pallas kernels, hats_of(): pl.pallas_call(functools.partial(hat_kernel, (part, half, tile_rows, angl...  2.3 us
    ppermute x3, waiting for transfers between devices, swapped(): lax.ppermute(value, axis, [(i, i ^ by) for i in range(lax.axis_size(axis))])  2.18 us
    pallas_call x1, Pallas kernels, body(): pl.pallas_call(functools.partial(filter_kernel, (tiles, outs, first_bin,...  2.01 us
  transfers between devices with their start and end apart: 8, of which 4 were waited for; matrix products, arithmetic and copies ran while one was open for 0% of the time, Pallas kernels for 18%

profile of v11, /device:TPU:0, one launch (start us, length us, event | category | flops | bytes accessed | tf_op | source)
XLA Modules:
  0.0 23.0 jit_solution(11227355049270813619)
XLA Ops:
  0.7 2.0 %filter.1 = (bf16[80,128]{1,0:T(8,128)(2,1)S(1)}, bf16[80,128]{1,0:T(8,128)(2,1)S(1)}, f32[8,128]{1,0:T(8,128)S(4)}, s32[8,128]{1,0:T(8,128)S(4)}) custom-call(f32[1]{0:T(128)S(6)} %copy.6.width, s32[2,32]{1,0:T(2,128)} %bitcast.17, f32[16,8,128]{2,1,0:T(8,128)} %constant.4.clone.trig_table, s32[16,8,128]{2,1,0:T(8,128)} %constant.5.clone.code_table, ...), custom_call_target="tpu_custom_call" | custom-call | tf_op jit(solution)/shard_map/filter/pallas_call | solution.py:360
  2.7 4.1 %collective-permute-start.1 = (bf16[80,128]{1,0:T(8,128)(2,1)S(1)}, bf16[80,128]{1,0:T(8,128)(2,1)S(1)}, u32[]{:S(2)}, u32[]{:S(2)}) collective-permute-start(bf16[80,128]{1,0:T(8,128)(2,1)S(1)} %get-tuple-element.23), channel_id=1, source_target_pairs={{0,8},{1,9},{2,10},{3,11},{4,12},{5,13},{6,14},{7,15},{8,0},{9,1},... | collective-permute-start | bytes 61448 | tf_op jit(solution)/shard_map/ppermute | solution.py:418
  6.8 1.3 %collective-permute-start.2 = (bf16[80,128]{1,0:T(8,128)(2,1)S(1)}, bf16[80,128]{1,0:T(8,128)(2,1)S(1)}, u32[]{:S(2)}, u32[]{:S(2)}) collective-permute-start(bf16[80,128]{1,0:T(8,128)(2,1)S(1)} %get-tuple-element.24), channel_id=1, source_target_pairs={{0,9},{1,8},{2,11},{3,10},{4,13},{5,12},{6,15},{7,14},{8,1},{9,0},... | collective-permute-start | bytes 61448 | tf_op jit(solution)/shard_map/ppermute | solution.py:418
  8.1 0.3 %collective-permute-start = (bf16[80,128]{1,0:T(8,128)(2,1)S(1)}, bf16[80,128]{1,0:T(8,128)(2,1)S(1)}, u32[]{:S(2)}, u32[]{:S(2)}) collective-permute-start(bf16[80,128]{1,0:T(8,128)(2,1)S(1)} %get-tuple-element.24), channel_id=1, source_target_pairs={{0,1},{1,0},{2,3},{3,2},{4,5},{5,4},{6,7},{7,6},{8,9},{9,8},{10,11... | collective-permute-start | bytes 61448 | tf_op jit(solution)/shard_map/ppermute | solution.py:418
  8.3 1.1 %hats.2.refs_1_.refs_4_ = bf16[8,1024,256]{2,1,0:T(8,128)(2,1)S(1)} custom-call(f32[8,128]{1,0:T(8,128)S(4)} %get-tuple-element.33.trig, s32[8,128]{1,0:T(8,128)S(4)} %get-tuple-element.34.codes), custom_call_target="tpu_custom_call" | custom-call | flops 33554432 | tf_op jit(solution)/shard_map/hats/pallas_call | solution.py:390
  9.5 0.0 collective-permute-done.1
  9.5 2.9 %collective-permute-done.2 = bf16[80,128]{1,0:T(8,128)(2,1)S(1)} collective-permute-done((bf16[80,128]{1,0:T(8,128)(2,1)S(1)}, bf16[80,128]{1,0:T(8,128)(2,1)S(1)}, u32[]{:S(2)}, u32[]{:S(2)}) %collective-permute-start.2) | collective-permute-done | bytes 20512 | tf_op jit(solution)/shard_map/ppermute | solution.py:418
  12.4 0.0 collective-permute-done
  12.4 2.6 %collective-permute-start.5 = (bf16[2,144,128]{2,1,0:T(8,128)(2,1)S(1)}, bf16[2,144,128]{2,1,0:T(8,128)(2,1)S(1)}, u32[]{:S(2)}, u32[]{:S(2)}) collective-permute-start(bf16[2,144,128]{2,1,0:T(8,128)(2,1)S(1)} %pad_maximum_fusion.3.refs_0_), channel_id=1, source_target_pairs={{0,6},{2,4},{4,2},{6,0},{8,14},{10,12},{12,10},{14,8},{1,7},{3,5},... | collective-permute-start | bytes 221192 | tf_op jit(solution)/shard_map/ppermute | solution.py:294
  15.0 0.5 %collective-permute-start.4 = (bf16[2,144,128]{2,1,0:T(8,128)(2,1)S(1)}, bf16[2,144,128]{2,1,0:T(8,128)(2,1)S(1)}, u32[]{:S(2)}, u32[]{:S(2)}) collective-permute-start(bf16[2,144,128]{2,1,0:T(8,128)(2,1)S(1)} %pad_maximum_fusion.3.refs_0_), channel_id=1, source_target_pairs={{0,2},{2,0},{4,6},{6,4},{8,10},{10,8},{12,14},{14,12},{1,3},{3,1},... | collective-permute-start | bytes 221192 | tf_op jit(solution)/shard_map/ppermute | solution.py:294
  15.5 0.4 %collective-permute-start.3 = (bf16[2,144,128]{2,1,0:T(8,128)(2,1)S(1)}, bf16[2,144,128]{2,1,0:T(8,128)(2,1)S(1)}, u32[]{:S(2)}, u32[]{:S(2)}) collective-permute-start(bf16[2,144,128]{2,1,0:T(8,128)(2,1)S(1)} %pad_maximum_fusion.3.refs_0_), channel_id=1, source_target_pairs={{0,4},{2,6},{4,0},{6,2},{8,12},{10,14},{12,8},{14,10},{1,5},{3,7},... | collective-permute-start | bytes 221192 | tf_op jit(solution)/shard_map/ppermute | solution.py:294
  16.0 1.2 %hats.3.refs_2_.refs_5_ = bf16[8,1024,256]{2,1,0:T(8,128)(2,1)S(1)} custom-call(f32[8,128]{1,0:T(8,128)S(4)} %get-tuple-element.33.trig, s32[8,128]{1,0:T(8,128)S(4)} %get-tuple-element.34.codes), custom_call_target="tpu_custom_call" | custom-call | flops 33554432 | tf_op jit(solution)/shard_map/hats/pallas_call | solution.py:390
  17.1 1.3 %collective-permute-done.5.refs_2_ = bf16[2,144,128]{2,1,0:T(8,128)(2,1)S(1)} collective-permute-done((bf16[2,144,128]{2,1,0:T(8,128)(2,1)S(1)}, bf16[2,144,128]{2,1,0:T(8,128)(2,1)S(1)}, u32[]{:S(2)}, u32[]{:S(2)}) %collective-permute-start.5) | collective-permute-done | bytes 73760 | tf_op jit(solution)/shard_map/ppermute | solution.py:294
  18.5 0.1 collective-permute-start.7
  18.6 0.5 %project.3.refs_6_ = f32[8,32,256]{2,1,0:T(8,128)S(1)} custom-call(s32[8,128]{1,0:T(8,128)S(4)} %get-tuple-element.34.codes, bf16[2,144,128]{2,1,0:T(8,128)(2,1)S(1)} %pad_maximum_fusion.3.refs_0_, bf16[8,1024,256]{2,1,0:T(8,128)(2,1)S(1)} %hats.2.refs_1_.refs_4_, bf16[8,1024,256]{2,1,0:T(8,128)(2,1)S(1)} %hats.3.refs_2_.refs_5_), custom_call_target="tpu_custom_call" | custom-call | flops 2147483648 | tf_op jit(solution)/shard_map/project/pallas_call | solution.py:442
  19.0 0.3 %collective-permute-done.4.refs_1_ = bf16[2,144,128]{2,1,0:T(8,128)(2,1)S(1)} collective-permute-done((bf16[2,144,128]{2,1,0:T(8,128)(2,1)S(1)}, bf16[2,144,128]{2,1,0:T(8,128)(2,1)S(1)}, u32[]{:S(2)}, u32[]{:S(2)}) %collective-permute-start.4) | collective-permute-done | bytes 73760 | tf_op jit(solution)/shard_map/ppermute | solution.py:294
  19.3 0.5 %collective-permute-done.3.refs_0_ = bf16[2,144,128]{2,1,0:T(8,128)(2,1)S(1)} collective-permute-done((bf16[2,144,128]{2,1,0:T(8,128)(2,1)S(1)}, bf16[2,144,128]{2,1,0:T(8,128)(2,1)S(1)}, u32[]{:S(2)}, u32[]{:S(2)}) %collective-permute-start.3) | collective-permute-done | bytes 73760 | tf_op jit(solution)/shard_map/ppermute | solution.py:294
  19.9 0.1 collective-permute-start.6
  20.0 0.0 collective-permute-done.7.refs_3_
  20.0 1.4 %project.4.refs_3_ = f32[8,32,256]{2,1,0:T(8,128)S(1)} custom-call(s32[8,128]{1,0:T(8,128)S(4)} %get-tuple-element.34.codes, bf16[2,144,128]{2,1,0:T(8,128)(2,1)S(1)} %collective-permute-done.3.refs_0_, bf16[2,144,128]{2,1,0:T(8,128)(2,1)S(1)} %collective-permute-done.4.refs_1_, bf16[2,144,128]{2,1,0:T(8,128)(2,1)S(1)} %collective-permute-done.5.refs_2_, ...), custom_call_target="tpu_custom_call" | custom-call | flops 2147483648 | tf_op jit(solution)/shard_map/project/pallas_call | solution.py:442
  21.4 0.0 collective-permute-done.6.refs_0_
  21.4 1.6 %project.5 = f32[1,32,2048]{2,1,0:T(8,128)} custom-call(s32[8,128]{1,0:T(8,128)S(4)} %get-tuple-element.34.codes, bf16[4,144,128]{2,1,0:T(8,128)(2,1)S(1)} %collective-permute-done.6.refs_0_, bf16[8,1024,256]{2,1,0:T(8,128)(2,1)S(1)} %hats.2.refs_1_.refs_4_, bf16[8,1024,256]{2,1,0:T(8,128)(2,1)S(1)} %hats.3.refs_2_.refs_5_, f32[8,32,256]{2,1,0:T(8,128)S(1)} %project.4.refs_3_), custom_call_target="tpu_custom_call" | custom-call | flops 2147483648 | tf_op jit(solution)/shard_map/project/pallas_call | solution.py:442
  (6 shorter events, 0.1 us)
Async XLA Ops:
  2.7 6.8 %collective-permute-start.1 = (bf16[80,128]{1,0:T(8,128)(2,1)S(1)}, bf16[80,128]{1,0:T(8,128)(2,1)S(1)}, u32[]{:S(2)}, u32[]{:S(2)}) collective-permute-start(bf16[80,128]{1,0:T(8,128)(2,1)S(1)} %get-tuple-element.23), channel_id=1, source_target_pairs={{0,8},{1,9},{2,10},{3,11},{4,12},{5,13},{6,14},{7,15},{8,0},{9,1},... | collective-permute-start | bytes 61448 | tf_op jit(solution)/shard_map/ppermute | solution.py:418
  6.8 5.6 %collective-permute-start.2 = (bf16[80,128]{1,0:T(8,128)(2,1)S(1)}, bf16[80,128]{1,0:T(8,128)(2,1)S(1)}, u32[]{:S(2)}, u32[]{:S(2)}) collective-permute-start(bf16[80,128]{1,0:T(8,128)(2,1)S(1)} %get-tuple-element.24), channel_id=1, source_target_pairs={{0,9},{1,8},{2,11},{3,10},{4,13},{5,12},{6,15},{7,14},{8,1},{9,0},... | collective-permute-start | bytes 61448 | tf_op jit(solution)/shard_map/ppermute | solution.py:418
  8.1 4.3 %collective-permute-start = (bf16[80,128]{1,0:T(8,128)(2,1)S(1)}, bf16[80,128]{1,0:T(8,128)(2,1)S(1)}, u32[]{:S(2)}, u32[]{:S(2)}) collective-permute-start(bf16[80,128]{1,0:T(8,128)(2,1)S(1)} %get-tuple-element.24), channel_id=1, source_target_pairs={{0,1},{1,0},{2,3},{3,2},{4,5},{5,4},{6,7},{7,6},{8,9},{9,8},{10,11... | collective-permute-start | bytes 61448 | tf_op jit(solution)/shard_map/ppermute | solution.py:418
  12.4 6.0 %collective-permute-start.5 = (bf16[2,144,128]{2,1,0:T(8,128)(2,1)S(1)}, bf16[2,144,128]{2,1,0:T(8,128)(2,1)S(1)}, u32[]{:S(2)}, u32[]{:S(2)}) collective-permute-start(bf16[2,144,128]{2,1,0:T(8,128)(2,1)S(1)} %pad_maximum_fusion.3.refs_0_), channel_id=1, source_target_pairs={{0,6},{2,4},{4,2},{6,0},{8,14},{10,12},{12,10},{14,8},{1,7},{3,5},... | collective-permute-start | bytes 221192 | tf_op jit(solution)/shard_map/ppermute | solution.py:294
  15.0 4.4 %collective-permute-start.4 = (bf16[2,144,128]{2,1,0:T(8,128)(2,1)S(1)}, bf16[2,144,128]{2,1,0:T(8,128)(2,1)S(1)}, u32[]{:S(2)}, u32[]{:S(2)}) collective-permute-start(bf16[2,144,128]{2,1,0:T(8,128)(2,1)S(1)} %pad_maximum_fusion.3.refs_0_), channel_id=1, source_target_pairs={{0,2},{2,0},{4,6},{6,4},{8,10},{10,8},{12,14},{14,12},{1,3},{3,1},... | collective-permute-start | bytes 221192 | tf_op jit(solution)/shard_map/ppermute | solution.py:294
  15.5 4.4 %collective-permute-start.3 = (bf16[2,144,128]{2,1,0:T(8,128)(2,1)S(1)}, bf16[2,144,128]{2,1,0:T(8,128)(2,1)S(1)}, u32[]{:S(2)}, u32[]{:S(2)}) collective-permute-start(bf16[2,144,128]{2,1,0:T(8,128)(2,1)S(1)} %pad_maximum_fusion.3.refs_0_), channel_id=1, source_target_pairs={{0,4},{2,6},{4,0},{6,2},{8,12},{10,14},{12,8},{14,10},{1,5},{3,7},... | collective-permute-start | bytes 221192 | tf_op jit(solution)/shard_map/ppermute | solution.py:294
  18.5 1.5 %collective-permute-start.7 = (bf16[4,144,128]{2,1,0:T(8,128)(2,1)S(1)}, bf16[4,144,128]{2,1,0:T(8,128)(2,1)S(1)}, u32[]{:S(2)}, u32[]{:S(2)}) collective-permute-start(bf16[4,144,128]{2,1,0:T(8,128)(2,1)S(1)} %pad_maximum_fusion.1), channel_id=1, source_target_pairs={{0,16},{16,0},{1,17},{17,1},{2,18},{18,2},{3,19},{19,3},{4,20},{20... | collective-permute-start | bytes 442376 | tf_op jit(solution)/shard_map/ppermute | solution.py:290
  19.9 1.5 %collective-permute-start.6 = (bf16[4,144,128]{2,1,0:T(8,128)(2,1)S(1)}, bf16[4,144,128]{2,1,0:T(8,128)(2,1)S(1)}, u32[]{:S(2)}, u32[]{:S(2)}) collective-permute-start(bf16[4,144,128]{2,1,0:T(8,128)(2,1)S(1)} %pad_maximum_fusion), channel_id=1, source_target_pairs={{0,16},{16,0},{1,17},{17,1},{2,18},{18,2},{3,19},{19,3},{4,20},{20... | collective-permute-start | bytes 442376 | tf_op jit(solution)/shard_map/ppermute | solution.py:290

commit v12 on v9

--- a/solution.py
+++ b/solution.py
@@ -71,8 +71,8 @@
     place = lax.axis_index("segment") * lax.axis_size("angle") + lax.axis_index("angle")
     sources = [(rows_ref.at[i], padded.at[i, :, pl.ds(ahead, bins)]) for i in range(local)]
     sources = [
+        (blocks_ref, blocks),
         *sources,
-        (blocks_ref, blocks),
         (trig_table.at[place], trig),
         (code_table.at[place], codes),
     ]
@@ -102,7 +102,7 @@
     )
     paganin = split(paganin)
 
-    for copy in copies:
+    for copy in copies[: local + 1]:
         copy.wait()
     first = place * local
     mine = lax.axis_index("tile")
@@ -139,6 +139,8 @@
                 part = jnp.concatenate([part, rest], axis=0)
             at = j * rows_of_block
             outputs[turn][at : at + part.shape[0], :] = part.astype(jnp.bfloat16)
+    for copy in copies[local + 1 :]:
+        copy.wait()
 
 
 def pack(value, groups):

time: 23.1 us -> 23.2 us (level)
  no operation moved by 1% of the time
where the time goes in v12:
time: 23.2 us; the launch traced here: 23.1 us
  starting transfers between devices  9.27 us (40%)
  Pallas kernels  7.93 us (34%)
  waiting for transfers between devices  5.11 us (22%)
  between operations  0.74 us (3%)
    ppermute x3, starting transfers between devices, joint(): return lax.ppermute(cut[turn], ('angle', 'tile'), pairs)  5.64 us
    ppermute x3, starting transfers between devices, swapped(): lax.ppermute(value, axis, [(i, i ^ by) for i in range(lax.axis_size(axis))])  3.55 us
    pallas_call x3, Pallas kernels, project(): pl.pallas_call(functools.partial(project_kernel, (parts, sources, len(win...  3.46 us
    ppermute x3, waiting for transfers between devices, joint(): return lax.ppermute(cut[turn], ('angle', 'tile'), pairs)  2.88 us
    pallas_call x2, Pallas kernels, hats_of(): pl.pallas_call(functools.partial(hat_kernel, (part, half, tile_rows, angl...  2.3 us
    pallas_call x1, Pallas kernels, body(): pl.pallas_call(functools.partial(filter_kernel, (tiles, outs, first_bin,...  2.17 us
    ppermute x3, waiting for transfers between devices, swapped(): lax.ppermute(value, axis, [(i, i ^ by) for i in range(lax.axis_size(axis))])  2.05 us
  transfers between devices with their start and end apart: 9, of which 5 were waited for; matrix products, arithmetic and copies ran while one was open for 0% of the time, Pallas kernels for 18%

profile of v12, /device:TPU:0, one launch (start us, length us, event | category | flops | bytes accessed | tf_op | source)
XLA Modules:
  0.0 23.1 jit_solution(16342226506547808067)
XLA Ops:
  0.7 2.2 %filter.1 = (bf16[80,128]{1,0:T(8,128)(2,1)S(1)}, bf16[80,128]{1,0:T(8,128)(2,1)S(1)}, f32[8,128]{1,0:T(8,128)S(4)}, s32[8,128]{1,0:T(8,128)S(4)}) custom-call(f32[1]{0:T(128)S(6)} %copy.6.width, s32[2,32]{1,0:T(2,128)} %bitcast.17, f32[16,8,128]{2,1,0:T(8,128)} %constant.4.clone.trig_table, s32[16,8,128]{2,1,0:T(8,128)} %constant.5.clone.code_table, ...), custom_call_target="tpu_custom_call" | custom-call | tf_op jit(solution)/shard_map/filter/pallas_call | solution.py:362
  2.8 4.1 %collective-permute-start.1 = (bf16[80,128]{1,0:T(8,128)(2,1)S(1)}, bf16[80,128]{1,0:T(8,128)(2,1)S(1)}, u32[]{:S(2)}, u32[]{:S(2)}) collective-permute-start(bf16[80,128]{1,0:T(8,128)(2,1)S(1)} %get-tuple-element.24), channel_id=1, source_target_pairs={{0,8},{1,9},{2,10},{3,11},{4,12},{5,13},{6,14},{7,15},{8,0},{9,1},... | collective-permute-start | bytes 61448 | tf_op jit(solution)/shard_map/ppermute | solution.py:420
  6.9 1.3 %collective-permute-start.2 = (bf16[80,128]{1,0:T(8,128)(2,1)S(1)}, bf16[80,128]{1,0:T(8,128)(2,1)S(1)}, u32[]{:S(2)}, u32[]{:S(2)}) collective-permute-start(bf16[80,128]{1,0:T(8,128)(2,1)S(1)} %get-tuple-element.25), channel_id=1, source_target_pairs={{0,9},{1,8},{2,11},{3,10},{4,13},{5,12},{6,15},{7,14},{8,1},{9,0},... | collective-permute-start | bytes 61448 | tf_op jit(solution)/shard_map/ppermute | solution.py:420
  8.2 0.3 %collective-permute-start = (bf16[80,128]{1,0:T(8,128)(2,1)S(1)}, bf16[80,128]{1,0:T(8,128)(2,1)S(1)}, u32[]{:S(2)}, u32[]{:S(2)}) collective-permute-start(bf16[80,128]{1,0:T(8,128)(2,1)S(1)} %get-tuple-element.25), channel_id=1, source_target_pairs={{0,1},{1,0},{2,3},{3,2},{4,5},{5,4},{6,7},{7,6},{8,9},{9,8},{10,11... | collective-permute-start | bytes 61448 | tf_op jit(solution)/shard_map/ppermute | solution.py:420
  8.5 1.1 %hats.2.refs_2_.refs_4_.refs_1_ = bf16[8,1024,256]{2,1,0:T(8,128)(2,1)S(1)} custom-call(f32[8,128]{1,0:T(8,128)S(4)} %get-tuple-element.35.trig, s32[8,128]{1,0:T(8,128)S(4)} %get-tuple-element.36.codes), custom_call_target="tpu_custom_call" | custom-call | flops 33554432 | tf_op jit(solution)/shard_map/hats/pallas_call | solution.py:392
  9.6 0.0 collective-permute-done.1
  9.6 2.9 %collective-permute-done.2 = bf16[80,128]{1,0:T(8,128)(2,1)S(1)} collective-permute-done((bf16[80,128]{1,0:T(8,128)(2,1)S(1)}, bf16[80,128]{1,0:T(8,128)(2,1)S(1)}, u32[]{:S(2)}, u32[]{:S(2)}) %collective-permute-start.2) | collective-permute-done | bytes 20512 | tf_op jit(solution)/shard_map/ppermute | solution.py:420
  12.5 0.0 collective-permute-done
  12.6 2.6 %collective-permute-start.6 = (bf16[2,144,128]{2,1,0:T(8,128)(2,1)S(1)}, bf16[2,144,128]{2,1,0:T(8,128)(2,1)S(1)}, u32[]{:S(2)}, u32[]{:S(2)}) collective-permute-start(bf16[2,144,128]{2,1,0:T(8,128)(2,1)S(1)} %pad_maximum_fusion.2.refs_0_), channel_id=1, source_target_pairs={{0,6},{2,4},{4,2},{6,0},{8,14},{10,12},{12,10},{14,8},{1,7},{3,5},... | collective-permute-start | bytes 221192 | tf_op jit(solution)/shard_map/ppermute | solution.py:296
  15.1 0.0 collective-permute-start.5
  15.1 0.5 %collective-permute-start.4 = (bf16[2,144,128]{2,1,0:T(8,128)(2,1)S(1)}, bf16[2,144,128]{2,1,0:T(8,128)(2,1)S(1)}, u32[]{:S(2)}, u32[]{:S(2)}) collective-permute-start(bf16[2,144,128]{2,1,0:T(8,128)(2,1)S(1)} %pad_maximum_fusion.2.refs_0_), channel_id=1, source_target_pairs={{0,2},{2,0},{4,6},{6,4},{8,10},{10,8},{12,14},{14,12},{1,3},{3,1},... | collective-permute-start | bytes 221192 | tf_op jit(solution)/shard_map/ppermute | solution.py:296
  15.7 0.5 %collective-permute-start.3 = (bf16[2,144,128]{2,1,0:T(8,128)(2,1)S(1)}, bf16[2,144,128]{2,1,0:T(8,128)(2,1)S(1)}, u32[]{:S(2)}, u32[]{:S(2)}) collective-permute-start(bf16[2,144,128]{2,1,0:T(8,128)(2,1)S(1)} %pad_maximum_fusion.2.refs_0_), channel_id=1, source_target_pairs={{0,4},{2,6},{4,0},{6,2},{8,12},{10,14},{12,8},{14,10},{1,5},{3,7},... | collective-permute-start | bytes 221192 | tf_op jit(solution)/shard_map/ppermute | solution.py:296
  16.1 1.2 %hats.3.refs_3_.refs_5_.refs_2_ = bf16[8,1024,256]{2,1,0:T(8,128)(2,1)S(1)} custom-call(f32[8,128]{1,0:T(8,128)S(4)} %get-tuple-element.35.trig, s32[8,128]{1,0:T(8,128)S(4)} %get-tuple-element.36.codes), custom_call_target="tpu_custom_call" | custom-call | flops 33554432 | tf_op jit(solution)/shard_map/hats/pallas_call | solution.py:392
  17.3 0.6 %collective-permute-done.6.refs_2_ = bf16[2,144,128]{2,1,0:T(8,128)(2,1)S(1)} collective-permute-done((bf16[2,144,128]{2,1,0:T(8,128)(2,1)S(1)}, bf16[2,144,128]{2,1,0:T(8,128)(2,1)S(1)}, u32[]{:S(2)}, u32[]{:S(2)}) %collective-permute-start.6) | collective-permute-done | bytes 73760 | tf_op jit(solution)/shard_map/ppermute | solution.py:296
  17.9 0.0 collective-permute-done.5.refs_1_
  17.9 0.0 collective-permute-start.8
  17.9 0.7 %project.3.refs_6_ = f32[8,32,256]{2,1,0:T(8,128)S(1)} custom-call(s32[8,128]{1,0:T(8,128)S(4)} %get-tuple-element.36.codes, bf16[2,144,128]{2,1,0:T(8,128)(2,1)S(1)} %pad_maximum_fusion.2.refs_0_, bf16[2,144,128]{2,1,0:T(8,128)(2,1)S(1)} %collective-permute-done.5.refs_1_, bf16[8,1024,256]{2,1,0:T(8,128)(2,1)S(1)} %hats.2.refs_2_.refs_4_.refs_1_, ...), custom_call_target="tpu_custom_call" | custom-call | flops 2147483648 | tf_op jit(solution)/shard_map/project/pallas_call | solution.py:444
  18.6 1.2 %collective-permute-done.4.refs_1_ = bf16[2,144,128]{2,1,0:T(8,128)(2,1)S(1)} collective-permute-done((bf16[2,144,128]{2,1,0:T(8,128)(2,1)S(1)}, bf16[2,144,128]{2,1,0:T(8,128)(2,1)S(1)}, u32[]{:S(2)}, u32[]{:S(2)}) %collective-permute-start.4) | collective-permute-done | bytes 73760 | tf_op jit(solution)/shard_map/ppermute | solution.py:296
  19.8 0.3 %collective-permute-done.3.refs_0_ = bf16[2,144,128]{2,1,0:T(8,128)(2,1)S(1)} collective-permute-done((bf16[2,144,128]{2,1,0:T(8,128)(2,1)S(1)}, bf16[2,144,128]{2,1,0:T(8,128)(2,1)S(1)}, u32[]{:S(2)}, u32[]{:S(2)}) %collective-permute-start.3) | collective-permute-done | bytes 73760 | tf_op jit(solution)/shard_map/ppermute | solution.py:296
  20.1 0.1 collective-permute-start.7
  20.2 0.0 collective-permute-done.8.refs_3_
  20.2 1.2 %project.4.refs_3_ = f32[8,32,256]{2,1,0:T(8,128)S(1)} custom-call(s32[8,128]{1,0:T(8,128)S(4)} %get-tuple-element.36.codes, bf16[2,144,128]{2,1,0:T(8,128)(2,1)S(1)} %collective-permute-done.3.refs_0_, bf16[2,144,128]{2,1,0:T(8,128)(2,1)S(1)} %collective-permute-done.4.refs_1_, bf16[2,144,128]{2,1,0:T(8,128)(2,1)S(1)} %collective-permute-done.6.refs_2_, ...), custom_call_target="tpu_custom_call" | custom-call | flops 2147483648 | tf_op jit(solution)/shard_map/project/pallas_call | solution.py:444
  21.4 0.2 collective-permute-done.7.refs_0_
  21.5 1.6 %project.5 = f32[1,32,2048]{2,1,0:T(8,128)} custom-call(s32[8,128]{1,0:T(8,128)S(4)} %get-tuple-element.36.codes, bf16[4,144,128]{2,1,0:T(8,128)(2,1)S(1)} %collective-permute-done.7.refs_0_, bf16[8,1024,256]{2,1,0:T(8,128)(2,1)S(1)} %hats.2.refs_2_.refs_4_.refs_1_, bf16[8,1024,256]{2,1,0:T(8,128)(2,1)S(1)} %hats.3.refs_3_.refs_5_.refs_2_, ...), custom_call_target="tpu_custom_call" | custom-call | flops 2147483648 | tf_op jit(solution)/shard_map/project/pallas_call | solution.py:444
  (5 shorter events, 0.0 us)
Async XLA Ops:
  2.8 6.8 %collective-permute-start.1 = (bf16[80,128]{1,0:T(8,128)(2,1)S(1)}, bf16[80,128]{1,0:T(8,128)(2,1)S(1)}, u32[]{:S(2)}, u32[]{:S(2)}) collective-permute-start(bf16[80,128]{1,0:T(8,128)(2,1)S(1)} %get-tuple-element.24), channel_id=1, source_target_pairs={{0,8},{1,9},{2,10},{3,11},{4,12},{5,13},{6,14},{7,15},{8,0},{9,1},... | collective-permute-start | bytes 61448 | tf_op jit(solution)/shard_map/ppermute | solution.py:420
  6.9 5.6 %collective-permute-start.2 = (bf16[80,128]{1,0:T(8,128)(2,1)S(1)}, bf16[80,128]{1,0:T(8,128)(2,1)S(1)}, u32[]{:S(2)}, u32[]{:S(2)}) collective-permute-start(bf16[80,128]{1,0:T(8,128)(2,1)S(1)} %get-tuple-element.25), channel_id=1, source_target_pairs={{0,9},{1,8},{2,11},{3,10},{4,13},{5,12},{6,15},{7,14},{8,1},{9,0},... | collective-permute-start | bytes 61448 | tf_op jit(solution)/shard_map/ppermute | solution.py:420
  8.2 4.3 %collective-permute-start = (bf16[80,128]{1,0:T(8,128)(2,1)S(1)}, bf16[80,128]{1,0:T(8,128)(2,1)S(1)}, u32[]{:S(2)}, u32[]{:S(2)}) collective-permute-start(bf16[80,128]{1,0:T(8,128)(2,1)S(1)} %get-tuple-element.25), channel_id=1, source_target_pairs={{0,1},{1,0},{2,3},{3,2},{4,5},{5,4},{6,7},{7,6},{8,9},{9,8},{10,11... | collective-permute-start | bytes 61448 | tf_op jit(solution)/shard_map/ppermute | solution.py:420
  12.6 5.3 %collective-permute-start.6 = (bf16[2,144,128]{2,1,0:T(8,128)(2,1)S(1)}, bf16[2,144,128]{2,1,0:T(8,128)(2,1)S(1)}, u32[]{:S(2)}, u32[]{:S(2)}) collective-permute-start(bf16[2,144,128]{2,1,0:T(8,128)(2,1)S(1)} %pad_maximum_fusion.2.refs_0_), channel_id=1, source_target_pairs={{0,6},{2,4},{4,2},{6,0},{8,14},{10,12},{12,10},{14,8},{1,7},{3,5},... | collective-permute-start | bytes 221192 | tf_op jit(solution)/shard_map/ppermute | solution.py:296
  15.1 2.8 %collective-permute-start.5 = (bf16[2,144,128]{2,1,0:T(8,128)(2,1)S(1)}, bf16[2,144,128]{2,1,0:T(8,128)(2,1)S(1)}, u32[]{:S(2)}, u32[]{:S(2)}) collective-permute-start(bf16[2,144,128]{2,1,0:T(8,128)(2,1)S(1)} %pad_maximum_fusion.2.refs_0_), channel_id=1, source_target_pairs={{0,16},{16,0},{1,17},{17,1},{2,18},{18,2},{3,19},{19,3},{4,20},{20... | collective-permute-start | bytes 221192 | tf_op jit(solution)/shard_map/ppermute | solution.py:292
  15.1 4.7 %collective-permute-start.4 = (bf16[2,144,128]{2,1,0:T(8,128)(2,1)S(1)}, bf16[2,144,128]{2,1,0:T(8,128)(2,1)S(1)}, u32[]{:S(2)}, u32[]{:S(2)}) collective-permute-start(bf16[2,144,128]{2,1,0:T(8,128)(2,1)S(1)} %pad_maximum_fusion.2.refs_0_), channel_id=1, source_target_pairs={{0,2},{2,0},{4,6},{6,4},{8,10},{10,8},{12,14},{14,12},{1,3},{3,1},... | collective-permute-start | bytes 221192 | tf_op jit(solution)/shard_map/ppermute | solution.py:296
  15.7 4.4 %collective-permute-start.3 = (bf16[2,144,128]{2,1,0:T(8,128)(2,1)S(1)}, bf16[2,144,128]{2,1,0:T(8,128)(2,1)S(1)}, u32[]{:S(2)}, u32[]{:S(2)}) collective-permute-start(bf16[2,144,128]{2,1,0:T(8,128)(2,1)S(1)} %pad_maximum_fusion.2.refs_0_), channel_id=1, source_target_pairs={{0,4},{2,6},{4,0},{6,2},{8,12},{10,14},{12,8},{14,10},{1,5},{3,7},... | collective-permute-start | bytes 221192 | tf_op jit(solution)/shard_map/ppermute | solution.py:296
  17.9 2.3 %collective-permute-start.8 = (bf16[2,144,128]{2,1,0:T(8,128)(2,1)S(1)}, bf16[2,144,128]{2,1,0:T(8,128)(2,1)S(1)}, u32[]{:S(2)}, u32[]{:S(2)}) collective-permute-start(bf16[2,144,128]{2,1,0:T(8,128)(2,1)S(1)} %collective-permute-done.6.refs_2_), channel_id=1, source_target_pairs={{0,16},{16,0},{1,17},{17,1},{2,18},{18,2},{3,19},{19,3},{4,20},{20... | collective-permute-start | bytes 221192 | tf_op jit(solution)/shard_map/ppermute | solution.py:292
  20.1 1.4 %collective-permute-start.7 = (bf16[4,144,128]{2,1,0:T(8,128)(2,1)S(1)}, bf16[4,144,128]{2,1,0:T(8,128)(2,1)S(1)}, u32[]{:S(2)}, u32[]{:S(2)}) collective-permute-start(bf16[4,144,128]{2,1,0:T(8,128)(2,1)S(1)} %pad_maximum_fusion), channel_id=1, source_target_pairs={{0,16},{16,0},{1,17},{17,1},{2,18},{18,2},{3,19},{19,3},{4,20},{20... | collective-permute-start | bytes 442376 | tf_op jit(solution)/shard_map/ppermute | solution.py:292

commit v13 on v12

--- a/solution.py
+++ b/solution.py
@@ -71,8 +71,8 @@
     place = lax.axis_index("segment") * lax.axis_size("angle") + lax.axis_index("angle")
     sources = [(rows_ref.at[i], padded.at[i, :, pl.ds(ahead, bins)]) for i in range(local)]
     sources = [
+        *sources,
         (blocks_ref, blocks),
-        *sources,
         (trig_table.at[place], trig),
         (code_table.at[place], codes),
     ]

time: 23.2 us -> 23.1 us (level)
  no operation moved by 1% of the time
where the time goes in v13:
time: 23.1 us; the launch traced here: 22.9 us
  starting transfers between devices  9.27 us (40%)
  Pallas kernels  7.76 us (34%)
  waiting for transfers between devices  5.12 us (22%)
  between operations  0.74 us (3%)
    ppermute x3, starting transfers between devices, joint(): return lax.ppermute(cut[turn], ('angle', 'tile'), pairs)  5.64 us
    ppermute x3, starting transfers between devices, swapped(): lax.ppermute(value, axis, [(i, i ^ by) for i in range(lax.axis_size(axis))])  3.55 us
    pallas_call x3, Pallas kernels, project(): pl.pallas_call(functools.partial(project_kernel, (parts, sources, len(win...  3.45 us
    ppermute x3, waiting for transfers between devices, joint(): return lax.ppermute(cut[turn], ('angle', 'tile'), pairs)  2.88 us
    pallas_call x2, Pallas kernels, hats_of(): pl.pallas_call(functools.partial(hat_kernel, (part, half, tile_rows, angl...  2.3 us
    ppermute x3, waiting for transfers between devices, swapped(): lax.ppermute(value, axis, [(i, i ^ by) for i in range(lax.axis_size(axis))])  2.06 us
    pallas_call x1, Pallas kernels, body(): pl.pallas_call(functools.partial(filter_kernel, (tiles, outs, first_bin,...  2.01 us
  transfers between devices with their start and end apart: 9, of which 5 were waited for; matrix products, arithmetic and copies ran while one was open for 0% of the time, Pallas kernels for 18%

profile of v13, /device:TPU:0, one launch (start us, length us, event | category | flops | bytes accessed | tf_op | source)
XLA Modules:
  0.0 22.9 jit_solution(2054540598870585890)
XLA Ops:
  0.7 2.0 %filter.1 = (bf16[80,128]{1,0:T(8,128)(2,1)S(1)}, bf16[80,128]{1,0:T(8,128)(2,1)S(1)}, f32[8,128]{1,0:T(8,128)S(4)}, s32[8,128]{1,0:T(8,128)S(4)}) custom-call(f32[1]{0:T(128)S(6)} %copy.6.width, s32[2,32]{1,0:T(2,128)} %bitcast.17, f32[16,8,128]{2,1,0:T(8,128)} %constant.4.clone.trig_table, s32[16,8,128]{2,1,0:T(8,128)} %constant.5.clone.code_table, ...), custom_call_target="tpu_custom_call" | custom-call | tf_op jit(solution)/shard_map/filter/pallas_call | solution.py:362
  2.7 4.1 %collective-permute-start.1 = (bf16[80,128]{1,0:T(8,128)(2,1)S(1)}, bf16[80,128]{1,0:T(8,128)(2,1)S(1)}, u32[]{:S(2)}, u32[]{:S(2)}) collective-permute-start(bf16[80,128]{1,0:T(8,128)(2,1)S(1)} %get-tuple-element.24), channel_id=1, source_target_pairs={{0,8},{1,9},{2,10},{3,11},{4,12},{5,13},{6,14},{7,15},{8,0},{9,1},... | collective-permute-start | bytes 61448 | tf_op jit(solution)/shard_map/ppermute | solution.py:420
  6.8 1.3 %collective-permute-start.2 = (bf16[80,128]{1,0:T(8,128)(2,1)S(1)}, bf16[80,128]{1,0:T(8,128)(2,1)S(1)}, u32[]{:S(2)}, u32[]{:S(2)}) collective-permute-start(bf16[80,128]{1,0:T(8,128)(2,1)S(1)} %get-tuple-element.25), channel_id=1, source_target_pairs={{0,9},{1,8},{2,11},{3,10},{4,13},{5,12},{6,15},{7,14},{8,1},{9,0},... | collective-permute-start | bytes 61448 | tf_op jit(solution)/shard_map/ppermute | solution.py:420
  8.1 0.2 %collective-permute-start = (bf16[80,128]{1,0:T(8,128)(2,1)S(1)}, bf16[80,128]{1,0:T(8,128)(2,1)S(1)}, u32[]{:S(2)}, u32[]{:S(2)}) collective-permute-start(bf16[80,128]{1,0:T(8,128)(2,1)S(1)} %get-tuple-element.25), channel_id=1, source_target_pairs={{0,1},{1,0},{2,3},{3,2},{4,5},{5,4},{6,7},{7,6},{8,9},{9,8},{10,11... | collective-permute-start | bytes 61448 | tf_op jit(solution)/shard_map/ppermute | solution.py:420
  8.3 1.1 %hats.2.refs_2_.refs_4_.refs_1_ = bf16[8,1024,256]{2,1,0:T(8,128)(2,1)S(1)} custom-call(f32[8,128]{1,0:T(8,128)S(4)} %get-tuple-element.35.trig, s32[8,128]{1,0:T(8,128)S(4)} %get-tuple-element.36.codes), custom_call_target="tpu_custom_call" | custom-call | flops 33554432 | tf_op jit(solution)/shard_map/hats/pallas_call | solution.py:392
  9.5 0.0 collective-permute-done.1
  9.5 2.9 %collective-permute-done.2 = bf16[80,128]{1,0:T(8,128)(2,1)S(1)} collective-permute-done((bf16[80,128]{1,0:T(8,128)(2,1)S(1)}, bf16[80,128]{1,0:T(8,128)(2,1)S(1)}, u32[]{:S(2)}, u32[]{:S(2)}) %collective-permute-start.2) | collective-permute-done | bytes 20512 | tf_op jit(solution)/shard_map/ppermute | solution.py:420
  12.4 0.0 collective-permute-done
  12.4 2.6 %collective-permute-start.6 = (bf16[2,144,128]{2,1,0:T(8,128)(2,1)S(1)}, bf16[2,144,128]{2,1,0:T(8,128)(2,1)S(1)}, u32[]{:S(2)}, u32[]{:S(2)}) collective-permute-start(bf16[2,144,128]{2,1,0:T(8,128)(2,1)S(1)} %pad_maximum_fusion.2.refs_0_), channel_id=1, source_target_pairs={{0,6},{2,4},{4,2},{6,0},{8,14},{10,12},{12,10},{14,8},{1,7},{3,5},... | collective-permute-start | bytes 221192 | tf_op jit(solution)/shard_map/ppermute | solution.py:296
  15.0 0.0 collective-permute-start.5
  15.0 0.5 %collective-permute-start.4 = (bf16[2,144,128]{2,1,0:T(8,128)(2,1)S(1)}, bf16[2,144,128]{2,1,0:T(8,128)(2,1)S(1)}, u32[]{:S(2)}, u32[]{:S(2)}) collective-permute-start(bf16[2,144,128]{2,1,0:T(8,128)(2,1)S(1)} %pad_maximum_fusion.2.refs_0_), channel_id=1, source_target_pairs={{0,2},{2,0},{4,6},{6,4},{8,10},{10,8},{12,14},{14,12},{1,3},{3,1},... | collective-permute-start | bytes 221192 | tf_op jit(solution)/shard_map/ppermute | solution.py:296
  15.5 0.4 %collective-permute-start.3 = (bf16[2,144,128]{2,1,0:T(8,128)(2,1)S(1)}, bf16[2,144,128]{2,1,0:T(8,128)(2,1)S(1)}, u32[]{:S(2)}, u32[]{:S(2)}) collective-permute-start(bf16[2,144,128]{2,1,0:T(8,128)(2,1)S(1)} %pad_maximum_fusion.2.refs_0_), channel_id=1, source_target_pairs={{0,4},{2,6},{4,0},{6,2},{8,12},{10,14},{12,8},{14,10},{1,5},{3,7},... | collective-permute-start | bytes 221192 | tf_op jit(solution)/shard_map/ppermute | solution.py:296
  16.0 1.2 %hats.3.refs_3_.refs_5_.refs_2_ = bf16[8,1024,256]{2,1,0:T(8,128)(2,1)S(1)} custom-call(f32[8,128]{1,0:T(8,128)S(4)} %get-tuple-element.35.trig, s32[8,128]{1,0:T(8,128)S(4)} %get-tuple-element.36.codes), custom_call_target="tpu_custom_call" | custom-call | flops 33554432 | tf_op jit(solution)/shard_map/hats/pallas_call | solution.py:392
  17.1 0.6 %collective-permute-done.6.refs_2_ = bf16[2,144,128]{2,1,0:T(8,128)(2,1)S(1)} collective-permute-done((bf16[2,144,128]{2,1,0:T(8,128)(2,1)S(1)}, bf16[2,144,128]{2,1,0:T(8,128)(2,1)S(1)}, u32[]{:S(2)}, u32[]{:S(2)}) %collective-permute-start.6) | collective-permute-done | bytes 73760 | tf_op jit(solution)/shard_map/ppermute | solution.py:296
  17.7 0.0 collective-permute-done.5.refs_1_
  17.7 0.0 collective-permute-start.8
  17.7 0.7 %project.3.refs_6_ = f32[8,32,256]{2,1,0:T(8,128)S(1)} custom-call(s32[8,128]{1,0:T(8,128)S(4)} %get-tuple-element.36.codes, bf16[2,144,128]{2,1,0:T(8,128)(2,1)S(1)} %pad_maximum_fusion.2.refs_0_, bf16[2,144,128]{2,1,0:T(8,128)(2,1)S(1)} %collective-permute-done.5.refs_1_, bf16[8,1024,256]{2,1,0:T(8,128)(2,1)S(1)} %hats.2.refs_2_.refs_4_.refs_1_, ...), custom_call_target="tpu_custom_call" | custom-call | flops 2147483648 | tf_op jit(solution)/shard_map/project/pallas_call | solution.py:444
  18.5 1.2 %collective-permute-done.4.refs_1_ = bf16[2,144,128]{2,1,0:T(8,128)(2,1)S(1)} collective-permute-done((bf16[2,144,128]{2,1,0:T(8,128)(2,1)S(1)}, bf16[2,144,128]{2,1,0:T(8,128)(2,1)S(1)}, u32[]{:S(2)}, u32[]{:S(2)}) %collective-permute-start.4) | collective-permute-done | bytes 73760 | tf_op jit(solution)/shard_map/ppermute | solution.py:296
  19.7 0.3 %collective-permute-done.3.refs_0_ = bf16[2,144,128]{2,1,0:T(8,128)(2,1)S(1)} collective-permute-done((bf16[2,144,128]{2,1,0:T(8,128)(2,1)S(1)}, bf16[2,144,128]{2,1,0:T(8,128)(2,1)S(1)}, u32[]{:S(2)}, u32[]{:S(2)}) %collective-permute-start.3) | collective-permute-done | bytes 73760 | tf_op jit(solution)/shard_map/ppermute | solution.py:296
  19.9 0.1 collective-permute-start.7
  20.0 0.0 collective-permute-done.8.refs_3_
  20.0 1.2 %project.4.refs_3_ = f32[8,32,256]{2,1,0:T(8,128)S(1)} custom-call(s32[8,128]{1,0:T(8,128)S(4)} %get-tuple-element.36.codes, bf16[2,144,128]{2,1,0:T(8,128)(2,1)S(1)} %collective-permute-done.3.refs_0_, bf16[2,144,128]{2,1,0:T(8,128)(2,1)S(1)} %collective-permute-done.4.refs_1_, bf16[2,144,128]{2,1,0:T(8,128)(2,1)S(1)} %collective-permute-done.6.refs_2_, ...), custom_call_target="tpu_custom_call" | custom-call | flops 2147483648 | tf_op jit(solution)/shard_map/project/pallas_call | solution.py:444
  21.2 0.2 collective-permute-done.7.refs_0_
  21.4 1.6 %project.5 = f32[1,32,2048]{2,1,0:T(8,128)} custom-call(s32[8,128]{1,0:T(8,128)S(4)} %get-tuple-element.36.codes, bf16[4,144,128]{2,1,0:T(8,128)(2,1)S(1)} %collective-permute-done.7.refs_0_, bf16[8,1024,256]{2,1,0:T(8,128)(2,1)S(1)} %hats.2.refs_2_.refs_4_.refs_1_, bf16[8,1024,256]{2,1,0:T(8,128)(2,1)S(1)} %hats.3.refs_3_.refs_5_.refs_2_, ...), custom_call_target="tpu_custom_call" | custom-call | flops 2147483648 | tf_op jit(solution)/shard_map/project/pallas_call | solution.py:444
  (5 shorter events, 0.0 us)
Async XLA Ops:
  2.7 6.8 %collective-permute-start.1 = (bf16[80,128]{1,0:T(8,128)(2,1)S(1)}, bf16[80,128]{1,0:T(8,128)(2,1)S(1)}, u32[]{:S(2)}, u32[]{:S(2)}) collective-permute-start(bf16[80,128]{1,0:T(8,128)(2,1)S(1)} %get-tuple-element.24), channel_id=1, source_target_pairs={{0,8},{1,9},{2,10},{3,11},{4,12},{5,13},{6,14},{7,15},{8,0},{9,1},... | collective-permute-start | bytes 61448 | tf_op jit(solution)/shard_map/ppermute | solution.py:420
  6.8 5.6 %collective-permute-start.2 = (bf16[80,128]{1,0:T(8,128)(2,1)S(1)}, bf16[80,128]{1,0:T(8,128)(2,1)S(1)}, u32[]{:S(2)}, u32[]{:S(2)}) collective-permute-start(bf16[80,128]{1,0:T(8,128)(2,1)S(1)} %get-tuple-element.25), channel_id=1, source_target_pairs={{0,9},{1,8},{2,11},{3,10},{4,13},{5,12},{6,15},{7,14},{8,1},{9,0},... | collective-permute-start | bytes 61448 | tf_op jit(solution)/shard_map/ppermute | solution.py:420
  8.1 4.3 %collective-permute-start = (bf16[80,128]{1,0:T(8,128)(2,1)S(1)}, bf16[80,128]{1,0:T(8,128)(2,1)S(1)}, u32[]{:S(2)}, u32[]{:S(2)}) collective-permute-start(bf16[80,128]{1,0:T(8,128)(2,1)S(1)} %get-tuple-element.25), channel_id=1, source_target_pairs={{0,1},{1,0},{2,3},{3,2},{4,5},{5,4},{6,7},{7,6},{8,9},{9,8},{10,11... | collective-permute-start | bytes 61448 | tf_op jit(solution)/shard_map/ppermute | solution.py:420
  12.4 5.3 %collective-permute-start.6 = (bf16[2,144,128]{2,1,0:T(8,128)(2,1)S(1)}, bf16[2,144,128]{2,1,0:T(8,128)(2,1)S(1)}, u32[]{:S(2)}, u32[]{:S(2)}) collective-permute-start(bf16[2,144,128]{2,1,0:T(8,128)(2,1)S(1)} %pad_maximum_fusion.2.refs_0_), channel_id=1, source_target_pairs={{0,6},{2,4},{4,2},{6,0},{8,14},{10,12},{12,10},{14,8},{1,7},{3,5},... | collective-permute-start | bytes 221192 | tf_op jit(solution)/shard_map/ppermute | solution.py:296
  15.0 2.8 %collective-permute-start.5 = (bf16[2,144,128]{2,1,0:T(8,128)(2,1)S(1)}, bf16[2,144,128]{2,1,0:T(8,128)(2,1)S(1)}, u32[]{:S(2)}, u32[]{:S(2)}) collective-permute-start(bf16[2,144,128]{2,1,0:T(8,128)(2,1)S(1)} %pad_maximum_fusion.2.refs_0_), channel_id=1, source_target_pairs={{0,16},{16,0},{1,17},{17,1},{2,18},{18,2},{3,19},{19,3},{4,20},{20... | collective-permute-start | bytes 221192 | tf_op jit(solution)/shard_map/ppermute | solution.py:292
  15.0 4.7 %collective-permute-start.4 = (bf16[2,144,128]{2,1,0:T(8,128)(2,1)S(1)}, bf16[2,144,128]{2,1,0:T(8,128)(2,1)S(1)}, u32[]{:S(2)}, u32[]{:S(2)}) collective-permute-start(bf16[2,144,128]{2,1,0:T(8,128)(2,1)S(1)} %pad_maximum_fusion.2.refs_0_), channel_id=1, source_target_pairs={{0,2},{2,0},{4,6},{6,4},{8,10},{10,8},{12,14},{14,12},{1,3},{3,1},... | collective-permute-start | bytes 221192 | tf_op jit(solution)/shard_map/ppermute | solution.py:296
  15.5 4.4 %collective-permute-start.3 = (bf16[2,144,128]{2,1,0:T(8,128)(2,1)S(1)}, bf16[2,144,128]{2,1,0:T(8,128)(2,1)S(1)}, u32[]{:S(2)}, u32[]{:S(2)}) collective-permute-start(bf16[2,144,128]{2,1,0:T(8,128)(2,1)S(1)} %pad_maximum_fusion.2.refs_0_), channel_id=1, source_target_pairs={{0,4},{2,6},{4,0},{6,2},{8,12},{10,14},{12,8},{14,10},{1,5},{3,7},... | collective-permute-start | bytes 221192 | tf_op jit(solution)/shard_map/ppermute | solution.py:296
  17.7 2.3 %collective-permute-start.8 = (bf16[2,144,128]{2,1,0:T(8,128)(2,1)S(1)}, bf16[2,144,128]{2,1,0:T(8,128)(2,1)S(1)}, u32[]{:S(2)}, u32[]{:S(2)}) collective-permute-start(bf16[2,144,128]{2,1,0:T(8,128)(2,1)S(1)} %collective-permute-done.6.refs_2_), channel_id=1, source_target_pairs={{0,16},{16,0},{1,17},{17,1},{2,18},{18,2},{3,19},{19,3},{4,20},{20... | collective-permute-start | bytes 221192 | tf_op jit(solution)/shard_map/ppermute | solution.py:292
  19.9 1.4 %collective-permute-start.7 = (bf16[4,144,128]{2,1,0:T(8,128)(2,1)S(1)}, bf16[4,144,128]{2,1,0:T(8,128)(2,1)S(1)}, u32[]{:S(2)}, u32[]{:S(2)}) collective-permute-start(bf16[4,144,128]{2,1,0:T(8,128)(2,1)S(1)} %pad_maximum_fusion), channel_id=1, source_target_pairs={{0,16},{16,0},{1,17},{17,1},{2,18},{18,2},{3,19},{19,3},{4,20},{20... | collective-permute-start | bytes 442376 | tf_op jit(solution)/shard_map/ppermute | solution.py:292

commit v14 on v9

--- a/solution.py
+++ b/solution.py
@@ -190,7 +190,7 @@
             hats[chunk, pl.ds(at + rows.shape[0], gap.shape[0]), :] = gap
         return carry
 
-    lax.fori_loop(0, count, step, 0, unroll=2)
+    lax.fori_loop(0, count, step, 0, unroll=4)
 
 
 def project_kernel(plan, codes, *refs):

time: 23.1 us -> 23.1 us (level)
  transfers between devices with their start and end apart: 9 -> 9, of which waited for: 5 -> 5; matrix products, arithmetic and copies ran while one was open for 0% -> 0% of each run, Pallas kernels for 18% -> 17%
where the time goes in v14:
time: 23.1 us; the launch traced here: 22.9 us
  starting transfers between devices  9.27 us (40%)
  Pallas kernels  7.58 us (33%)
  waiting for transfers between devices  5.3 us (23%)
  between operations  0.74 us (3%)
    ppermute x3, starting transfers between devices, joint(): return lax.ppermute(cut[turn], ('angle', 'tile'), pairs)  5.64 us
    ppermute x3, starting transfers between devices, swapped(): lax.ppermute(value, axis, [(i, i ^ by) for i in range(lax.axis_size(axis))])  3.55 us
    pallas_call x3, Pallas kernels, project(): pl.pallas_call(functools.partial(project_kernel, (parts, sources, len(win...  3.46 us
    ppermute x3, waiting for transfers between devices, joint(): return lax.ppermute(cut[turn], ('angle', 'tile'), pairs)  2.97 us
    ppermute x3, waiting for transfers between devices, swapped(): lax.ppermute(value, axis, [(i, i ^ by) for i in range(lax.axis_size(axis))])  2.16 us
    pallas_call x2, Pallas kernels, hats_of(): pl.pallas_call(functools.partial(hat_kernel, (part, half, tile_rows, angl...  2.11 us
    pallas_call x1, Pallas kernels, body(): pl.pallas_call(functools.partial(filter_kernel, (tiles, outs, first_bin,...  2.01 us
  transfers between devices with their start and end apart: 9, of which 5 were waited for; matrix products, arithmetic and copies ran while one was open for 0% of the time, Pallas kernels for 17%

profile of v14, /device:TPU:0, one launch (start us, length us, event | category | flops | bytes accessed | tf_op | source)
XLA Modules:
  0.0 22.9 jit_solution(14894583100595362655)
XLA Ops:
  0.7 2.0 %filter.1 = (bf16[80,128]{1,0:T(8,128)(2,1)S(1)}, bf16[80,128]{1,0:T(8,128)(2,1)S(1)}, f32[8,128]{1,0:T(8,128)S(4)}, s32[8,128]{1,0:T(8,128)S(4)}) custom-call(f32[1]{0:T(128)S(6)} %copy.6.width, s32[2,32]{1,0:T(2,128)} %bitcast.17, f32[16,8,128]{2,1,0:T(8,128)} %constant.4.clone.trig_table, s32[16,8,128]{2,1,0:T(8,128)} %constant.5.clone.code_table, ...), custom_call_target="tpu_custom_call" | custom-call | tf_op jit(solution)/shard_map/filter/pallas_call | solution.py:360
  2.7 4.1 %collective-permute-start.1 = (bf16[80,128]{1,0:T(8,128)(2,1)S(1)}, bf16[80,128]{1,0:T(8,128)(2,1)S(1)}, u32[]{:S(2)}, u32[]{:S(2)}) collective-permute-start(bf16[80,128]{1,0:T(8,128)(2,1)S(1)} %get-tuple-element.24), channel_id=1, source_target_pairs={{0,8},{1,9},{2,10},{3,11},{4,12},{5,13},{6,14},{7,15},{8,0},{9,1},... | collective-permute-start | bytes 61448 | tf_op jit(solution)/shard_map/ppermute | solution.py:418
  6.8 1.3 %collective-permute-start.2 = (bf16[80,128]{1,0:T(8,128)(2,1)S(1)}, bf16[80,128]{1,0:T(8,128)(2,1)S(1)}, u32[]{:S(2)}, u32[]{:S(2)}) collective-permute-start(bf16[80,128]{1,0:T(8,128)(2,1)S(1)} %get-tuple-element.25), channel_id=1, source_target_pairs={{0,9},{1,8},{2,11},{3,10},{4,13},{5,12},{6,15},{7,14},{8,1},{9,0},... | collective-permute-start | bytes 61448 | tf_op jit(solution)/shard_map/ppermute | solution.py:418
  8.1 0.2 %collective-permute-start = (bf16[80,128]{1,0:T(8,128)(2,1)S(1)}, bf16[80,128]{1,0:T(8,128)(2,1)S(1)}, u32[]{:S(2)}, u32[]{:S(2)}) collective-permute-start(bf16[80,128]{1,0:T(8,128)(2,1)S(1)} %get-tuple-element.25), channel_id=1, source_target_pairs={{0,1},{1,0},{2,3},{3,2},{4,5},{5,4},{6,7},{7,6},{8,9},{9,8},{10,11... | collective-permute-start | bytes 61448 | tf_op jit(solution)/shard_map/ppermute | solution.py:418
  8.3 1.1 %hats.2.refs_2_.refs_4_.refs_1_ = bf16[8,1024,256]{2,1,0:T(8,128)(2,1)S(1)} custom-call(f32[8,128]{1,0:T(8,128)S(4)} %get-tuple-element.35.trig, s32[8,128]{1,0:T(8,128)S(4)} %get-tuple-element.36.codes), custom_call_target="tpu_custom_call" | custom-call | flops 33554432 | tf_op jit(solution)/shard_map/hats/pallas_call | solution.py:390
  9.4 0.0 collective-permute-done.1
  9.4 3.0 %collective-permute-done.2 = bf16[80,128]{1,0:T(8,128)(2,1)S(1)} collective-permute-done((bf16[80,128]{1,0:T(8,128)(2,1)S(1)}, bf16[80,128]{1,0:T(8,128)(2,1)S(1)}, u32[]{:S(2)}, u32[]{:S(2)}) %collective-permute-start.2) | collective-permute-done | bytes 20512 | tf_op jit(solution)/shard_map/ppermute | solution.py:418
  12.4 0.0 collective-permute-done
  12.4 2.6 %collective-permute-start.6 = (bf16[2,144,128]{2,1,0:T(8,128)(2,1)S(1)}, bf16[2,144,128]{2,1,0:T(8,128)(2,1)S(1)}, u32[]{:S(2)}, u32[]{:S(2)}) collective-permute-start(bf16[2,144,128]{2,1,0:T(8,128)(2,1)S(1)} %pad_maximum_fusion.2.refs_0_), channel_id=1, source_target_pairs={{0,6},{2,4},{4,2},{6,0},{8,14},{10,12},{12,10},{14,8},{1,7},{3,5},... | collective-permute-start | bytes 221192 | tf_op jit(solution)/shard_map/ppermute | solution.py:294
  15.0 0.0 collective-permute-start.5
  15.0 0.5 %collective-permute-start.4 = (bf16[2,144,128]{2,1,0:T(8,128)(2,1)S(1)}, bf16[2,144,128]{2,1,0:T(8,128)(2,1)S(1)}, u32[]{:S(2)}, u32[]{:S(2)}) collective-permute-start(bf16[2,144,128]{2,1,0:T(8,128)(2,1)S(1)} %pad_maximum_fusion.2.refs_0_), channel_id=1, source_target_pairs={{0,2},{2,0},{4,6},{6,4},{8,10},{10,8},{12,14},{14,12},{1,3},{3,1},... | collective-permute-start | bytes 221192 | tf_op jit(solution)/shard_map/ppermute | solution.py:294
  15.5 0.4 %collective-permute-start.3 = (bf16[2,144,128]{2,1,0:T(8,128)(2,1)S(1)}, bf16[2,144,128]{2,1,0:T(8,128)(2,1)S(1)}, u32[]{:S(2)}, u32[]{:S(2)}) collective-permute-start(bf16[2,144,128]{2,1,0:T(8,128)(2,1)S(1)} %pad_maximum_fusion.2.refs_0_), channel_id=1, source_target_pairs={{0,4},{2,6},{4,0},{6,2},{8,12},{10,14},{12,8},{14,10},{1,5},{3,7},... | collective-permute-start | bytes 221192 | tf_op jit(solution)/shard_map/ppermute | solution.py:294
  16.0 1.1 %hats.3.refs_3_.refs_5_.refs_2_ = bf16[8,1024,256]{2,1,0:T(8,128)(2,1)S(1)} custom-call(f32[8,128]{1,0:T(8,128)S(4)} %get-tuple-element.35.trig, s32[8,128]{1,0:T(8,128)S(4)} %get-tuple-element.36.codes), custom_call_target="tpu_custom_call" | custom-call | flops 33554432 | tf_op jit(solution)/shard_map/hats/pallas_call | solution.py:390
  17.0 0.7 %collective-permute-done.6.refs_2_ = bf16[2,144,128]{2,1,0:T(8,128)(2,1)S(1)} collective-permute-done((bf16[2,144,128]{2,1,0:T(8,128)(2,1)S(1)}, bf16[2,144,128]{2,1,0:T(8,128)(2,1)S(1)}, u32[]{:S(2)}, u32[]{:S(2)}) %collective-permute-start.6) | collective-permute-done | bytes 73760 | tf_op jit(solution)/shard_map/ppermute | solution.py:294
  17.7 0.0 collective-permute-done.5.refs_1_
  17.7 0.0 collective-permute-start.8
  17.7 0.7 %project.3.refs_6_ = f32[8,32,256]{2,1,0:T(8,128)S(1)} custom-call(s32[8,128]{1,0:T(8,128)S(4)} %get-tuple-element.36.codes, bf16[2,144,128]{2,1,0:T(8,128)(2,1)S(1)} %pad_maximum_fusion.2.refs_0_, bf16[2,144,128]{2,1,0:T(8,128)(2,1)S(1)} %collective-permute-done.5.refs_1_, bf16[8,1024,256]{2,1,0:T(8,128)(2,1)S(1)} %hats.2.refs_2_.refs_4_.refs_1_, ...), custom_call_target="tpu_custom_call" | custom-call | flops 2147483648 | tf_op jit(solution)/shard_map/project/pallas_call | solution.py:442
  18.5 1.2 %collective-permute-done.4.refs_1_ = bf16[2,144,128]{2,1,0:T(8,128)(2,1)S(1)} collective-permute-done((bf16[2,144,128]{2,1,0:T(8,128)(2,1)S(1)}, bf16[2,144,128]{2,1,0:T(8,128)(2,1)S(1)}, u32[]{:S(2)}, u32[]{:S(2)}) %collective-permute-start.4) | collective-permute-done | bytes 73760 | tf_op jit(solution)/shard_map/ppermute | solution.py:294
  19.7 0.3 %collective-permute-done.3.refs_0_ = bf16[2,144,128]{2,1,0:T(8,128)(2,1)S(1)} collective-permute-done((bf16[2,144,128]{2,1,0:T(8,128)(2,1)S(1)}, bf16[2,144,128]{2,1,0:T(8,128)(2,1)S(1)}, u32[]{:S(2)}, u32[]{:S(2)}) %collective-permute-start.3) | collective-permute-done | bytes 73760 | tf_op jit(solution)/shard_map/ppermute | solution.py:294
  19.9 0.1 collective-permute-start.7
  20.0 0.0 collective-permute-done.8.refs_3_
  20.0 1.2 %project.4.refs_3_ = f32[8,32,256]{2,1,0:T(8,128)S(1)} custom-call(s32[8,128]{1,0:T(8,128)S(4)} %get-tuple-element.36.codes, bf16[2,144,128]{2,1,0:T(8,128)(2,1)S(1)} %collective-permute-done.3.refs_0_, bf16[2,144,128]{2,1,0:T(8,128)(2,1)S(1)} %collective-permute-done.4.refs_1_, bf16[2,144,128]{2,1,0:T(8,128)(2,1)S(1)} %collective-permute-done.6.refs_2_, ...), custom_call_target="tpu_custom_call" | custom-call | flops 2147483648 | tf_op jit(solution)/shard_map/project/pallas_call | solution.py:442
  21.2 0.2 collective-permute-done.7.refs_0_
  21.4 1.6 %project.5 = f32[1,32,2048]{2,1,0:T(8,128)} custom-call(s32[8,128]{1,0:T(8,128)S(4)} %get-tuple-element.36.codes, bf16[4,144,128]{2,1,0:T(8,128)(2,1)S(1)} %collective-permute-done.7.refs_0_, bf16[8,1024,256]{2,1,0:T(8,128)(2,1)S(1)} %hats.2.refs_2_.refs_4_.refs_1_, bf16[8,1024,256]{2,1,0:T(8,128)(2,1)S(1)} %hats.3.refs_3_.refs_5_.refs_2_, ...), custom_call_target="tpu_custom_call" | custom-call | flops 2147483648 | tf_op jit(solution)/shard_map/project/pallas_call | solution.py:442
  (5 shorter events, 0.0 us)
Async XLA Ops:
  2.7 6.7 %collective-permute-start.1 = (bf16[80,128]{1,0:T(8,128)(2,1)S(1)}, bf16[80,128]{1,0:T(8,128)(2,1)S(1)}, u32[]{:S(2)}, u32[]{:S(2)}) collective-permute-start(bf16[80,128]{1,0:T(8,128)(2,1)S(1)} %get-tuple-element.24), channel_id=1, source_target_pairs={{0,8},{1,9},{2,10},{3,11},{4,12},{5,13},{6,14},{7,15},{8,0},{9,1},... | collective-permute-start | bytes 61448 | tf_op jit(solution)/shard_map/ppermute | solution.py:418
  6.8 5.6 %collective-permute-start.2 = (bf16[80,128]{1,0:T(8,128)(2,1)S(1)}, bf16[80,128]{1,0:T(8,128)(2,1)S(1)}, u32[]{:S(2)}, u32[]{:S(2)}) collective-permute-start(bf16[80,128]{1,0:T(8,128)(2,1)S(1)} %get-tuple-element.25), channel_id=1, source_target_pairs={{0,9},{1,8},{2,11},{3,10},{4,13},{5,12},{6,15},{7,14},{8,1},{9,0},... | collective-permute-start | bytes 61448 | tf_op jit(solution)/shard_map/ppermute | solution.py:418
  8.1 4.3 %collective-permute-start = (bf16[80,128]{1,0:T(8,128)(2,1)S(1)}, bf16[80,128]{1,0:T(8,128)(2,1)S(1)}, u32[]{:S(2)}, u32[]{:S(2)}) collective-permute-start(bf16[80,128]{1,0:T(8,128)(2,1)S(1)} %get-tuple-element.25), channel_id=1, source_target_pairs={{0,1},{1,0},{2,3},{3,2},{4,5},{5,4},{6,7},{7,6},{8,9},{9,8},{10,11... | collective-permute-start | bytes 61448 | tf_op jit(solution)/shard_map/ppermute | solution.py:418
  12.4 5.3 %collective-permute-start.6 = (bf16[2,144,128]{2,1,0:T(8,128)(2,1)S(1)}, bf16[2,144,128]{2,1,0:T(8,128)(2,1)S(1)}, u32[]{:S(2)}, u32[]{:S(2)}) collective-permute-start(bf16[2,144,128]{2,1,0:T(8,128)(2,1)S(1)} %pad_maximum_fusion.2.refs_0_), channel_id=1, source_target_pairs={{0,6},{2,4},{4,2},{6,0},{8,14},{10,12},{12,10},{14,8},{1,7},{3,5},... | collective-permute-start | bytes 221192 | tf_op jit(solution)/shard_map/ppermute | solution.py:294
  15.0 2.7 %collective-permute-start.5 = (bf16[2,144,128]{2,1,0:T(8,128)(2,1)S(1)}, bf16[2,144,128]{2,1,0:T(8,128)(2,1)S(1)}, u32[]{:S(2)}, u32[]{:S(2)}) collective-permute-start(bf16[2,144,128]{2,1,0:T(8,128)(2,1)S(1)} %pad_maximum_fusion.2.refs_0_), channel_id=1, source_target_pairs={{0,16},{16,0},{1,17},{17,1},{2,18},{18,2},{3,19},{19,3},{4,20},{20... | collective-permute-start | bytes 221192 | tf_op jit(solution)/shard_map/ppermute | solution.py:290
  15.0 4.7 %collective-permute-start.4 = (bf16[2,144,128]{2,1,0:T(8,128)(2,1)S(1)}, bf16[2,144,128]{2,1,0:T(8,128)(2,1)S(1)}, u32[]{:S(2)}, u32[]{:S(2)}) collective-permute-start(bf16[2,144,128]{2,1,0:T(8,128)(2,1)S(1)} %pad_maximum_fusion.2.refs_0_), channel_id=1, source_target_pairs={{0,2},{2,0},{4,6},{6,4},{8,10},{10,8},{12,14},{14,12},{1,3},{3,1},... | collective-permute-start | bytes 221192 | tf_op jit(solution)/shard_map/ppermute | solution.py:294
  15.5 4.4 %collective-permute-start.3 = (bf16[2,144,128]{2,1,0:T(8,128)(2,1)S(1)}, bf16[2,144,128]{2,1,0:T(8,128)(2,1)S(1)}, u32[]{:S(2)}, u32[]{:S(2)}) collective-permute-start(bf16[2,144,128]{2,1,0:T(8,128)(2,1)S(1)} %pad_maximum_fusion.2.refs_0_), channel_id=1, source_target_pairs={{0,4},{2,6},{4,0},{6,2},{8,12},{10,14},{12,8},{14,10},{1,5},{3,7},... | collective-permute-start | bytes 221192 | tf_op jit(solution)/shard_map/ppermute | solution.py:294
  17.7 2.3 %collective-permute-start.8 = (bf16[2,144,128]{2,1,0:T(8,128)(2,1)S(1)}, bf16[2,144,128]{2,1,0:T(8,128)(2,1)S(1)}, u32[]{:S(2)}, u32[]{:S(2)}) collective-permute-start(bf16[2,144,128]{2,1,0:T(8,128)(2,1)S(1)} %collective-permute-done.6.refs_2_), channel_id=1, source_target_pairs={{0,16},{16,0},{1,17},{17,1},{2,18},{18,2},{3,19},{19,3},{4,20},{20... | collective-permute-start | bytes 221192 | tf_op jit(solution)/shard_map/ppermute | solution.py:290
  19.9 1.4 %collective-permute-start.7 = (bf16[4,144,128]{2,1,0:T(8,128)(2,1)S(1)}, bf16[4,144,128]{2,1,0:T(8,128)(2,1)S(1)}, u32[]{:S(2)}, u32[]{:S(2)}) collective-permute-start(bf16[4,144,128]{2,1,0:T(8,128)(2,1)S(1)} %pad_maximum_fusion), channel_id=1, source_target_pairs={{0,16},{16,0},{1,17},{17,1},{2,18},{18,2},{3,19},{19,3},{4,20},{20... | collective-permute-start | bytes 442376 | tf_op jit(solution)/shard_map/ppermute | solution.py:290
